TPU v7x, 256 devices: a whole 4x4x8 slice. The times are simulated.
256 devices in a mesh: seq: 64 (over z, y, core), tp: 4 (over x).
Axes of the slice: x: 4, y: 4, z: 8, core: 2. Of those that a mesh axis runs over, the one named last changes fastest.
Arguments:
- residual: bfloat16 [16384, 4096], P('seq', 'tp'), may hold values from -6 to 6
- cotangent: bfloat16 [16384, 4096], P('seq', 'tp'), may hold values from -6 to 6
- kept_slots: int32 [4096], P('seq'), may hold values from -1 to 255, as said below
- query: bfloat16 [4096, 2048], P('seq', 'tp'), may hold values from -6 to 6
- rotated_key_slots: bfloat16 [4096, 512], P('seq', 'tp'), may hold values from -6 to 6
- kept_value_slots: bfloat16 [4096, 512], P('seq', 'tp'), may hold values from -6 to 6
- router: float32 [4096], P('seq'), may hold values from 0.2 to 1
- out_weight: bfloat16 [2048, 4096], P('tp'), may hold values from -0.125 to 0.125
Outputs:
- updated: bfloat16 [16384, 4096], P('seq', 'tp')
- grad_query: bfloat16 [4096, 2048], P('seq', 'tp')
- key_gradient_slots: bfloat16 [4096, 512], P('seq', 'tp')
- value_gradient_slots: bfloat16 [4096, 512], P('seq', 'tp')
- grad_router: float32 [4096], P('seq')
- grad_weight: bfloat16 [2048, 4096], P('tp', 'seq')
Inputs may be any that keep to these rules, and one draw needn't show every extreme that they name: `kept_slots`: slot c of shard s holds the in-shard position of the shard's c-th kept token, positions rising with c; after the shard's last kept token its slots hold -1. 2048 slots are live in all, and some shard has all 64 slots live.
All inputs are finite; a program needn't handle non-finite values.
Results may differ from a plain program's by a relative error of at most 0.03.
Values may be sent and summed in bfloat16 or wider, within the bound.
No kernel may reach another device: no remote copies, remote signals or barrier semaphores. Data moves between devices by JAX's collectives and lax.ppermute only.
A program may use at most 64 MiB of HBM per device.

v0:
```python
import functools
import math

import jax
import jax.numpy as jnp
from jax import lax
from jax.experimental import pallas as pl
from jax.experimental.pallas import tpu as pltpu
from jax.sharding import PartitionSpec as P

HEAD = 128
NZ, NY, NC, NX = 8, 4, 2, 4
SLOTS = 64
ROWS = NZ * SLOTS
HEADS = 4
NEG = -1e30
DEAD = 100.0
SCALE = 1.0 / math.sqrt(HEAD)
LOG2E = math.log2(math.e)
BF = jnp.bfloat16
F32 = jnp.float32


def seq_move(a, dz=0, dy=0, dc=0):
    pairs = []
    for z in range(NZ):
        for y in range(NY):
            for c in range(NC):
                to = ((z + dz) % NZ * NY + (y + dy) % NY) * NC + (c ^ dc)
                pairs.append(((z * NY + y) * NC + c, to))
    return lax.ppermute(a, "seq", pairs)


def tp_move(a, dx):
    return lax.ppermute(a, "tp", [(x, (x + dx) % NX) for x in range(NX)])


def near_z(a):
    return jnp.concatenate([seq_move(a, dz=1), a, seq_move(a, dz=-1)], axis=0)


def far_z(near):
    low = seq_move(near, dz=3)
    high = seq_move(near[: 2 * near.shape[0] // 3], dz=-3)
    return high, low, near


def stage(values, *others):
    return lax.optimization_barrier((*values, *others))[: len(values)]


def dot(a, b, da, db):
    return lax.dot_general(a, b, (((da,), (db,)), ((), ())), preferred_element_type=F32)


def head_rows(ref):
    return jnp.concatenate([ref[:, h * HEAD : (h + 1) * HEAD] for h in range(HEADS)], axis=0)


def masked_scores(place, dy, dc, kv_ref, q_rows, diff):
    z, y, c = place[0], place[1], place[2]
    keys = kv_ref[:, :HEAD]
    scores = dot(keys, q_rows, 1, 1)
    own = (z * NY + y) * NC + c
    other_y = (y + NY - dy) & (NY - 1)
    other_c = c ^ dc
    out = []
    for k in range(NZ):
        shard = (((z + 2 + k) & (NZ - 1)) * NY + other_y) * NC + other_c
        live = kv_ref[k * SLOTS : (k + 1) * SLOTS, HEAD : HEAD + 1].astype(F32) < 0.5 * DEAD
        ok = jnp.logical_and(diff <= (own - shard) * SLOTS, live)
        piece = scores[k * SLOTS : (k + 1) * SLOTS] * (SCALE * LOG2E)
        out.append(jnp.where(ok, piece, NEG))
    return jnp.concatenate(out, axis=0)


def slot_difference():
    row = lax.broadcasted_iota(jnp.int32, (SLOTS, HEADS * SLOTS), 0)
    lane = lax.broadcasted_iota(jnp.int32, (SLOTS, HEADS * SLOTS), 1)
    return row - (lane & (SLOTS - 1))


FIRST = [(0, 0), (1, 0), (3, 0), (2, 0)]
SECOND = [(0, 1), (1, 1), (3, 1), (2, 1)]


def forward_kernel(blocks, first, last, place, q_ref, *refs):
    kv_refs, refs = refs[: len(blocks)], refs[len(blocks) :]
    q_rows = head_rows(q_ref)
    diff = slot_difference()
    if first:
        top = jnp.full((1, HEADS * SLOTS), NEG, F32)
        total = jnp.zeros((1, HEADS * SLOTS), F32)
        acc = jnp.zeros((HEAD, HEADS * SLOTS), F32)
    else:
        stats, acc = refs[0], refs[1][...]
        top, total = stats[0:1], stats[8:9]
        refs = refs[2:]
    for (dy, dc), kv_ref in zip(blocks, kv_refs):
        t = masked_scores(place, dy, dc, kv_ref, q_rows, diff)
        new_top = jnp.maximum(top, jnp.max(t, axis=0, keepdims=True))
        old = jnp.exp2(top - new_top)
        e = jnp.exp2(t - new_top)
        total = total * old + jnp.sum(e, axis=0, keepdims=True)
        acc = acc * old + dot(kv_ref[:, HEAD:], e.astype(BF), 0, 0)
        top = new_top
    if not last:
        refs[0][0:8] = jnp.broadcast_to(top, (8, HEADS * SLOTS))
        refs[0][8:16] = jnp.broadcast_to(total, (8, HEADS * SLOTS))
        refs[1][...] = acc
        return
    att_ref, lse_ref = refs
    out = (acc / total).T.astype(BF)
    for h in range(HEADS):
        att_ref[:, h * HEAD : (h + 1) * HEAD] = out[h * SLOTS : (h + 1) * SLOTS]
    lse_ref[...] = jnp.broadcast_to(top + jnp.log(total) * LOG2E, lse_ref.shape)


STEPS = (0, 1, 3, 2)


def backward_kernel(dc, place, q_ref, g_ref, att_ref, lse_ref, *refs):
    kv_refs, refs = refs[:NY], refs[NY:]
    q_rows = head_rows(q_ref)
    g_rows = head_rows(g_ref)
    att_rows = head_rows(att_ref)
    diff = slot_difference()
    delta = jnp.sum((g_rows.astype(F32) * att_rows.astype(F32)).T, axis=0, keepdims=True)
    lse = lse_ref[0:1]
    if dc == 1:
        acc = jnp.zeros((HEAD, HEADS * SLOTS), F32)
        outs = [refs[0].at[i * ROWS : (i + 1) * ROWS] for i in range(NY)]
    else:
        acc, refs = refs[0][...], refs[1:]
        outs = refs[:NY]
    for dy, kv_ref, out_ref in zip(STEPS, kv_refs, outs):
        t = masked_scores(place, dy, dc, kv_ref, q_rows, diff)
        p = jnp.exp2(t - lse)
        dp = dot(kv_ref[:, HEAD:], g_rows, 1, 1)
        ds = (p * (dp - delta)).astype(BF)
        out_ref[:, :HEAD] = (dot(ds, q_rows, 1, 0) * SCALE).astype(BF)
        out_ref[:, HEAD:] = dot(p.astype(BF), g_rows, 1, 0).astype(BF)
        acc = acc + dot(kv_ref[:, :HEAD], ds, 0, 0)
    if dc == 1:
        refs[1][...] = acc
    else:
        grad = (acc * SCALE).T.astype(BF)
        for h in range(HEADS):
            refs[NY][:, h * HEAD : (h + 1) * HEAD] = grad[h * SLOTS : (h + 1) * SLOTS]


def attn_grad_kernel(place, *refs):
    chunks, w_ref, g_ref, groups, full = refs[:4], refs[4], refs[5], refs[6:9], refs[9]
    z, x = place[0], place[3]
    width = w_ref.shape[1] // NX
    acc = None
    for m in range(NX):
        start = pl.multiple_of(((x + NX - m) & (NX - 1)) * width, width)
        chunk = chunks[m][...]
        full[:, pl.ds(start, width)] = chunk
        term = dot(chunk, w_ref[:, pl.ds(start, width)], 1, 1)
        acc = term if acc is None else acc + term
    g_ref[...] = acc.astype(BF)
    part = w_ref.shape[1] // NZ
    for group, offsets in zip(groups, ((2, 3, 4), (5, 6), (7, 8, 9))):
        for i, d in enumerate(offsets):
            start = pl.multiple_of(((z + d) & (NZ - 1)) * part, part)
            group[i * SLOTS : (i + 1) * SLOTS] = full[:, pl.ds(start, part)]


def project_kernel(place, att_ref, g_ref, w_ref, *outs):
    x = place[3]
    width = w_ref.shape[1] // NX
    att = att_ref[...]
    delta = jnp.sum(att.astype(F32) * g_ref[...].astype(F32), axis=1, keepdims=True)
    high = delta.astype(BF).astype(F32)
    mid = (delta - high).astype(BF).astype(F32)
    low = delta - high - mid
    lane = lax.broadcasted_iota(jnp.int32, (SLOTS, HEAD), 1)
    zero = jnp.zeros((), F32)
    extra = jnp.where(lane == 0, high, jnp.where(lane == 1, mid, jnp.where(lane == 2, low, zero)))
    for m in range(NX):
        start = pl.multiple_of(((x + NX - m) & (NX - 1)) * width, width)
        outs[m][:, :width] = dot(att, w_ref[:, pl.ds(start, width)], 1, 0).astype(BF)
        outs[m][:, width:] = extra.astype(BF)


def weight_kernel(place, high, low, near, own, from_low, from_high, from_below, from_above, *refs):
    outs, att, rows = refs[:NY], refs[NY], refs[NY + 1]
    y = place[1]
    att[: 2 * SLOTS] = high[...]
    att[2 * SLOTS : 5 * SLOTS] = low[...]
    att[5 * SLOTS :] = near[...]
    order = (
        (from_below, 2),
        (from_high, 0),
        (from_below, 1),
        (from_low, 1),
        (from_above, 1),
        (from_below, 0),
        (own, 1),
        (from_above, 0),
    )
    for k, (ref, i) in enumerate(order):
        rows[k * SLOTS : (k + 1) * SLOTS] = ref[i * SLOTS : (i + 1) * SLOTS]
    width = rows.shape[1] // NY
    for m in range(NY):
        start = pl.multiple_of(((y + NY - m) & (NY - 1)) * width, width)
        outs[m][...] = dot(att[...], rows[:, pl.ds(start, width)], 0, 0).astype(BF)


VM = pl.BlockSpec(memory_space=pltpu.VMEM)
SM = pl.BlockSpec(memory_space=pltpu.SMEM)


def call(kernel, place, args, shapes, flops, scratch=(), limit=32):
    size = sum(math.prod(a.shape) * a.dtype.itemsize for a in args)
    size += sum(math.prod(s.shape) * s.dtype.itemsize for s in shapes)
    return pl.pallas_call(
        kernel,
        out_shape=shapes,
        in_specs=[SM] + [VM] * len(args),
        out_specs=[VM] * len(shapes),
        scratch_shapes=list(scratch),
        compiler_params=pltpu.CompilerParams(vmem_limit_bytes=limit * 1024 * 1024),
        cost_estimate=pl.CostEstimate(flops=flops, bytes_accessed=size, transcendentals=0),
    )(place, *args)


def shape(dims, dtype):
    return jax.ShapeDtypeStruct(dims, dtype)


def add(*parts):
    total = parts[0].astype(F32)
    for p in parts[1:]:
        total = total + p.astype(F32)
    return total


def on_device(
    residual, cotangent, kept_slots, query, rotated_key_slots, kept_value_slots, router, out_weight
):
    s = lax.axis_index("seq")
    z, y, c = s // (NY * NC), s // NC % NY, s % NC
    place = jnp.stack([z, y, c, lax.axis_index("tp")]).astype(jnp.int32)
    live = kept_slots >= 0
    live_col = live[:, None]

    tokens = residual.shape[0]
    width = out_weight.shape[1]
    feats = out_weight.shape[0]
    lanes = HEADS * SLOTS
    hot = (kept_slots[:, None] == jnp.arange(tokens, dtype=jnp.int32)[None, :]).astype(BF)
    weight_col = jnp.where(live, router, 0.0)[:, None]
    proj_grad = (weight_col * dot(hot, cotangent, 1, 0)).astype(BF)
    kv = jnp.concatenate(
        [rotated_key_slots, jnp.where(live_col, kept_value_slots, jnp.asarray(DEAD, BF))], axis=1
    )

    kv, proj_grad = stage((kv, proj_grad))
    kv_near = near_z(kv)
    chunks = {m: tp_move(proj_grad, m) for m in (1, 3, 2)}
    kv_near, chunks[1], chunks[3] = stage((kv_near, chunks[1], chunks[3]))
    kv_z = jnp.concatenate(far_z(kv_near), axis=0)
    attn_grad, far_up, far_down, own_part = call(
        attn_grad_kernel,
        place,
        [proj_grad, chunks[1], chunks[2], chunks[3], out_weight],
        [shape((SLOTS, feats), BF)]
        + [shape((n * SLOTS, width // NZ), BF) for n in (3, 2, 3)],
        2 * SLOTS * width * feats,
        [pltpu.VMEM((SLOTS, width), BF)],
    )
    kv_z, far_up, far_down = stage((kv_z, far_up, far_down))
    kv_y = [kv_z, seq_move(kv_z, dy=1), seq_move(kv_z, dy=-1), seq_move(kv_z, dy=2)]
    from_low = seq_move(far_up, dz=3)
    from_high = seq_move(far_down, dz=-3)
    kv_y = stage(kv_y, from_low, from_high)
    kv_c = [seq_move(a, dc=1) for a in kv_y]
    state = call(
        functools.partial(forward_kernel, FIRST, True, False),
        place,
        [query, *kv_y],
        [shape((16, lanes), F32), shape((HEAD, lanes), F32)],
        4 * len(FIRST) * ROWS * lanes * HEAD,
    )
    attended, lse = call(
        functools.partial(forward_kernel, SECOND, False, True),
        place,
        [query, *stage(kv_c, *state), *state],
        [shape((SLOTS, feats), BF), shape((8, lanes), F32)],
        4 * len(SECOND) * ROWS * lanes * HEAD,
    )
    n = SLOTS
    for_above = jnp.concatenate([own_part[2 * n :], from_low[2 * n :], from_high[n:]], axis=0)
    for_below = jnp.concatenate([own_part[:n], from_low[:n]], axis=0)
    for_above, for_below = stage((for_above, for_below), attended)
    att_near = near_z(attended)
    from_below = seq_move(for_above, dz=1)
    from_above = seq_move(for_below, dz=-1)
    other, acc = call(
        functools.partial(backward_kernel, 1),
        place,
        [query, attn_grad, attended, lse, *kv_c],
        [shape((NY * ROWS, 2 * HEAD), BF), shape((HEAD, lanes), F32)],
        10 * NY * ROWS * lanes * HEAD,
    )
    other, acc = stage((other, acc))
    theirs = seq_move(other, dc=1)
    *own, grad_query = call(
        functools.partial(backward_kernel, 0),
        place,
        [query, attn_grad, attended, lse, *kv_y, acc],
        [shape((ROWS, 2 * HEAD), BF)] * NY + [shape((SLOTS, feats), BF)],
        10 * NY * ROWS * lanes * HEAD,
    )
    projected = call(
        project_kernel,
        place,
        [attended, attn_grad, out_weight],
        [shape((SLOTS, width // NX + HEAD), BF)] * NX,
        2 * SLOTS * width * feats,
    )
    sums = [add(a, theirs[i * ROWS : (i + 1) * ROWS]).astype(BF) for i, a in enumerate(own)]
    *sums, att_near = stage((*sums, att_near), from_below, from_above, *projected)
    parts = [sums[0]] + [seq_move(sums[i], dy=-STEPS[i]) for i in range(1, NY)]
    att_z = far_z(att_near)
    projected = [projected[0]] + [tp_move(projected[m], -m) for m in (1, 3, 2)]
    weight_parts = call(
        weight_kernel,
        place,
        [*att_z, own_part, from_low, from_high, from_below, from_above],
        [shape((feats, width // NZ // NY), BF)] * NY,
        2 * ROWS * feats * (width // NZ),
        [pltpu.VMEM((ROWS, feats), BF), pltpu.VMEM((ROWS, width // NZ), BF)],
    )
    *parts, w0, w1, w2, w3 = stage((*parts, *weight_parts), *projected)
    sum_up = add(*[p[: 3 * n] for p in parts]).astype(BF)
    sum_down = add(*[p[3 * n : 5 * n] for p in parts]).astype(BF)
    sum_low = seq_move(sum_up, dz=3)
    sum_high = seq_move(sum_down, dz=-3)
    weight_sum = add(
        w0, seq_move(w1, dy=-1), seq_move(w2, dy=-2), seq_move(w3, dy=-3)
    ).astype(BF)
    near = [p[5 * n :] for p in parts]
    below = add(*[p[:n] for p in near], sum_low[:n]).astype(BF)
    above = add(*[p[2 * n :] for p in near], sum_low[2 * n :], sum_high[n:]).astype(BF)
    here = add(*[p[n : 2 * n] for p in near], sum_low[n : 2 * n], sum_high[:n])
    below, above, here, weight_sum = stage((below, above, here, weight_sum))
    weight_sum = add(weight_sum, seq_move(weight_sum, dc=1))
    here = add(here, seq_move(below, dz=-1), seq_move(above, dz=1))
    here = jnp.where(live_col, here, 0.0).astype(BF)
    half = width // NZ // NY // NC
    grad_weight = lax.dynamic_slice_in_dim(weight_sum, c * half, half, 1).astype(BF)

    mine = add(*projected)
    contribution = (weight_col * mine[:, : width // NX]).astype(BF)
    router_sum = mine[:, width // NX] + mine[:, width // NX + 1] + mine[:, width // NX + 2]
    grad_router = jnp.where(live, router_sum / router, 0.0)
    updated = (residual.astype(F32) + dot(hot, contribution, 0, 0)).astype(BF)
    grad_query = jnp.where(live_col, grad_query, jnp.zeros((), BF))
    return (updated, grad_query, here[:, :HEAD], here[:, HEAD:], grad_router, grad_weight)


def solution(mesh):
    return jax.shard_map(
        on_device,
        mesh=mesh,
        in_specs=(
            P("seq", "tp"),
            P("seq", "tp"),
            P("seq"),
            P("seq", "tp"),
            P("seq", "tp"),
            P("seq", "tp"),
            P("seq"),
            P("tp", None),
        ),
        out_specs=(
            P("seq", "tp"),
            P("seq", "tp"),
            P("seq", "tp"),
            P("seq", "tp"),
            P("seq"),
            P("tp", "seq"),
        ),
        check_vma=False,
    )
```

profile of v0, /device:TPU:2, one launch (start us, length us, event | category | flops | bytes accessed | tf_op | source)
XLA Modules:
  0.0 115.4 jit_solution(17868022067632334157)
XLA Ops:
  0.7 0.7 broadcast_compare_fusion
  1.4 0.7 broadcast_select_fusion.2
  2.1 0.8 broadcast_select_fusion.1
  2.8 0.7 pad_maximum_fusion.5
  3.6 0.9 fusion.1.refs_0_
  4.5 2.0 %collective-permute-start = (bf16[64,256]{1,0:T(8,128)(2,1)S(1)}, bf16[64,256]{1,0:T(8,128)(2,1)S(1)}, u32[]{:S(2)}, u32[]{:S(2)}) collective-permute-start(bf16[64,256]{1,0:T(8,128)(2,1)S(1)} %pad_maximum_fusion.5), channel_id=1, source_target_pairs={{0,32},{4,36},{8,40},{12,44},{16,48},{20,52},{24,56},{28,60},{32,6... | collective-permute-start | bytes 98312 | tf_op jit(solution)/shard_map/ppermute | solution.py:31
  6.5 4.0 %collective-permute-start.1 = (bf16[64,256]{1,0:T(8,128)(2,1)S(1)}, bf16[64,256]{1,0:T(8,128)(2,1)S(1)}, u32[]{:S(2)}, u32[]{:S(2)}) collective-permute-start(bf16[64,256]{1,0:T(8,128)(2,1)S(1)} %pad_maximum_fusion.5), channel_id=1, source_target_pairs={{0,224},{4,228},{8,232},{12,236},{16,240},{20,244},{24,248},{28,25... | collective-permute-start | bytes 98312 | tf_op jit(solution)/shard_map/ppermute | solution.py:31
  10.5 1.5 %collective-permute-start.2 = (bf16[64,1024]{1,0:T(8,128)(2,1)S(1)}, bf16[64,1024]{1,0:T(8,128)(2,1)S(1)}, u32[]{:S(2)}, u32[]{:S(2)}) collective-permute-start(bf16[64,1024]{1,0:T(8,128)(2,1)S(1)} %fusion.1.refs_0_), channel_id=1, source_target_pairs={{0,1},{1,2},{2,3},{3,0},{4,5},{5,6},{6,7},{7,4},{8,9},{9,10},{10,1... | collective-permute-start | bytes 393224 | tf_op jit(solution)/shard_map/ppermute | solution.py:35
  12.0 0.5 collective-permute-start.3
  12.5 2.1 %collective-permute-start.6 = (bf16[64,1024]{1,0:T(8,128)(2,1)S(1)}, bf16[64,1024]{1,0:T(8,128)(2,1)S(1)}, u32[]{:S(2)}, u32[]{:S(2)}) collective-permute-start(bf16[64,1024]{1,0:T(8,128)(2,1)S(1)} %fusion.1.refs_0_), channel_id=1, source_target_pairs={{0,2},{1,3},{2,0},{3,1},{4,6},{5,7},{6,4},{7,5},{8,10},{9,11},{10,... | collective-permute-start | bytes 393224 | tf_op jit(solution)/shard_map/ppermute | solution.py:35
  14.7 0.8 collective-permute-done.2.refs_1_
  15.5 2.9 %collective-permute-done.3.refs_3_ = bf16[64,1024]{1,0:T(8,128)(2,1)S(1)} collective-permute-done((bf16[64,1024]{1,0:T(8,128)(2,1)S(1)}, bf16[64,1024]{1,0:T(8,128)(2,1)S(1)}, u32[]{:S(2)}, u32[]{:S(2)}) %collective-permute-start.3) | collective-permute-done | bytes 131104 | tf_op jit(solution)/shard_map/ppermute | solution.py:35
  18.4 1.8 %collective-permute-start.5 = (bf16[192,256]{1,0:T(8,128)(2,1)S(1)}, bf16[192,256]{1,0:T(8,128)(2,1)S(1)}, u32[]{:S(2)}, u32[]{:S(2)}) collective-permute-start(bf16[192,256]{1,0:T(8,128)(2,1)S(1)} %pad_maximum_fusion.4), channel_id=1, source_target_pairs={{0,96},{4,100},{8,104},{12,108},{16,112},{20,116},{24,120},{28,124... | collective-permute-start | bytes 294920 | tf_op jit(solution)/shard_map/ppermute | solution.py:31
  20.2 3.2 %collective-permute-start.4 = (bf16[128,256]{1,0:T(8,128)(2,1)S(1)}, bf16[128,256]{1,0:T(8,128)(2,1)S(1)}, u32[]{:S(2)}, u32[]{:S(2)}) collective-permute-start(bf16[128,256]{1,0:T(8,128)(2,1)S(1)} %slice.142), channel_id=1, source_target_pairs={{0,160},{4,164},{8,168},{12,172},{16,176},{20,180},{24,184},{28,18... | collective-permute-start | bytes 196616 | tf_op jit(solution)/shard_map/ppermute | solution.py:31
  23.5 2.2 %copy-done.1 = bf16[512,4096]{1,0:T(8,128)(2,1)S(1)} copy-done((bf16[512,4096]{1,0:T(8,128)(2,1)S(1)}, bf16[512,4096]{1,0:T(8,128)(2,1)}, u32[]{:S(2)}) %copy-start.1) | copy-done | bytes 4194328
  25.7 1.9 %shard_map.127 = (bf16[64,512]{1,0:T(8,128)(2,1)S(1)}, bf16[192,512]{1,0:T(8,128)(2,1)S(1)}, bf16[128,512]{1,0:T(8,128)(2,1)S(1)}, bf16[192,512]{1,0:T(8,128)(2,1)S(1)}) custom-call(s32[4]{0:T(128)S(1)} %pad_add_fusion.place, bf16[64,1024]{1,0:T(8,128)(2,1)S(1)} %fusion.1.refs_0_, bf16[64,1024]{1,0:T(8,128)(2,1)S(1)} %collective-permute-done.2.refs_1_, ...), custom_call_target="tpu_custom_call" | custom-call | flops 268435456 | bytes 5308416 | tf_op jit(solution)/shard_map/pallas_call | solution.py:219
  27.8 1.7 %collective-permute-start.7 = (bf16[512,256]{1,0:T(8,128)(2,1)S(1)}, bf16[512,256]{1,0:T(8,128)(2,1)S(1)}, u32[]{:S(2)}, u32[]{:S(2)}) collective-permute-start(bf16[512,256]{1,0:T(8,128)(2,1)S(1)} %pad_maximum_fusion.refs_0_), channel_id=1, source_target_pairs={{0,8},{4,12},{8,16},{12,20},{16,24},{20,28},{24,0},{28,4},{32,40},... | collective-permute-start | bytes 786440 | tf_op jit(solution)/shard_map/ppermute | solution.py:31
  29.4 1.7 %collective-permute-start.8 = (bf16[512,256]{1,0:T(8,128)(2,1)S(1)}, bf16[512,256]{1,0:T(8,128)(2,1)S(1)}, u32[]{:S(2)}, u32[]{:S(2)}) collective-permute-start(bf16[512,256]{1,0:T(8,128)(2,1)S(1)} %pad_maximum_fusion.refs_0_), channel_id=1, source_target_pairs={{0,24},{4,28},{8,0},{12,4},{16,8},{20,12},{24,16},{28,20},{32,56},... | collective-permute-start | bytes 786440 | tf_op jit(solution)/shard_map/ppermute | solution.py:31
  31.1 2.0 %collective-permute-start.9 = (bf16[512,256]{1,0:T(8,128)(2,1)S(1)}, bf16[512,256]{1,0:T(8,128)(2,1)S(1)}, u32[]{:S(2)}, u32[]{:S(2)}) collective-permute-start(bf16[512,256]{1,0:T(8,128)(2,1)S(1)} %pad_maximum_fusion.refs_0_), channel_id=1, source_target_pairs={{0,16},{4,20},{8,24},{12,28},{16,0},{20,4},{24,8},{28,12},{32,48},... | collective-permute-start | bytes 786440 | tf_op jit(solution)/shard_map/ppermute | solution.py:31
  33.1 2.7 %collective-permute-start.10 = (bf16[192,512]{1,0:T(8,128)(2,1)S(1)}, bf16[192,512]{1,0:T(8,128)(2,1)S(1)}, u32[]{:S(2)}, u32[]{:S(2)}) collective-permute-start(bf16[192,512]{1,0:T(8,128)(2,1)S(1)} %get-tuple-element.72), channel_id=1, source_target_pairs={{0,96},{4,100},{8,104},{12,108},{16,112},{20,116},{24,120},{28,124... | collective-permute-start | bytes 589832 | tf_op jit(solution)/shard_map/ppermute | solution.py:31
  35.8 2.3 %collective-permute-start.11 = (bf16[128,512]{1,0:T(8,128)(2,1)S(1)}, bf16[128,512]{1,0:T(8,128)(2,1)S(1)}, u32[]{:S(2)}, u32[]{:S(2)}) collective-permute-start(bf16[128,512]{1,0:T(8,128)(2,1)S(1)} %get-tuple-element.73), channel_id=1, source_target_pairs={{0,160},{4,164},{8,168},{12,172},{16,176},{20,180},{24,184},{28,18... | collective-permute-start | bytes 393224 | tf_op jit(solution)/shard_map/ppermute | solution.py:31
  38.1 5.4 %collective-permute-done.11.from_high = bf16[128,512]{1,0:T(8,128)(2,1)S(1)} collective-permute-done((bf16[128,512]{1,0:T(8,128)(2,1)S(1)}, bf16[128,512]{1,0:T(8,128)(2,1)S(1)}, u32[]{:S(2)}, u32[]{:S(2)}) %collective-permute-start.11) | collective-permute-done | bytes 131104 | tf_op jit(solution)/shard_map/ppermute | solution.py:31
  43.5 2.7 %collective-permute-done.10.from_low = bf16[192,512]{1,0:T(8,128)(2,1)S(1)} collective-permute-done((bf16[192,512]{1,0:T(8,128)(2,1)S(1)}, bf16[192,512]{1,0:T(8,128)(2,1)S(1)}, u32[]{:S(2)}, u32[]{:S(2)}) %collective-permute-start.10) | collective-permute-done | bytes 196640 | tf_op jit(solution)/shard_map/ppermute | solution.py:31
  46.4 0.5 collective-permute-start.13
  47.0 0.4 collective-permute-start.15
  47.4 2.4 %shard_map.128 = (f32[16,256]{1,0:T(8,128)S(1)}, f32[128,256]{1,0:T(8,128)S(1)}) custom-call(s32[4]{0:T(128)S(1)} %pad_add_fusion.place, bf16[64,512]{1,0:T(8,128)(2,1)S(1)} %copy-done.3, bf16[512,256]{1,0:T(8,128)(2,1)S(1)} %pad_maximum_fusion.refs_0_, bf16[512,256]{1,0:T(8,128)(2,1)S(1)} %collective-permute-done.7.refs_1_, ...), custom_call_target="tpu_custom_call" | custom-call | flops 268435456 | bytes 1261568 | tf_op jit(solution)/shard_map/pallas_call | solution.py:219
  49.9 2.4 %shard_map.129 = (bf16[64,512]{1,0:T(8,128)(2,1)S(1)}, f32[8,256]{1,0:T(8,128)S(1)}) custom-call(s32[4]{0:T(128)S(1)} %pad_add_fusion.place, bf16[64,512]{1,0:T(8,128)(2,1)S(1)} %copy-done.3, bf16[512,256]{1,0:T(8,128)(2,1)S(1)} %collective-permute-done.12.refs_0_, bf16[512,256]{1,0:T(8,128)(2,1)S(1)} %collective-permute-done.13.refs_1_, ...), custom_call_target="tpu_custom_call" | custom-call | flops 268435456 | bytes 1335296 | tf_op jit(solution)/shard_map/pallas_call | solution.py:219
  52.3 2.2 %shard_map.131 = (bf16[2048,256]{1,0:T(8,128)(2,1)S(1)}, f32[128,256]{1,0:T(8,128)S(1)}) custom-call(s32[4]{0:T(128)S(1)} %pad_add_fusion.place, bf16[64,512]{1,0:T(8,128)(2,1)S(1)} %copy-done.3, bf16[64,512]{1,0:T(8,128)(2,1)S(1)} %get-tuple-element.85.g_ref, bf16[64,512]{1,0:T(8,128)(2,1)S(1)} %get-tuple-element.84.att_ref, ...), custom_call_target="tpu_custom_call" | custom-call | flops 671088640 | bytes 2433024 | tf_op jit(solution)/shard_map/pallas_call | solution.py:219
  54.7 1.5 %collective-permute-start.20 = (bf16[64,512]{1,0:T(8,128)(2,1)S(1)}, bf16[64,512]{1,0:T(8,128)(2,1)S(1)}, u32[]{:S(2)}, u32[]{:S(2)}) collective-permute-start(bf16[64,512]{1,0:T(8,128)(2,1)S(1)} %get-tuple-element.84.att_ref), channel_id=1, source_target_pairs={{0,32},{4,36},{8,40},{12,44},{16,48},{20,52},{24,56},{28,60},{32,6... | collective-permute-start | bytes 196616 | tf_op jit(solution)/shard_map/ppermute | solution.py:31
  56.3 1.8 %collective-permute-start.21 = (bf16[64,512]{1,0:T(8,128)(2,1)S(1)}, bf16[64,512]{1,0:T(8,128)(2,1)S(1)}, u32[]{:S(2)}, u32[]{:S(2)}) collective-permute-start(bf16[64,512]{1,0:T(8,128)(2,1)S(1)} %get-tuple-element.84.att_ref), channel_id=1, source_target_pairs={{0,224},{4,228},{8,232},{12,236},{16,240},{20,244},{24,248},{28,25... | collective-permute-start | bytes 196616 | tf_op jit(solution)/shard_map/ppermute | solution.py:31
  58.0 1.4 %shard_map.130 = (bf16[64,1152]{1,0:T(8,128)(2,1)S(1)}, bf16[64,1152]{1,0:T(8,128)(2,1)S(1)}, bf16[64,1152]{1,0:T(8,128)(2,1)S(1)}, bf16[64,1152]{1,0:T(8,128)(2,1)S(1)}) custom-call(s32[4]{0:T(128)S(1)} %pad_add_fusion.place, bf16[64,512]{1,0:T(8,128)(2,1)S(1)} %get-tuple-element.84.att_ref, bf16[64,512]{1,0:T(8,128)(2,1)S(1)} %get-tuple-element.85.g_ref, ...), custom_call_target="tpu_custom_call" | custom-call | flops 268435456 | bytes 4915200 | tf_op jit(solution)/shard_map/pallas_call | solution.py:219
  59.5 0.4 collective-permute-start.16
  59.9 1.7 %collective-permute-start.17 = (bf16[64,1152]{1,0:T(8,128)(2,1)S(1)}, bf16[64,1152]{1,0:T(8,128)(2,1)S(1)}, u32[]{:S(2)}, u32[]{:S(2)}) collective-permute-start(bf16[64,1152]{1,0:T(8,128)(2,1)S(1)} %get-tuple-element.88), channel_id=1, source_target_pairs={{0,1},{1,2},{2,3},{3,0},{4,5},{5,6},{6,7},{7,4},{8,9},{9,10},{10,1... | collective-permute-start | bytes 442376 | tf_op jit(solution)/shard_map/ppermute | solution.py:35
  61.6 2.3 %shard_map.132 = (bf16[512,256]{1,0:T(8,128)(2,1)S(1)}, bf16[512,256]{1,0:T(8,128)(2,1)S(1)}, bf16[512,256]{1,0:T(8,128)(2,1)S(1)}, bf16[512,256]{1,0:T(8,128)(2,1)S(1)}, bf16[64,512]{1,0:T(8,128)(2,1)S(1)}) custom-call(s32[4]{0:T(128)S(1)} %pad_add_fusion.place, bf16[64,512]{1,0:T(8,128)(2,1)S(1)} %copy-done.3, ...), custom_call_target="tpu_custom_call" | custom-call | flops 671088640 | bytes 2498560 | tf_op jit(solution)/shard_map/pallas_call | solution.py:219
  63.8 4.3 %collective-permute-start.18 = (bf16[64,1152]{1,0:T(8,128)(2,1)S(1)}, bf16[64,1152]{1,0:T(8,128)(2,1)S(1)}, u32[]{:S(2)}, u32[]{:S(2)}) collective-permute-start(bf16[64,1152]{1,0:T(8,128)(2,1)S(1)} %get-tuple-element.89), channel_id=1, source_target_pairs={{0,2},{1,3},{2,0},{3,1},{4,6},{5,7},{6,4},{7,5},{8,10},{9,11},{10,... | collective-permute-start | bytes 442376 | tf_op jit(solution)/shard_map/ppermute | solution.py:35
  68.2 0.7 broadcast_select_fusion
  68.9 1.7 %collective-permute-start.22 = (bf16[192,512]{1,0:T(8,128)(2,1)S(1)}, bf16[192,512]{1,0:T(8,128)(2,1)S(1)}, u32[]{:S(2)}, u32[]{:S(2)}) collective-permute-start(bf16[192,512]{1,0:T(8,128)(2,1)S(1)} %pad_maximum_fusion.2), channel_id=1, source_target_pairs={{0,32},{4,36},{8,40},{12,44},{16,48},{20,52},{24,56},{28,60},{32,6... | collective-permute-start | bytes 589832 | tf_op jit(solution)/shard_map/ppermute | solution.py:31
  70.6 1.8 %collective-permute-start.23 = (bf16[128,512]{1,0:T(8,128)(2,1)S(1)}, bf16[128,512]{1,0:T(8,128)(2,1)S(1)}, u32[]{:S(2)}, u32[]{:S(2)}) collective-permute-start(bf16[128,512]{1,0:T(8,128)(2,1)S(1)} %pad_maximum_fusion.3), channel_id=1, source_target_pairs={{0,224},{4,228},{8,232},{12,236},{16,240},{20,244},{24,248},{28,25... | collective-permute-start | bytes 393224 | tf_op jit(solution)/shard_map/ppermute | solution.py:31
  72.8 3.1 %collective-permute-done.23.from_above = bf16[128,512]{1,0:T(8,128)(2,1)S(1)} collective-permute-done((bf16[128,512]{1,0:T(8,128)(2,1)S(1)}, bf16[128,512]{1,0:T(8,128)(2,1)S(1)}, u32[]{:S(2)}, u32[]{:S(2)}) %collective-permute-start.23) | collective-permute-done | bytes 131104 | tf_op jit(solution)/shard_map/ppermute | solution.py:31
  76.0 3.5 %collective-permute-start.28 = (bf16[192,512]{1,0:T(8,128)(2,1)S(1)}, bf16[192,512]{1,0:T(8,128)(2,1)S(1)}, u32[]{:S(2)}, u32[]{:S(2)}) collective-permute-start(bf16[192,512]{1,0:T(8,128)(2,1)S(1)} %pad_maximum_fusion.1.near), channel_id=1, source_target_pairs={{0,96},{4,100},{8,104},{12,108},{16,112},{20,116},{24,120},{28,124... | collective-permute-start | bytes 589832 | tf_op jit(solution)/shard_map/ppermute | solution.py:31
  79.5 1.6 %collective-permute-start.27 = (bf16[128,512]{1,0:T(8,128)(2,1)S(1)}, bf16[128,512]{1,0:T(8,128)(2,1)S(1)}, u32[]{:S(2)}, u32[]{:S(2)}) collective-permute-start(bf16[128,512]{1,0:T(8,128)(2,1)S(1)} %slice.153), channel_id=1, source_target_pairs={{0,160},{4,164},{8,168},{12,172},{16,176},{20,180},{24,184},{28,18... | collective-permute-start | bytes 393224 | tf_op jit(solution)/shard_map/ppermute | solution.py:31
  81.1 1.1 collective-permute-start.24
  82.1 1.0 collective-permute-start.25
  83.1 1.6 %collective-permute-start.26 = (bf16[512,256]{1,0:T(8,128)(2,1)S(1)}, bf16[512,256]{1,0:T(8,128)(2,1)S(1)}, u32[]{:S(2)}, u32[]{:S(2)}) collective-permute-start(bf16[512,256]{1,0:T(8,128)(2,1)S(1)} %get-tuple-element.104), channel_id=1, source_target_pairs={{0,16},{4,20},{8,24},{12,28},{16,0},{20,4},{24,8},{28,12},{32,48},... | collective-permute-start | bytes 786440 | tf_op jit(solution)/shard_map/ppermute | solution.py:31
  84.7 1.2 %fusion = bf16[256,1024]{1,0:T(8,128)(2,1)} fusion(bf16[256,1024]{1,0:T(8,128)(2,1)S(1)} %copy-done.4, f32[64,1152]{1,0:T(8,128)S(1)} %convert_add_fusion, f32[64]{0:T(128)S(1)} %broadcast_select_fusion.2, s32[64]{0:T(128)S(1)} %copy-done.5), kind=kOutput, calls=%fused_computation.1 | convolution fusion | flops 34488320 | bytes 1311744 | tf_op jit(solution)/shard_map/dot_general | solution.py:53
  85.9 2.8 %collective-permute-done.27.high = bf16[128,512]{1,0:T(8,128)(2,1)S(1)} collective-permute-done((bf16[128,512]{1,0:T(8,128)(2,1)S(1)}, bf16[128,512]{1,0:T(8,128)(2,1)S(1)}, u32[]{:S(2)}, u32[]{:S(2)}) %collective-permute-start.27) | collective-permute-done | bytes 131104 | tf_op jit(solution)/shard_map/ppermute | solution.py:31
  88.7 2.0 %collective-permute-done.28.low = bf16[192,512]{1,0:T(8,128)(2,1)S(1)} collective-permute-done((bf16[192,512]{1,0:T(8,128)(2,1)S(1)}, bf16[192,512]{1,0:T(8,128)(2,1)S(1)}, u32[]{:S(2)}, u32[]{:S(2)}) %collective-permute-start.28) | collective-permute-done | bytes 196640 | tf_op jit(solution)/shard_map/ppermute | solution.py:31
  90.6 1.3 %shard_map.133 = (bf16[512,128]{1,0:T(8,128)(2,1)S(1)}, bf16[512,128]{1,0:T(8,128)(2,1)S(1)}, bf16[512,128]{1,0:T(8,128)(2,1)S(1)}, bf16[512,128]{1,0:T(8,128)(2,1)S(1)}) custom-call(s32[4]{0:T(128)S(1)} %pad_add_fusion.place, bf16[128,512]{1,0:T(8,128)(2,1)S(1)} %collective-permute-done.27.high, bf16[192,512]{1,0:T(8,128)(2,1)S(1)} %collective-permute-done.28.low, ...), custom_call_target="tpu_custom_call" | custom-call | flops 268435456 | bytes 1900544 | tf_op jit(solution)/shard_map/pallas_call | solution.py:219
  92.0 2.5 %collective-permute-done.25 = bf16[512,256]{1,0:T(8,128)(2,1)S(1)} collective-permute-done((bf16[512,256]{1,0:T(8,128)(2,1)S(1)}, bf16[512,256]{1,0:T(8,128)(2,1)S(1)}, u32[]{:S(2)}, u32[]{:S(2)}) %collective-permute-start.25) | collective-permute-done | bytes 262176 | tf_op jit(solution)/shard_map/ppermute | solution.py:31
  94.5 1.8 %collective-permute-start.29 = (bf16[192,256]{1,0:T(8,128)(2,1)S(1)}, bf16[192,256]{1,0:T(8,128)(2,1)S(1)}, u32[]{:S(2)}, u32[]{:S(2)}) collective-permute-start(bf16[192,256]{1,0:T(8,128)(2,1)S(1)} %add_convert_fusion.6), channel_id=1, source_target_pairs={{0,96},{4,100},{8,104},{12,108},{16,112},{20,116},{24,120},{28,124... | collective-permute-start | bytes 294920 | tf_op jit(solution)/shard_map/ppermute | solution.py:31
  96.3 3.3 %collective-permute-start.30 = (bf16[128,256]{1,0:T(8,128)(2,1)S(1)}, bf16[128,256]{1,0:T(8,128)(2,1)S(1)}, u32[]{:S(2)}, u32[]{:S(2)}) collective-permute-start(bf16[128,256]{1,0:T(8,128)(2,1)S(1)} %add_convert_fusion.7), channel_id=1, source_target_pairs={{0,160},{4,164},{8,168},{12,172},{16,176},{20,180},{24,184},{28,18... | collective-permute-start | bytes 196616 | tf_op jit(solution)/shard_map/ppermute | solution.py:31
  99.8 0.8 collective-permute-start.31
  100.6 0.7 collective-permute-start.32
  101.3 1.3 %collective-permute-start.33 = (bf16[512,128]{1,0:T(8,128)(2,1)S(1)}, bf16[512,128]{1,0:T(8,128)(2,1)S(1)}, u32[]{:S(2)}, u32[]{:S(2)}) collective-permute-start(bf16[512,128]{1,0:T(8,128)(2,1)S(1)} %get-tuple-element.117), channel_id=1, source_target_pairs={{0,8},{4,12},{8,16},{12,20},{16,24},{20,28},{24,0},{28,4},{32,40},... | collective-permute-start | bytes 393224 | tf_op jit(solution)/shard_map/ppermute | solution.py:31
  102.6 0.8 collective-permute-done.29
  103.4 1.4 %collective-permute-done.31 = bf16[512,128]{1,0:T(8,128)(2,1)S(1)} collective-permute-done((bf16[512,128]{1,0:T(8,128)(2,1)S(1)}, bf16[512,128]{1,0:T(8,128)(2,1)S(1)}, u32[]{:S(2)}, u32[]{:S(2)}) %collective-permute-start.31) | collective-permute-done | bytes 131104 | tf_op jit(solution)/shard_map/ppermute | solution.py:31
  104.9 2.3 %collective-permute-done.32 = bf16[512,128]{1,0:T(8,128)(2,1)S(1)} collective-permute-done((bf16[512,128]{1,0:T(8,128)(2,1)S(1)}, bf16[512,128]{1,0:T(8,128)(2,1)S(1)}, u32[]{:S(2)}, u32[]{:S(2)}) %collective-permute-start.32) | collective-permute-done | bytes 131104 | tf_op jit(solution)/shard_map/ppermute | solution.py:31
  107.2 1.3 %collective-permute-done.33 = bf16[512,128]{1,0:T(8,128)(2,1)S(1)} collective-permute-done((bf16[512,128]{1,0:T(8,128)(2,1)S(1)}, bf16[512,128]{1,0:T(8,128)(2,1)S(1)}, u32[]{:S(2)}, u32[]{:S(2)}) %collective-permute-start.33) | collective-permute-done | bytes 131104 | tf_op jit(solution)/shard_map/ppermute | solution.py:31
  108.6 2.0 %collective-permute-start.35 = (bf16[64,256]{1,0:T(8,128)(2,1)S(1)}, bf16[64,256]{1,0:T(8,128)(2,1)S(1)}, u32[]{:S(2)}, u32[]{:S(2)}) collective-permute-start(bf16[64,256]{1,0:T(8,128)(2,1)S(1)} %get-tuple-element.120), channel_id=1, source_target_pairs={{0,32},{4,36},{8,40},{12,44},{16,48},{20,52},{24,56},{28,60},{32,6... | collective-permute-start | bytes 98312 | tf_op jit(solution)/shard_map/ppermute | solution.py:31
  110.6 0.5 divide_select_fusion
  111.2 1.4 %collective-permute-done.34 = bf16[64,256]{1,0:T(8,128)(2,1)S(1)} collective-permute-done((bf16[64,256]{1,0:T(8,128)(2,1)S(1)}, bf16[64,256]{1,0:T(8,128)(2,1)S(1)}, u32[]{:S(2)}, u32[]{:S(2)}) %collective-permute-start.34) | collective-permute-done | bytes 32800 | tf_op jit(solution)/shard_map/ppermute | solution.py:31
  112.5 1.3 %collective-permute-done.35 = bf16[64,256]{1,0:T(8,128)(2,1)S(1)} collective-permute-done((bf16[64,256]{1,0:T(8,128)(2,1)S(1)}, bf16[64,256]{1,0:T(8,128)(2,1)S(1)}, u32[]{:S(2)}, u32[]{:S(2)}) %collective-permute-start.35) | collective-permute-done | bytes 32800 | tf_op jit(solution)/shard_map/ppermute | solution.py:31
  113.9 0.6 fusion.10
  114.7 0.7 copy.15
  (61 shorter events, 1.9 us)
Async XLA Ops:
  0.6 2.9 %copy-start = (bf16[256,1024]{1,0:T(8,128)(2,1)S(1)}, bf16[256,1024]{1,0:T(8,128)(2,1)}, u32[]{:S(2)}) copy-start(bf16[256,1024]{1,0:T(8,128)(2,1)} %param.9) | copy-start | bytes 1572868
  0.6 46.8 %copy-start.3 = (bf16[64,512]{1,0:T(8,128)(2,1)S(1)}, bf16[64,512]{1,0:T(8,128)(2,1)}, u32[]{:S(2)}) copy-start(bf16[64,512]{1,0:T(8,128)(2,1)} %q_ref.7) | copy-start | bytes 196612
  4.5 10.2 %collective-permute-start = (bf16[64,256]{1,0:T(8,128)(2,1)S(1)}, bf16[64,256]{1,0:T(8,128)(2,1)S(1)}, u32[]{:S(2)}, u32[]{:S(2)}) collective-permute-start(bf16[64,256]{1,0:T(8,128)(2,1)S(1)} %pad_maximum_fusion.5), channel_id=1, source_target_pairs={{0,32},{4,36},{8,40},{12,44},{16,48},{20,52},{24,56},{28,60},{32,6... | collective-permute-start | bytes 98312 | tf_op jit(solution)/shard_map/ppermute | solution.py:31
  6.5 8.2 %collective-permute-start.1 = (bf16[64,256]{1,0:T(8,128)(2,1)S(1)}, bf16[64,256]{1,0:T(8,128)(2,1)S(1)}, u32[]{:S(2)}, u32[]{:S(2)}) collective-permute-start(bf16[64,256]{1,0:T(8,128)(2,1)S(1)} %pad_maximum_fusion.5), channel_id=1, source_target_pairs={{0,224},{4,228},{8,232},{12,236},{16,240},{20,244},{24,248},{28,25... | collective-permute-start | bytes 98312 | tf_op jit(solution)/shard_map/ppermute | solution.py:31
  10.5 5.0 %collective-permute-start.2 = (bf16[64,1024]{1,0:T(8,128)(2,1)S(1)}, bf16[64,1024]{1,0:T(8,128)(2,1)S(1)}, u32[]{:S(2)}, u32[]{:S(2)}) collective-permute-start(bf16[64,1024]{1,0:T(8,128)(2,1)S(1)} %fusion.1.refs_0_), channel_id=1, source_target_pairs={{0,1},{1,2},{2,3},{3,0},{4,5},{5,6},{6,7},{7,4},{8,9},{9,10},{10,1... | collective-permute-start | bytes 393224 | tf_op jit(solution)/shard_map/ppermute | solution.py:35
  12.0 6.4 %collective-permute-start.3 = (bf16[64,1024]{1,0:T(8,128)(2,1)S(1)}, bf16[64,1024]{1,0:T(8,128)(2,1)S(1)}, u32[]{:S(2)}, u32[]{:S(2)}) collective-permute-start(bf16[64,1024]{1,0:T(8,128)(2,1)S(1)} %fusion.1.refs_0_), channel_id=1, source_target_pairs={{0,3},{1,0},{2,1},{3,2},{4,7},{5,4},{6,5},{7,6},{8,11},{9,8},{10,9... | collective-permute-start | bytes 393224 | tf_op jit(solution)/shard_map/ppermute | solution.py:35
  12.5 11.0 %collective-permute-start.6 = (bf16[64,1024]{1,0:T(8,128)(2,1)S(1)}, bf16[64,1024]{1,0:T(8,128)(2,1)S(1)}, u32[]{:S(2)}, u32[]{:S(2)}) collective-permute-start(bf16[64,1024]{1,0:T(8,128)(2,1)S(1)} %fusion.1.refs_0_), channel_id=1, source_target_pairs={{0,2},{1,3},{2,0},{3,1},{4,6},{5,7},{6,4},{7,5},{8,10},{9,11},{10,... | collective-permute-start | bytes 393224 | tf_op jit(solution)/shard_map/ppermute | solution.py:35
  18.4 9.4 %collective-permute-start.5 = (bf16[192,256]{1,0:T(8,128)(2,1)S(1)}, bf16[192,256]{1,0:T(8,128)(2,1)S(1)}, u32[]{:S(2)}, u32[]{:S(2)}) collective-permute-start(bf16[192,256]{1,0:T(8,128)(2,1)S(1)} %pad_maximum_fusion.4), channel_id=1, source_target_pairs={{0,96},{4,100},{8,104},{12,108},{16,112},{20,116},{24,120},{28,124... | collective-permute-start | bytes 294920 | tf_op jit(solution)/shard_map/ppermute | solution.py:31
  20.2 7.4 %collective-permute-start.4 = (bf16[128,256]{1,0:T(8,128)(2,1)S(1)}, bf16[128,256]{1,0:T(8,128)(2,1)S(1)}, u32[]{:S(2)}, u32[]{:S(2)}) collective-permute-start(bf16[128,256]{1,0:T(8,128)(2,1)S(1)} %slice.142), channel_id=1, source_target_pairs={{0,160},{4,164},{8,168},{12,172},{16,176},{20,180},{24,184},{28,18... | collective-permute-start | bytes 196616 | tf_op jit(solution)/shard_map/ppermute | solution.py:31
  23.5 2.2 %copy-start.1 = (bf16[512,4096]{1,0:T(8,128)(2,1)S(1)}, bf16[512,4096]{1,0:T(8,128)(2,1)}, u32[]{:S(2)}) copy-start(bf16[512,4096]{1,0:T(8,128)(2,1)} %w_ref.1) | copy-start | bytes 12582916
  27.8 18.5 %collective-permute-start.7 = (bf16[512,256]{1,0:T(8,128)(2,1)S(1)}, bf16[512,256]{1,0:T(8,128)(2,1)S(1)}, u32[]{:S(2)}, u32[]{:S(2)}) collective-permute-start(bf16[512,256]{1,0:T(8,128)(2,1)S(1)} %pad_maximum_fusion.refs_0_), channel_id=1, source_target_pairs={{0,8},{4,12},{8,16},{12,20},{16,24},{20,28},{24,0},{28,4},{32,40},... | collective-permute-start | bytes 786440 | tf_op jit(solution)/shard_map/ppermute | solution.py:31
  29.4 16.8 %collective-permute-start.8 = (bf16[512,256]{1,0:T(8,128)(2,1)S(1)}, bf16[512,256]{1,0:T(8,128)(2,1)S(1)}, u32[]{:S(2)}, u32[]{:S(2)}) collective-permute-start(bf16[512,256]{1,0:T(8,128)(2,1)S(1)} %pad_maximum_fusion.refs_0_), channel_id=1, source_target_pairs={{0,24},{4,28},{8,0},{12,4},{16,8},{20,12},{24,16},{28,20},{32,56},... | collective-permute-start | bytes 786440 | tf_op jit(solution)/shard_map/ppermute | solution.py:31
  31.1 15.2 %collective-permute-start.9 = (bf16[512,256]{1,0:T(8,128)(2,1)S(1)}, bf16[512,256]{1,0:T(8,128)(2,1)S(1)}, u32[]{:S(2)}, u32[]{:S(2)}) collective-permute-start(bf16[512,256]{1,0:T(8,128)(2,1)S(1)} %pad_maximum_fusion.refs_0_), channel_id=1, source_target_pairs={{0,16},{4,20},{8,24},{12,28},{16,0},{20,4},{24,8},{28,12},{32,48},... | collective-permute-start | bytes 786440 | tf_op jit(solution)/shard_map/ppermute | solution.py:31
  33.1 13.2 %collective-permute-start.10 = (bf16[192,512]{1,0:T(8,128)(2,1)S(1)}, bf16[192,512]{1,0:T(8,128)(2,1)S(1)}, u32[]{:S(2)}, u32[]{:S(2)}) collective-permute-start(bf16[192,512]{1,0:T(8,128)(2,1)S(1)} %get-tuple-element.72), channel_id=1, source_target_pairs={{0,96},{4,100},{8,104},{12,108},{16,112},{20,116},{24,120},{28,124... | collective-permute-start | bytes 589832 | tf_op jit(solution)/shard_map/ppermute | solution.py:31
  35.8 7.7 %collective-permute-start.11 = (bf16[128,512]{1,0:T(8,128)(2,1)S(1)}, bf16[128,512]{1,0:T(8,128)(2,1)S(1)}, u32[]{:S(2)}, u32[]{:S(2)}) collective-permute-start(bf16[128,512]{1,0:T(8,128)(2,1)S(1)} %get-tuple-element.73), channel_id=1, source_target_pairs={{0,160},{4,164},{8,168},{12,172},{16,176},{20,180},{24,184},{28,18... | collective-permute-start | bytes 393224 | tf_op jit(solution)/shard_map/ppermute | solution.py:31
  38.1 19.9 %copy-start.2 = (bf16[512,4096]{1,0:T(8,128)(2,1)S(1)}, bf16[512,4096]{1,0:T(8,128)(2,1)}, u32[]{:S(2)}) copy-start(bf16[512,4096]{1,0:T(8,128)(2,1)} %w_ref.1) | copy-start | bytes 12582916
  46.3 3.6 %collective-permute-start.12 = (bf16[512,256]{1,0:T(8,128)(2,1)S(1)}, bf16[512,256]{1,0:T(8,128)(2,1)S(1)}, u32[]{:S(2)}, u32[]{:S(2)}) collective-permute-start(bf16[512,256]{1,0:T(8,128)(2,1)S(1)} %pad_maximum_fusion.refs_0_), channel_id=1, source_target_pairs={{0,4},{4,0},{8,12},{12,8},{16,20},{20,16},{24,28},{28,24},{32,36},... | collective-permute-start | bytes 786440 | tf_op jit(solution)/shard_map/ppermute | solution.py:31
  46.4 3.5 %collective-permute-start.13 = (bf16[512,256]{1,0:T(8,128)(2,1)S(1)}, bf16[512,256]{1,0:T(8,128)(2,1)S(1)}, u32[]{:S(2)}, u32[]{:S(2)}) collective-permute-start(bf16[512,256]{1,0:T(8,128)(2,1)S(1)} %collective-permute-done.7.refs_1_), channel_id=1, source_target_pairs={{0,4},{4,0},{8,12},{12,8},{16,20},{20,16},{24,28},{28,24},{32,36},... | collective-permute-start | bytes 786440 | tf_op jit(solution)/shard_map/ppermute | solution.py:31
  46.9 3.0 %collective-permute-start.14 = (bf16[512,256]{1,0:T(8,128)(2,1)S(1)}, bf16[512,256]{1,0:T(8,128)(2,1)S(1)}, u32[]{:S(2)}, u32[]{:S(2)}) collective-permute-start(bf16[512,256]{1,0:T(8,128)(2,1)S(1)} %collective-permute-done.8.refs_2_), channel_id=1, source_target_pairs={{0,4},{4,0},{8,12},{12,8},{16,20},{20,16},{24,28},{28,24},{32,36},... | collective-permute-start | bytes 786440 | tf_op jit(solution)/shard_map/ppermute | solution.py:31
  47.0 2.9 %collective-permute-start.15 = (bf16[512,256]{1,0:T(8,128)(2,1)S(1)}, bf16[512,256]{1,0:T(8,128)(2,1)S(1)}, u32[]{:S(2)}, u32[]{:S(2)}) collective-permute-start(bf16[512,256]{1,0:T(8,128)(2,1)S(1)} %collective-permute-done.9.refs_3_), channel_id=1, source_target_pairs={{0,4},{4,0},{8,12},{12,8},{16,20},{20,16},{24,28},{28,24},{32,36},... | collective-permute-start | bytes 786440 | tf_op jit(solution)/shard_map/ppermute | solution.py:31
  54.5 18.1 %collective-permute-start.19 = (bf16[2048,256]{1,0:T(8,128)(2,1)S(1)}, bf16[2048,256]{1,0:T(8,128)(2,1)S(1)}, u32[]{:S(2)}, u32[]{:S(2)}) collective-permute-start(bf16[2048,256]{1,0:T(8,128)(2,1)S(1)} %get-tuple-element.94), channel_id=1, source_target_pairs={{0,4},{4,0},{8,12},{12,8},{16,20},{20,16},{24,28},{28,24},{32,36},... | collective-permute-start | bytes 3145736 | tf_op jit(solution)/shard_map/ppermute | solution.py:31
  54.7 9.1 %collective-permute-start.20 = (bf16[64,512]{1,0:T(8,128)(2,1)S(1)}, bf16[64,512]{1,0:T(8,128)(2,1)S(1)}, u32[]{:S(2)}, u32[]{:S(2)}) collective-permute-start(bf16[64,512]{1,0:T(8,128)(2,1)S(1)} %get-tuple-element.84.att_ref), channel_id=1, source_target_pairs={{0,32},{4,36},{8,40},{12,44},{16,48},{20,52},{24,56},{28,60},{32,6... | collective-permute-start | bytes 196616 | tf_op jit(solution)/shard_map/ppermute | solution.py:31
  56.3 12.6 %collective-permute-start.21 = (bf16[64,512]{1,0:T(8,128)(2,1)S(1)}, bf16[64,512]{1,0:T(8,128)(2,1)S(1)}, u32[]{:S(2)}, u32[]{:S(2)}) collective-permute-start(bf16[64,512]{1,0:T(8,128)(2,1)S(1)} %get-tuple-element.84.att_ref), channel_id=1, source_target_pairs={{0,224},{4,228},{8,232},{12,236},{16,240},{20,244},{24,248},{28,25... | collective-permute-start | bytes 196616 | tf_op jit(solution)/shard_map/ppermute | solution.py:31
  59.4 25.3 %copy-start.4 = (bf16[256,1024]{1,0:T(8,128)(2,1)S(1)}, bf16[256,1024]{1,0:T(8,128)(2,1)}, u32[]{:S(2)}) copy-start(bf16[256,1024]{1,0:T(8,128)(2,1)} %param.8) | copy-start | bytes 1572868
  59.4 25.2 %copy-start.5 = (s32[64]{0:T(128)S(1)}, s32[64]{0:T(128)}, u32[]{:S(2)}) copy-start(s32[64]{0:T(128)} %param.10) | copy-start | bytes 772
  59.5 11.2 %collective-permute-start.16 = (bf16[64,1152]{1,0:T(8,128)(2,1)S(1)}, bf16[64,1152]{1,0:T(8,128)(2,1)S(1)}, u32[]{:S(2)}, u32[]{:S(2)}) collective-permute-start(bf16[64,1152]{1,0:T(8,128)(2,1)S(1)} %get-tuple-element.87), channel_id=1, source_target_pairs={{0,3},{1,0},{2,1},{3,2},{4,7},{5,4},{6,5},{7,6},{8,11},{9,8},{10,9... | collective-permute-start | bytes 442376 | tf_op jit(solution)/shard_map/ppermute | solution.py:35
  59.9 12.6 %collective-permute-start.17 = (bf16[64,1152]{1,0:T(8,128)(2,1)S(1)}, bf16[64,1152]{1,0:T(8,128)(2,1)S(1)}, u32[]{:S(2)}, u32[]{:S(2)}) collective-permute-start(bf16[64,1152]{1,0:T(8,128)(2,1)S(1)} %get-tuple-element.88), channel_id=1, source_target_pairs={{0,1},{1,2},{2,3},{3,0},{4,5},{5,6},{6,7},{7,4},{8,9},{9,10},{10,1... | collective-permute-start | bytes 442376 | tf_op jit(solution)/shard_map/ppermute | solution.py:35
  63.8 8.6 %collective-permute-start.18 = (bf16[64,1152]{1,0:T(8,128)(2,1)S(1)}, bf16[64,1152]{1,0:T(8,128)(2,1)S(1)}, u32[]{:S(2)}, u32[]{:S(2)}) collective-permute-start(bf16[64,1152]{1,0:T(8,128)(2,1)S(1)} %get-tuple-element.89), channel_id=1, source_target_pairs={{0,2},{1,3},{2,0},{3,1},{4,6},{5,7},{6,4},{7,5},{8,10},{9,11},{10,... | collective-permute-start | bytes 442376 | tf_op jit(solution)/shard_map/ppermute | solution.py:35
  68.9 7.0 %collective-permute-start.22 = (bf16[192,512]{1,0:T(8,128)(2,1)S(1)}, bf16[192,512]{1,0:T(8,128)(2,1)S(1)}, u32[]{:S(2)}, u32[]{:S(2)}) collective-permute-start(bf16[192,512]{1,0:T(8,128)(2,1)S(1)} %pad_maximum_fusion.2), channel_id=1, source_target_pairs={{0,32},{4,36},{8,40},{12,44},{16,48},{20,52},{24,56},{28,60},{32,6... | collective-permute-start | bytes 589832 | tf_op jit(solution)/shard_map/ppermute | solution.py:31
  70.6 5.3 %collective-permute-start.23 = (bf16[128,512]{1,0:T(8,128)(2,1)S(1)}, bf16[128,512]{1,0:T(8,128)(2,1)S(1)}, u32[]{:S(2)}, u32[]{:S(2)}) collective-permute-start(bf16[128,512]{1,0:T(8,128)(2,1)S(1)} %pad_maximum_fusion.3), channel_id=1, source_target_pairs={{0,224},{4,228},{8,232},{12,236},{16,240},{20,244},{24,248},{28,25... | collective-permute-start | bytes 393224 | tf_op jit(solution)/shard_map/ppermute | solution.py:31
  72.5 38.1 %copy-start.6 = (f32[64]{0:T(128)S(1)}, f32[64]{0:T(128)}, u32[]{:S(2)}) copy-start(f32[64]{0:T(128)} %param.14) | copy-start | bytes 772
  76.0 14.7 %collective-permute-start.28 = (bf16[192,512]{1,0:T(8,128)(2,1)S(1)}, bf16[192,512]{1,0:T(8,128)(2,1)S(1)}, u32[]{:S(2)}, u32[]{:S(2)}) collective-permute-start(bf16[192,512]{1,0:T(8,128)(2,1)S(1)} %pad_maximum_fusion.1.near), channel_id=1, source_target_pairs={{0,96},{4,100},{8,104},{12,108},{16,112},{20,116},{24,120},{28,124... | collective-permute-start | bytes 589832 | tf_op jit(solution)/shard_map/ppermute | solution.py:31
  79.5 9.2 %collective-permute-start.27 = (bf16[128,512]{1,0:T(8,128)(2,1)S(1)}, bf16[128,512]{1,0:T(8,128)(2,1)S(1)}, u32[]{:S(2)}, u32[]{:S(2)}) collective-permute-start(bf16[128,512]{1,0:T(8,128)(2,1)S(1)} %slice.153), channel_id=1, source_target_pairs={{0,160},{4,164},{8,168},{12,172},{16,176},{20,180},{24,184},{28,18... | collective-permute-start | bytes 393224 | tf_op jit(solution)/shard_map/ppermute | solution.py:31
  81.1 10.9 %collective-permute-start.24 = (bf16[512,256]{1,0:T(8,128)(2,1)S(1)}, bf16[512,256]{1,0:T(8,128)(2,1)S(1)}, u32[]{:S(2)}, u32[]{:S(2)}) collective-permute-start(bf16[512,256]{1,0:T(8,128)(2,1)S(1)} %get-tuple-element.102), channel_id=1, source_target_pairs={{0,24},{4,28},{8,0},{12,4},{16,8},{20,12},{24,16},{28,20},{32,56},... | collective-permute-start | bytes 786440 | tf_op jit(solution)/shard_map/ppermute | solution.py:31
  82.1 12.3 %collective-permute-start.25 = (bf16[512,256]{1,0:T(8,128)(2,1)S(1)}, bf16[512,256]{1,0:T(8,128)(2,1)S(1)}, u32[]{:S(2)}, u32[]{:S(2)}) collective-permute-start(bf16[512,256]{1,0:T(8,128)(2,1)S(1)} %get-tuple-element.103), channel_id=1, source_target_pairs={{0,8},{4,12},{8,16},{12,20},{16,24},{20,28},{24,0},{28,4},{32,40},... | collective-permute-start | bytes 786440 | tf_op jit(solution)/shard_map/ppermute | solution.py:31
  83.1 11.3 %collective-permute-start.26 = (bf16[512,256]{1,0:T(8,128)(2,1)S(1)}, bf16[512,256]{1,0:T(8,128)(2,1)S(1)}, u32[]{:S(2)}, u32[]{:S(2)}) collective-permute-start(bf16[512,256]{1,0:T(8,128)(2,1)S(1)} %get-tuple-element.104), channel_id=1, source_target_pairs={{0,16},{4,20},{8,24},{12,28},{16,0},{20,4},{24,8},{28,12},{32,48},... | collective-permute-start | bytes 786440 | tf_op jit(solution)/shard_map/ppermute | solution.py:31
  94.5 8.8 %collective-permute-start.29 = (bf16[192,256]{1,0:T(8,128)(2,1)S(1)}, bf16[192,256]{1,0:T(8,128)(2,1)S(1)}, u32[]{:S(2)}, u32[]{:S(2)}) collective-permute-start(bf16[192,256]{1,0:T(8,128)(2,1)S(1)} %add_convert_fusion.6), channel_id=1, source_target_pairs={{0,96},{4,100},{8,104},{12,108},{16,112},{20,116},{24,120},{28,124... | collective-permute-start | bytes 294920 | tf_op jit(solution)/shard_map/ppermute | solution.py:31
  96.3 6.2 %collective-permute-start.30 = (bf16[128,256]{1,0:T(8,128)(2,1)S(1)}, bf16[128,256]{1,0:T(8,128)(2,1)S(1)}, u32[]{:S(2)}, u32[]{:S(2)}) collective-permute-start(bf16[128,256]{1,0:T(8,128)(2,1)S(1)} %add_convert_fusion.7), channel_id=1, source_target_pairs={{0,160},{4,164},{8,168},{12,172},{16,176},{20,180},{24,184},{28,18... | collective-permute-start | bytes 196616 | tf_op jit(solution)/shard_map/ppermute | solution.py:31
  99.8 5.0 %collective-permute-start.31 = (bf16[512,128]{1,0:T(8,128)(2,1)S(1)}, bf16[512,128]{1,0:T(8,128)(2,1)S(1)}, u32[]{:S(2)}, u32[]{:S(2)}) collective-permute-start(bf16[512,128]{1,0:T(8,128)(2,1)S(1)} %get-tuple-element.115), channel_id=1, source_target_pairs={{0,24},{4,28},{8,0},{12,4},{16,8},{20,12},{24,16},{28,20},{32,56},... | collective-permute-start | bytes 393224 | tf_op jit(solution)/shard_map/ppermute | solution.py:31
  100.6 6.6 %collective-permute-start.32 = (bf16[512,128]{1,0:T(8,128)(2,1)S(1)}, bf16[512,128]{1,0:T(8,128)(2,1)S(1)}, u32[]{:S(2)}, u32[]{:S(2)}) collective-permute-start(bf16[512,128]{1,0:T(8,128)(2,1)S(1)} %get-tuple-element.116), channel_id=1, source_target_pairs={{0,16},{4,20},{8,24},{12,28},{16,0},{20,4},{24,8},{28,12},{32,48},... | collective-permute-start | bytes 393224 | tf_op jit(solution)/shard_map/ppermute | solution.py:31
  101.3 7.2 %collective-permute-start.33 = (bf16[512,128]{1,0:T(8,128)(2,1)S(1)}, bf16[512,128]{1,0:T(8,128)(2,1)S(1)}, u32[]{:S(2)}, u32[]{:S(2)}) collective-permute-start(bf16[512,128]{1,0:T(8,128)(2,1)S(1)} %get-tuple-element.117), channel_id=1, source_target_pairs={{0,8},{4,12},{8,16},{12,20},{16,24},{20,28},{24,0},{28,4},{32,40},... | collective-permute-start | bytes 393224 | tf_op jit(solution)/shard_map/ppermute | solution.py:31
  108.5 4.0 %collective-permute-start.34 = (bf16[64,256]{1,0:T(8,128)(2,1)S(1)}, bf16[64,256]{1,0:T(8,128)(2,1)S(1)}, u32[]{:S(2)}, u32[]{:S(2)}) collective-permute-start(bf16[64,256]{1,0:T(8,128)(2,1)S(1)} %get-tuple-element.119), channel_id=1, source_target_pairs={{0,224},{4,228},{8,232},{12,236},{16,240},{20,244},{24,248},{28,25... | collective-permute-start | bytes 98312 | tf_op jit(solution)/shard_map/ppermute | solution.py:31
  108.6 5.2 %collective-permute-start.35 = (bf16[64,256]{1,0:T(8,128)(2,1)S(1)}, bf16[64,256]{1,0:T(8,128)(2,1)S(1)}, u32[]{:S(2)}, u32[]{:S(2)}) collective-permute-start(bf16[64,256]{1,0:T(8,128)(2,1)S(1)} %get-tuple-element.120), channel_id=1, source_target_pairs={{0,32},{4,36},{8,40},{12,44},{16,48},{20,52},{24,56},{28,60},{32,6... | collective-permute-start | bytes 98312 | tf_op jit(solution)/shard_map/ppermute | solution.py:31
  111.2 3.4 %collective-permute-start.36 = (bf16[512,128]{1,0:T(8,128)(2,1)S(1)}, bf16[512,128]{1,0:T(8,128)(2,1)S(1)}, u32[]{:S(2)}, u32[]{:S(2)}) collective-permute-start(bf16[512,128]{1,0:T(8,128)(2,1)S(1)} %add_convert_fusion.5), channel_id=1, source_target_pairs={{0,4},{4,0},{8,12},{12,8},{16,20},{20,16},{24,28},{28,24},{32,36},... | collective-permute-start | bytes 393224 | tf_op jit(solution)/shard_map/ppermute | solution.py:31
where the time goes:
time: 116 us; the launch traced here: 115 us
  starting transfers between devices  58.8 us (51%)
  waiting for transfers between devices  30.8 us (27%)
  Pallas kernels  13.9 us (12%)
  other arithmetic  5.27 us (5%)
  local copies, waits for them, and re-layouts  3.61 us (3%)
  matrix products  2.09 us (2%)
    ppermute x31, starting transfers between devices, seq_move(): return lax.ppermute(a, 'seq', pairs)  48.2 us
    ppermute x31, waiting for transfers between devices, seq_move(): return lax.ppermute(a, 'seq', pairs)  27.1 us
    pallas_call x7, Pallas kernels, call(): pl.pallas_call(kernel, out_shape=shapes, in_specs=[SM] + [VM] * len(args)...  13.9 us
    ppermute x6, starting transfers between devices, tp_move(): return lax.ppermute(a, 'tp', [(x, (x + dx) % NX) for x in range(NX)])  10.6 us
    ppermute x6, waiting for transfers between devices, tp_move(): return lax.ppermute(a, 'tp', [(x, (x + dx) % NX) for x in range(NX)])  3.7 us
    unnamed x15, local copies, waits for them, and re-layouts  2.95 us
  transfers between devices with their start and end apart: 37, of which 15 were waited for; matrix products, arithmetic and copies ran while one was open for 3% of the time, Pallas kernels for 8%

commit v1 on v0

--- a/solution.py
+++ b/solution.py
@@ -35,14 +35,31 @@
     return lax.ppermute(a, "tp", [(x, (x + dx) % NX) for x in range(NX)])
 
 
-def near_z(a):
-    return jnp.concatenate([seq_move(a, dz=1), a, seq_move(a, dz=-1)], axis=0)
-
-
-def far_z(near):
-    low = seq_move(near, dz=3)
-    high = seq_move(near[: 2 * near.shape[0] // 3], dz=-3)
-    return high, low, near
+LINES = [[(k * NY + j) * NC + i for k in range(NZ)] for j in range(NY) for i in range(NC)]
+
+
+def exchange_z(a):
+    return lax.all_to_all(
+        a, "seq", split_axis=0, concat_axis=0, axis_index_groups=LINES, tiled=True
+    )
+
+
+def sum_far(parts):
+    n = SLOTS
+    up = add(*[p[: 3 * n] for p in parts]).astype(BF)
+    down = add(*[p[3 * n : 5 * n] for p in parts]).astype(BF)
+    return seq_move(up, dz=3), seq_move(down, dz=-3), [p[5 * n :] for p in parts]
+
+
+def sum_near(low, high, near):
+    n = SLOTS
+    below = add(*[p[:n] for p in near], low[:n]).astype(BF)
+    above = add(*[p[2 * n :] for p in near], low[2 * n :], high[n:]).astype(BF)
+    return below, above, add(*[p[n : 2 * n] for p in near], low[n : 2 * n], high[:n])
+
+
+def sum_last(below, above, here):
+    return add(here, seq_move(below, dz=-1), seq_move(above, dz=1))
 
 
 def stage(values, *others):
@@ -66,7 +83,7 @@
     other_c = c ^ dc
     out = []
     for k in range(NZ):
-        shard = (((z + 2 + k) & (NZ - 1)) * NY + other_y) * NC + other_c
+        shard = (k * NY + other_y) * NC + other_c
         live = kv_ref[k * SLOTS : (k + 1) * SLOTS, HEAD : HEAD + 1].astype(F32) < 0.5 * DEAD
         ok = jnp.logical_and(diff <= (own - shard) * SLOTS, live)
         piece = scores[k * SLOTS : (k + 1) * SLOTS] * (SCALE * LOG2E)
@@ -104,15 +121,20 @@
         total = total * old + jnp.sum(e, axis=0, keepdims=True)
         acc = acc * old + dot(kv_ref[:, HEAD:], e.astype(BF), 0, 0)
         top = new_top
+    if last:
+        pieces, refs = refs[:NY], refs[NY:]
     if not last:
         refs[0][0:8] = jnp.broadcast_to(top, (8, HEADS * SLOTS))
         refs[0][8:16] = jnp.broadcast_to(total, (8, HEADS * SLOTS))
         refs[1][...] = acc
         return
-    att_ref, lse_ref = refs
+    att_ref, lse_ref, rows = refs[0], refs[1], refs[2:]
     out = (acc / total).T.astype(BF)
     for h in range(HEADS):
-        att_ref[:, h * HEAD : (h + 1) * HEAD] = out[h * SLOTS : (h + 1) * SLOTS]
+        for ref in (att_ref, *rows):
+            ref[:, h * HEAD : (h + 1) * HEAD] = out[h * SLOTS : (h + 1) * SLOTS]
+    for ref, piece in zip(rows, pieces):
+        ref[:, HEADS * HEAD :] = piece[...]
     lse_ref[...] = jnp.broadcast_to(top + jnp.log(total) * LOG2E, lse_ref.shape)
 
 
@@ -138,8 +160,13 @@
         p = jnp.exp2(t - lse)
         dp = dot(kv_ref[:, HEAD:], g_rows, 1, 1)
         ds = (p * (dp - delta)).astype(BF)
-        out_ref[:, :HEAD] = (dot(ds, q_rows, 1, 0) * SCALE).astype(BF)
-        out_ref[:, HEAD:] = dot(p.astype(BF), g_rows, 1, 0).astype(BF)
+        key_grad = (dot(ds, q_rows, 1, 0) * SCALE).astype(BF)
+        value_grad = dot(p.astype(BF), g_rows, 1, 0).astype(BF)
+        for k in range(NZ):
+            start = ((k + NZ - 2 - place[0]) & (NZ - 1)) * SLOTS
+            at = pl.ds(pl.multiple_of(start, SLOTS), SLOTS)
+            out_ref[at, :HEAD] = key_grad[k * SLOTS : (k + 1) * SLOTS]
+            out_ref[at, HEAD:] = value_grad[k * SLOTS : (k + 1) * SLOTS]
         acc = acc + dot(kv_ref[:, :HEAD], ds, 0, 0)
     if dc == 1:
         refs[1][...] = acc
@@ -150,8 +177,8 @@
 
 
 def attn_grad_kernel(place, *refs):
-    chunks, w_ref, g_ref, groups, full = refs[:4], refs[4], refs[5], refs[6:9], refs[9]
-    z, x = place[0], place[3]
+    chunks, w_ref, g_ref, pieces, full = refs[:4], refs[4], refs[5], refs[6:10], refs[10]
+    z, y, c, x = place[0], place[1], place[2], place[3]
     width = w_ref.shape[1] // NX
     acc = None
     for m in range(NX):
@@ -162,10 +189,19 @@
         acc = term if acc is None else acc + term
     g_ref[...] = acc.astype(BF)
     part = w_ref.shape[1] // NZ
-    for group, offsets in zip(groups, ((2, 3, 4), (5, 6), (7, 8, 9))):
-        for i, d in enumerate(offsets):
-            start = pl.multiple_of(((z + d) & (NZ - 1)) * part, part)
-            group[i * SLOTS : (i + 1) * SLOTS] = full[:, pl.ds(start, part)]
+    half = HEAD // NC
+    for m, piece in enumerate(pieces):
+        for k in range(0, NZ, 2):
+            pair = []
+            for d in (k, k + 1):
+                start = d * part + ((y + m) & (NY - 1)) * HEAD
+                pair.append(full[:, pl.ds(pl.multiple_of(start, HEAD), HEAD)].astype(F32))
+            first = jnp.concatenate([pair[0][:, :half], pair[1][:, :half]], axis=1)
+            second = jnp.concatenate([pair[0][:, half:], pair[1][:, half:]], axis=1)
+            mine = jnp.where(c == 0, first, second).astype(BF)
+            other = jnp.where(c == 0, second, first).astype(BF)
+            piece[:, k * half : (k + 2) * half] = mine
+            piece[:, (NZ + k) * half : (NZ + k + 2) * half] = other
 
 
 def project_kernel(place, att_ref, g_ref, w_ref, *outs):
@@ -185,28 +221,15 @@
         outs[m][:, width:] = extra.astype(BF)
 
 
-def weight_kernel(place, high, low, near, own, from_low, from_high, from_below, from_above, *refs):
-    outs, att, rows = refs[:NY], refs[NY], refs[NY + 1]
-    y = place[1]
-    att[: 2 * SLOTS] = high[...]
-    att[2 * SLOTS : 5 * SLOTS] = low[...]
-    att[5 * SLOTS :] = near[...]
-    order = (
-        (from_below, 2),
-        (from_high, 0),
-        (from_below, 1),
-        (from_low, 1),
-        (from_above, 1),
-        (from_below, 0),
-        (own, 1),
-        (from_above, 0),
-    )
-    for k, (ref, i) in enumerate(order):
-        rows[k * SLOTS : (k + 1) * SLOTS] = ref[i * SLOTS : (i + 1) * SLOTS]
-    width = rows.shape[1] // NY
-    for m in range(NY):
-        start = pl.multiple_of(((y + NY - m) & (NY - 1)) * width, width)
-        outs[m][...] = dot(att[...], rows[:, pl.ds(start, width)], 0, 0).astype(BF)
+def weight_kernel(place, *refs):
+    rows, (mine, other), (att, cols) = refs[:NY], refs[NY : NY + 2], refs[NY + 2 :]
+    feats = att.shape[1]
+    for i, ref in enumerate(rows):
+        att[i * SLOTS : (i + 1) * SLOTS] = ref[:, :feats]
+        cols[i * SLOTS : (i + 1) * SLOTS] = ref[:, feats:]
+    half = cols.shape[1] // NC
+    mine[...] = dot(cols[:, :half], att[...], 0, 0).astype(BF)
+    other[...] = dot(cols[:, half:], att[...], 0, 0).astype(BF)
 
 
 VM = pl.BlockSpec(memory_space=pltpu.VMEM)
@@ -258,25 +281,19 @@
         [rotated_key_slots, jnp.where(live_col, kept_value_slots, jnp.asarray(DEAD, BF))], axis=1
     )
 
-    kv, proj_grad = stage((kv, proj_grad))
-    kv_near = near_z(kv)
+    kv_z = exchange_z(jnp.broadcast_to(kv[None], (NZ, *kv.shape)).reshape(ROWS, 2 * HEAD))
     chunks = {m: tp_move(proj_grad, m) for m in (1, 3, 2)}
-    kv_near, chunks[1], chunks[3] = stage((kv_near, chunks[1], chunks[3]))
-    kv_z = jnp.concatenate(far_z(kv_near), axis=0)
-    attn_grad, far_up, far_down, own_part = call(
+    kv_z, chunks[1], chunks[2], chunks[3] = stage((kv_z, chunks[1], chunks[2], chunks[3]))
+    attn_grad, *pieces = call(
         attn_grad_kernel,
         place,
         [proj_grad, chunks[1], chunks[2], chunks[3], out_weight],
-        [shape((SLOTS, feats), BF)]
-        + [shape((n * SLOTS, width // NZ), BF) for n in (3, 2, 3)],
+        [shape((SLOTS, feats), BF)] + [shape((SLOTS, width // NY), BF)] * NY,
         2 * SLOTS * width * feats,
         [pltpu.VMEM((SLOTS, width), BF)],
     )
-    kv_z, far_up, far_down = stage((kv_z, far_up, far_down))
     kv_y = [kv_z, seq_move(kv_z, dy=1), seq_move(kv_z, dy=-1), seq_move(kv_z, dy=2)]
-    from_low = seq_move(far_up, dz=3)
-    from_high = seq_move(far_down, dz=-3)
-    kv_y = stage(kv_y, from_low, from_high)
+    *kv_y, attn_grad = stage((*kv_y, attn_grad))
     kv_c = [seq_move(a, dc=1) for a in kv_y]
     state = call(
         functools.partial(forward_kernel, FIRST, True, False),
@@ -285,20 +302,15 @@
         [shape((16, lanes), F32), shape((HEAD, lanes), F32)],
         4 * len(FIRST) * ROWS * lanes * HEAD,
     )
-    attended, lse = call(
+    attended, lse, *rows = call(
         functools.partial(forward_kernel, SECOND, False, True),
         place,
-        [query, *stage(kv_c, *state), *state],
-        [shape((SLOTS, feats), BF), shape((8, lanes), F32)],
+        [query, *stage(kv_c, *state), *state, *pieces],
+        [shape((SLOTS, feats), BF), shape((8, lanes), F32)]
+        + [shape((SLOTS, feats + width // NY), BF)] * NY,
         4 * len(SECOND) * ROWS * lanes * HEAD,
     )
-    n = SLOTS
-    for_above = jnp.concatenate([own_part[2 * n :], from_low[2 * n :], from_high[n:]], axis=0)
-    for_below = jnp.concatenate([own_part[:n], from_low[:n]], axis=0)
-    for_above, for_below = stage((for_above, for_below), attended)
-    att_near = near_z(attended)
-    from_below = seq_move(for_above, dz=1)
-    from_above = seq_move(for_below, dz=-1)
+    rows = [rows[0]] + [seq_move(rows[m], dy=m) for m in (1, 3, 2)]
     other, acc = call(
         functools.partial(backward_kernel, 1),
         place,
@@ -315,44 +327,33 @@
         [shape((ROWS, 2 * HEAD), BF)] * NY + [shape((SLOTS, feats), BF)],
         10 * NY * ROWS * lanes * HEAD,
     )
+    sums = [add(a, theirs[i * ROWS : (i + 1) * ROWS]).astype(BF) for i, a in enumerate(own)]
+    sums = stage(sums)
+    weight_mine, weight_other = call(
+        weight_kernel,
+        place,
+        rows,
+        [shape((width // NZ, feats), BF)] * 2,
+        4 * NY * SLOTS * feats * (width // NZ),
+        [pltpu.VMEM((NY * SLOTS, feats), BF), pltpu.VMEM((NY * SLOTS, width // NY), BF)],
+    )
+    weight_theirs = seq_move(weight_other, dc=1)
+    parts = [sums[0]] + [seq_move(sums[i], dy=-STEPS[i]) for i in range(1, NY)]
+    weight_sum = add(weight_mine, weight_theirs).astype(BF)
+    weight_sum = exchange_z(weight_sum)
+    parts = stage(parts)
     projected = call(
         project_kernel,
         place,
-        [attended, attn_grad, out_weight],
+        [stage((attended,), *parts)[0], attn_grad, out_weight],
         [shape((SLOTS, width // NX + HEAD), BF)] * NX,
         2 * SLOTS * width * feats,
     )
-    sums = [add(a, theirs[i * ROWS : (i + 1) * ROWS]).astype(BF) for i, a in enumerate(own)]
-    *sums, att_near = stage((*sums, att_near), from_below, from_above, *projected)
-    parts = [sums[0]] + [seq_move(sums[i], dy=-STEPS[i]) for i in range(1, NY)]
-    att_z = far_z(att_near)
     projected = [projected[0]] + [tp_move(projected[m], -m) for m in (1, 3, 2)]
-    weight_parts = call(
-        weight_kernel,
-        place,
-        [*att_z, own_part, from_low, from_high, from_below, from_above],
-        [shape((feats, width // NZ // NY), BF)] * NY,
-        2 * ROWS * feats * (width // NZ),
-        [pltpu.VMEM((ROWS, feats), BF), pltpu.VMEM((ROWS, width // NZ), BF)],
-    )
-    *parts, w0, w1, w2, w3 = stage((*parts, *weight_parts), *projected)
-    sum_up = add(*[p[: 3 * n] for p in parts]).astype(BF)
-    sum_down = add(*[p[3 * n : 5 * n] for p in parts]).astype(BF)
-    sum_low = seq_move(sum_up, dz=3)
-    sum_high = seq_move(sum_down, dz=-3)
-    weight_sum = add(
-        w0, seq_move(w1, dy=-1), seq_move(w2, dy=-2), seq_move(w3, dy=-3)
-    ).astype(BF)
-    near = [p[5 * n :] for p in parts]
-    below = add(*[p[:n] for p in near], sum_low[:n]).astype(BF)
-    above = add(*[p[2 * n :] for p in near], sum_low[2 * n :], sum_high[n:]).astype(BF)
-    here = add(*[p[n : 2 * n] for p in near], sum_low[n : 2 * n], sum_high[:n])
-    below, above, here, weight_sum = stage((below, above, here, weight_sum))
-    weight_sum = add(weight_sum, seq_move(weight_sum, dc=1))
-    here = add(here, seq_move(below, dz=-1), seq_move(above, dz=1))
-    here = jnp.where(live_col, here, 0.0).astype(BF)
-    half = width // NZ // NY // NC
-    grad_weight = lax.dynamic_slice_in_dim(weight_sum, c * half, half, 1).astype(BF)
+    below, above, here = sum_near(*sum_far(parts))
+    below, above = stage((below, above), *projected)
+    here = jnp.where(live_col, sum_last(below, above, here), 0.0).astype(BF)
+    grad_weight = add(*[weight_sum[k * SLOTS : (k + 1) * SLOTS] for k in range(NZ)]).astype(BF).T
 
     mine = add(*projected)
     contribution = (weight_col * mine[:, : width // NX]).astype(BF)

time: 116 us -> 109 us (0.940)
  the two profiles are of different devices: /device:TPU:2 before, /device:TPU:24 now
where the time goes in v1:
time: 109 us
  starting transfers between devices  46.4 us (43%)
  waiting for transfers between devices  33.5 us (31%)
  Pallas kernels  13.6 us (12%)
  other arithmetic  6.61 us (6%)
  local copies, waits for them, and re-layouts  5.74 us (5%)
  matrix products  2.09 us (2%)
    ppermute x19, waiting for transfers between devices, seq_move(): return lax.ppermute(a, 'seq', pairs)  21.9 us
    ppermute x19, starting transfers between devices, seq_move(): return lax.ppermute(a, 'seq', pairs)  20.7 us
    all_to_all x2, starting transfers between devices, exchange_z(): lax.all_to_all(a, 'seq', split_axis=0, concat_axis=0, axis_index_groups=L...  15.1 us
    pallas_call x7, Pallas kernels, call(): pl.pallas_call(kernel, out_shape=shapes, in_specs=[SM] + [VM] * len(args)...  13.6 us
    ppermute x6, waiting for transfers between devices, tp_move(): return lax.ppermute(a, 'tp', [(x, (x + dx) % NX) for x in range(NX)])  11.3 us
    ppermute x6, starting transfers between devices, tp_move(): return lax.ppermute(a, 'tp', [(x, (x + dx) % NX) for x in range(NX)])  10.5 us
    unnamed x14, local copies, waits for them, and re-layouts  4.4 us
  transfers between devices with their start and end apart: 27, of which 10 were waited for; matrix products, arithmetic and copies ran while one was open for 6% of the time, Pallas kernels for 8%

profile of v1, /device:TPU:24, one launch (start us, length us, event | category | flops | bytes accessed | tf_op | source)
XLA Modules:
  0.0 108.7 jit_solution(8911964492654229284)
XLA Ops:
  0.6 0.0 copy-start
  0.7 0.7 broadcast_compare_fusion
  1.4 0.8 broadcast_select_fusion.1
  2.2 0.7 pad_maximum_fusion
  2.9 0.7 broadcast_in_dim.54
  3.6 8.5 %all-to-all-start = ((bf16[8,64,256]{2,1,0:T(8,128)(2,1)}), bf16[8,64,256]{2,1,0:T(8,128)(2,1)S(1)}, u32[]{:S(2)}, u32[]{:S(2)}) async-start(bf16[8,64,256]{2,1,0:T(8,128)(2,1)} %broadcast_in_dim.54), calls=%async_computation | async-start | bytes 524288 | tf_op jit(solution)/shard_map/all_to_all | solution.py:42
  12.1 0.7 broadcast_select_fusion.2
  12.8 0.9 fusion.1.refs_0_
  13.7 1.6 %collective-permute-start = (bf16[64,1024]{1,0:T(8,128)(2,1)S(1)}, bf16[64,1024]{1,0:T(8,128)(2,1)S(1)}, u32[]{:S(2)}, u32[]{:S(2)}) collective-permute-start(bf16[64,1024]{1,0:T(8,128)(2,1)S(1)} %fusion.1.refs_0_), channel_id=1, source_target_pairs={{0,1},{1,2},{2,3},{3,0},{4,5},{5,6},{6,7},{7,4},{8,9},{9,10},{10,1... | collective-permute-start | bytes 393224 | tf_op jit(solution)/shard_map/ppermute | solution.py:35
  15.2 2.7 %collective-permute-start.1 = (bf16[64,1024]{1,0:T(8,128)(2,1)S(1)}, bf16[64,1024]{1,0:T(8,128)(2,1)S(1)}, u32[]{:S(2)}, u32[]{:S(2)}) collective-permute-start(bf16[64,1024]{1,0:T(8,128)(2,1)S(1)} %fusion.1.refs_0_), channel_id=1, source_target_pairs={{0,2},{1,3},{2,0},{3,1},{4,6},{5,7},{6,4},{7,5},{8,10},{9,11},{10,... | collective-permute-start | bytes 393224 | tf_op jit(solution)/shard_map/ppermute | solution.py:35
  18.0 1.4 %collective-permute-start.2 = (bf16[64,1024]{1,0:T(8,128)(2,1)S(1)}, bf16[64,1024]{1,0:T(8,128)(2,1)S(1)}, u32[]{:S(2)}, u32[]{:S(2)}) collective-permute-start(bf16[64,1024]{1,0:T(8,128)(2,1)S(1)} %fusion.1.refs_0_), channel_id=1, source_target_pairs={{0,3},{1,0},{2,1},{3,2},{4,7},{5,4},{6,5},{7,6},{8,11},{9,8},{10,9... | collective-permute-start | bytes 393224 | tf_op jit(solution)/shard_map/ppermute | solution.py:35
  19.4 1.0 collective-permute-done.refs_1_
  20.4 3.3 %collective-permute-done.1.refs_2_ = bf16[64,1024]{1,0:T(8,128)(2,1)S(1)} collective-permute-done((bf16[64,1024]{1,0:T(8,128)(2,1)S(1)}, bf16[64,1024]{1,0:T(8,128)(2,1)S(1)}, u32[]{:S(2)}, u32[]{:S(2)}) %collective-permute-start.1) | collective-permute-done | bytes 131104 | tf_op jit(solution)/shard_map/ppermute | solution.py:35
  23.7 0.3 all-to-all-done
  24.0 0.2 collective-permute-start.3
  24.2 1.8 %collective-permute-start.4 = (bf16[512,256]{1,0:T(8,128)(2,1)S(1)}, bf16[512,256]{1,0:T(8,128)(2,1)S(1)}, u32[]{:S(2)}, u32[]{:S(2)}) collective-permute-start(bf16[512,256]{1,0:T(8,128)(2,1)S(1)} %bitcast.12), channel_id=1, source_target_pairs={{0,24},{4,28},{8,0},{12,4},{16,8},{20,12},{24,16},{28,20},{32,56},... | collective-permute-start | bytes 786440 | tf_op jit(solution)/shard_map/ppermute | solution.py:31
  26.0 1.2 %collective-permute-start.5 = (bf16[512,256]{1,0:T(8,128)(2,1)S(1)}, bf16[512,256]{1,0:T(8,128)(2,1)S(1)}, u32[]{:S(2)}, u32[]{:S(2)}) collective-permute-start(bf16[512,256]{1,0:T(8,128)(2,1)S(1)} %bitcast.13), channel_id=1, source_target_pairs={{0,16},{4,20},{8,24},{12,28},{16,0},{20,4},{24,8},{28,12},{32,48},... | collective-permute-start | bytes 786440 | tf_op jit(solution)/shard_map/ppermute | solution.py:31
  27.2 0.1 pad_add_fusion.place
  27.3 2.2 %copy-done.1 = bf16[512,4096]{1,0:T(8,128)(2,1)S(1)} copy-done((bf16[512,4096]{1,0:T(8,128)(2,1)S(1)}, bf16[512,4096]{1,0:T(8,128)(2,1)}, u32[]{:S(2)}) %copy-start.1) | copy-done | bytes 4194328
  29.5 2.0 %shard_map.127 = (bf16[64,512]{1,0:T(8,128)(2,1)S(1)}, bf16[64,1024]{1,0:T(8,128)(2,1)S(1)}, bf16[64,1024]{1,0:T(8,128)(2,1)S(1)}, bf16[64,1024]{1,0:T(8,128)(2,1)S(1)}, bf16[64,1024]{1,0:T(8,128)(2,1)S(1)}) custom-call(s32[4]{0:T(128)S(1)} %pad_add_fusion.place, bf16[64,1024]{1,0:T(8,128)(2,1)S(1)} %fusion.1.refs_0_, ...), custom_call_target="tpu_custom_call" | custom-call | flops 268435456 | bytes 5308416 | tf_op jit(solution)/shard_map/pallas_call | solution.py:242
  31.5 1.7 %collective-permute-done.3.refs_1_ = bf16[512,256]{1,0:T(8,128)(2,1)S(1)} collective-permute-done((bf16[512,256]{1,0:T(8,128)(2,1)S(1)}, bf16[512,256]{1,0:T(8,128)(2,1)S(1)}, u32[]{:S(2)}, u32[]{:S(2)}) %collective-permute-start.3) | collective-permute-done | bytes 262176 | tf_op jit(solution)/shard_map/ppermute | solution.py:31
  33.2 4.3 %collective-permute-done.4.refs_2_ = bf16[512,256]{1,0:T(8,128)(2,1)S(1)} collective-permute-done((bf16[512,256]{1,0:T(8,128)(2,1)S(1)}, bf16[512,256]{1,0:T(8,128)(2,1)S(1)}, u32[]{:S(2)}, u32[]{:S(2)}) %collective-permute-start.4) | collective-permute-done | bytes 262176 | tf_op jit(solution)/shard_map/ppermute | solution.py:31
  37.5 0.5 collective-permute-start.7
  38.0 0.5 collective-permute-start.9
  38.5 2.4 %shard_map.128 = (f32[16,256]{1,0:T(8,128)S(1)}, f32[128,256]{1,0:T(8,128)S(1)}) custom-call(s32[4]{0:T(128)S(1)} %pad_add_fusion.place, bf16[64,512]{1,0:T(8,128)(2,1)S(1)} %copy-done.3, bf16[512,256]{1,0:T(8,128)(2,1)S(1)} %bitcast.15, bf16[512,256]{1,0:T(8,128)(2,1)S(1)} %collective-permute-done.3.refs_1_, ...), custom_call_target="tpu_custom_call" | custom-call | flops 268435456 | bytes 1261568 | tf_op jit(solution)/shard_map/pallas_call | solution.py:242
  41.0 2.4 %shard_map.129 = (bf16[64,512]{1,0:T(8,128)(2,1)S(1)}, f32[8,256]{1,0:T(8,128)S(1)}, bf16[64,1536]{1,0:T(8,128)(2,1)S(1)}, bf16[64,1536]{1,0:T(8,128)(2,1)S(1)},...) custom-call(s32[4]{0:T(128)S(1)} %pad_add_fusion.place, bf16[64,512]{1,0:T(8,128)(2,1)S(1)} %copy-done.3, ...), custom_call_target="tpu_custom_call" | custom-call | flops 268435456 | bytes 2646016 | tf_op jit(solution)/shard_map/pallas_call | solution.py:242
  43.4 2.2 %shard_map.130 = (bf16[2048,256]{1,0:T(8,128)(2,1)S(1)}, f32[128,256]{1,0:T(8,128)S(1)}) custom-call(s32[4]{0:T(128)S(1)} %pad_add_fusion.place, bf16[64,512]{1,0:T(8,128)(2,1)S(1)} %copy-done.3, bf16[64,512]{1,0:T(8,128)(2,1)S(1)} %get-tuple-element.76.g_ref, bf16[64,512]{1,0:T(8,128)(2,1)S(1)} %get-tuple-element.92.att_ref, ...), custom_call_target="tpu_custom_call" | custom-call | flops 671088640 | bytes 2433024 | tf_op jit(solution)/shard_map/pallas_call | solution.py:242
  45.6 0.1 collective-permute-start.10
  45.7 1.5 %collective-permute-start.21 = (bf16[64,1536]{1,0:T(8,128)(2,1)S(1)}, bf16[64,1536]{1,0:T(8,128)(2,1)S(1)}, u32[]{:S(2)}, u32[]{:S(2)}) collective-permute-start(bf16[64,1536]{1,0:T(8,128)(2,1)S(1)} %get-tuple-element.101), channel_id=1, source_target_pairs={{0,8},{4,12},{8,16},{12,20},{16,24},{20,28},{24,0},{28,4},{32,40},... | collective-permute-start | bytes 589832 | tf_op jit(solution)/shard_map/ppermute | solution.py:31
  47.2 0.6 collective-permute-start.22
  47.8 2.0 %collective-permute-start.23 = (bf16[64,1536]{1,0:T(8,128)(2,1)S(1)}, bf16[64,1536]{1,0:T(8,128)(2,1)S(1)}, u32[]{:S(2)}, u32[]{:S(2)}) collective-permute-start(bf16[64,1536]{1,0:T(8,128)(2,1)S(1)} %get-tuple-element.103), channel_id=1, source_target_pairs={{0,16},{4,20},{8,24},{12,28},{16,0},{20,4},{24,8},{28,12},{32,48},... | collective-permute-start | bytes 589832 | tf_op jit(solution)/shard_map/ppermute | solution.py:31
  49.8 2.3 %shard_map.131 = (bf16[512,256]{1,0:T(8,128)(2,1)S(1)}, bf16[512,256]{1,0:T(8,128)(2,1)S(1)}, bf16[512,256]{1,0:T(8,128)(2,1)S(1)}, bf16[512,256]{1,0:T(8,128)(2,1)S(1)}, bf16[64,512]{1,0:T(8,128)(2,1)S(1)}) custom-call(s32[4]{0:T(128)S(1)} %pad_add_fusion.place, bf16[64,512]{1,0:T(8,128)(2,1)S(1)} %copy-done.3, ...), custom_call_target="tpu_custom_call" | custom-call | flops 671088640 | bytes 2498560 | tf_op jit(solution)/shard_map/pallas_call | solution.py:242
  52.1 0.3 add_convert_fusion.1
  52.4 1.6 %collective-permute-start.11 = (bf16[512,256]{1,0:T(8,128)(2,1)S(1)}, bf16[512,256]{1,0:T(8,128)(2,1)S(1)}, u32[]{:S(2)}, u32[]{:S(2)}) collective-permute-start(bf16[512,256]{1,0:T(8,128)(2,1)S(1)} %get-tuple-element.85), channel_id=1, source_target_pairs={{0,24},{4,28},{8,0},{12,4},{16,8},{20,12},{24,16},{28,20},{32,56},... | collective-permute-start | bytes 786440 | tf_op jit(solution)/shard_map/ppermute | solution.py:31
  54.0 1.7 %collective-permute-start.12 = (bf16[512,256]{1,0:T(8,128)(2,1)S(1)}, bf16[512,256]{1,0:T(8,128)(2,1)S(1)}, u32[]{:S(2)}, u32[]{:S(2)}) collective-permute-start(bf16[512,256]{1,0:T(8,128)(2,1)S(1)} %get-tuple-element.86), channel_id=1, source_target_pairs={{0,8},{4,12},{8,16},{12,20},{16,24},{20,28},{24,0},{28,4},{32,40},... | collective-permute-start | bytes 786440 | tf_op jit(solution)/shard_map/ppermute | solution.py:31
  55.7 0.4 collective-permute-start.13
  56.2 3.9 %collective-permute-done.22.refs_2_ = bf16[64,1536]{1,0:T(8,128)(2,1)S(1)} collective-permute-done((bf16[64,1536]{1,0:T(8,128)(2,1)S(1)}, bf16[64,1536]{1,0:T(8,128)(2,1)S(1)}, u32[]{:S(2)}, u32[]{:S(2)}) %collective-permute-start.22) | collective-permute-done | bytes 196640 | tf_op jit(solution)/shard_map/ppermute | solution.py:31
  60.1 1.0 shard_map.133
  61.1 0.3 collective-permute-start.24
  61.4 0.7 broadcast_select_fusion
  62.1 8.7 %collective-permute-done.11 = bf16[512,256]{1,0:T(8,128)(2,1)S(1)} collective-permute-done((bf16[512,256]{1,0:T(8,128)(2,1)S(1)}, bf16[512,256]{1,0:T(8,128)(2,1)S(1)}, u32[]{:S(2)}, u32[]{:S(2)}) %collective-permute-start.11) | collective-permute-done | bytes 262176 | tf_op jit(solution)/shard_map/ppermute | solution.py:31
  70.9 0.1 add_convert_fusion.5
  70.9 3.2 %collective-permute-start.17 = (bf16[192,256]{1,0:T(8,128)(2,1)S(1)}, bf16[192,256]{1,0:T(8,128)(2,1)S(1)}, u32[]{:S(2)}, u32[]{:S(2)}) collective-permute-start(bf16[192,256]{1,0:T(8,128)(2,1)S(1)} %add_convert_fusion.5), channel_id=1, source_target_pairs={{0,96},{4,100},{8,104},{12,108},{16,112},{20,116},{24,120},{28,124... | collective-permute-start | bytes 294920 | tf_op jit(solution)/shard_map/ppermute | solution.py:31
  74.2 0.0 copy-start.4
  74.2 0.0 copy-start.5
  74.2 2.0 %collective-permute-start.18 = (bf16[128,256]{1,0:T(8,128)(2,1)S(1)}, bf16[128,256]{1,0:T(8,128)(2,1)S(1)}, u32[]{:S(2)}, u32[]{:S(2)}) collective-permute-start(bf16[128,256]{1,0:T(8,128)(2,1)S(1)} %add_convert_fusion.7), channel_id=1, source_target_pairs={{0,160},{4,164},{8,168},{12,172},{16,176},{20,180},{24,184},{28,18... | collective-permute-start | bytes 196616 | tf_op jit(solution)/shard_map/ppermute | solution.py:31
  76.2 0.9 add_convert_fusion
  77.1 6.7 %all-to-all-start.1 = ((bf16[8,64,512]{2,1,0:T(8,128)(2,1)}), bf16[8,64,512]{2,1,0:T(8,128)(2,1)S(1)}, u32[]{:S(2)}, u32[]{:S(2)}) async-start(bf16[8,64,512]{2,1,0:T(8,128)(2,1)} %bitcast.5), calls=%async_computation.1 | async-start | bytes 1048576 | tf_op jit(solution)/shard_map/all_to_all | solution.py:42
  83.8 2.2 %copy-done.2 = bf16[512,4096]{1,0:T(8,128)(2,1)S(1)} copy-done((bf16[512,4096]{1,0:T(8,128)(2,1)S(1)}, bf16[512,4096]{1,0:T(8,128)(2,1)}, u32[]{:S(2)}) %copy-start.2) | copy-done | bytes 4194328
  86.0 1.4 %shard_map.132 = (bf16[64,1152]{1,0:T(8,128)(2,1)S(1)}, bf16[64,1152]{1,0:T(8,128)(2,1)S(1)}, bf16[64,1152]{1,0:T(8,128)(2,1)S(1)}, bf16[64,1152]{1,0:T(8,128)(2,1)S(1)}) custom-call(s32[4]{0:T(128)S(1)} %pad_add_fusion.place, bf16[64,512]{1,0:T(8,128)(2,1)S(1)} %get-tuple-element.92.att_ref, bf16[64,512]{1,0:T(8,128)(2,1)S(1)} %get-tuple-element.76.g_ref, ...), custom_call_target="tpu_custom_call" | custom-call | flops 268435456 | bytes 4915200 | tf_op jit(solution)/shard_map/pallas_call | solution.py:242
  87.3 3.3 %collective-permute-start.14 = (bf16[64,1152]{1,0:T(8,128)(2,1)S(1)}, bf16[64,1152]{1,0:T(8,128)(2,1)S(1)}, u32[]{:S(2)}, u32[]{:S(2)}) collective-permute-start(bf16[64,1152]{1,0:T(8,128)(2,1)S(1)} %get-tuple-element.94), channel_id=1, source_target_pairs={{0,3},{1,0},{2,1},{3,2},{4,7},{5,4},{6,5},{7,6},{8,11},{9,8},{10,9... | collective-permute-start | bytes 442376 | tf_op jit(solution)/shard_map/ppermute | solution.py:35
  90.6 1.6 %collective-permute-start.16 = (bf16[64,1152]{1,0:T(8,128)(2,1)S(1)}, bf16[64,1152]{1,0:T(8,128)(2,1)S(1)}, u32[]{:S(2)}, u32[]{:S(2)}) collective-permute-start(bf16[64,1152]{1,0:T(8,128)(2,1)S(1)} %get-tuple-element.96), channel_id=1, source_target_pairs={{0,2},{1,3},{2,0},{3,1},{4,6},{5,7},{6,4},{7,5},{8,10},{9,11},{10,... | collective-permute-start | bytes 442376 | tf_op jit(solution)/shard_map/ppermute | solution.py:35
  92.2 0.1 add_convert_fusion.8
  92.2 2.7 %collective-permute-done.14 = bf16[64,1152]{1,0:T(8,128)(2,1)S(1)} collective-permute-done((bf16[64,1152]{1,0:T(8,128)(2,1)S(1)}, bf16[64,1152]{1,0:T(8,128)(2,1)S(1)}, u32[]{:S(2)}, u32[]{:S(2)}) %collective-permute-start.14) | collective-permute-done | bytes 147488 | tf_op jit(solution)/shard_map/ppermute | solution.py:35
  94.9 4.4 %collective-permute-done.15 = bf16[64,1152]{1,0:T(8,128)(2,1)S(1)} collective-permute-done((bf16[64,1152]{1,0:T(8,128)(2,1)S(1)}, bf16[64,1152]{1,0:T(8,128)(2,1)S(1)}, u32[]{:S(2)}, u32[]{:S(2)}) %collective-permute-start.15) | collective-permute-done | bytes 147488 | tf_op jit(solution)/shard_map/ppermute | solution.py:35
  99.3 3.0 %collective-permute-start.19 = (bf16[64,256]{1,0:T(8,128)(2,1)S(1)}, bf16[64,256]{1,0:T(8,128)(2,1)S(1)}, u32[]{:S(2)}, u32[]{:S(2)}) collective-permute-start(bf16[64,256]{1,0:T(8,128)(2,1)S(1)} %get-tuple-element.98), channel_id=1, source_target_pairs={{0,224},{4,228},{8,232},{12,236},{16,240},{20,244},{24,248},{28,25... | collective-permute-start | bytes 98312 | tf_op jit(solution)/shard_map/ppermute | solution.py:31
  102.2 0.1 convert_add_fusion
  102.3 0.2 fusion.6
  102.5 1.2 %fusion = bf16[256,1024]{1,0:T(8,128)(2,1)} fusion(bf16[256,1024]{1,0:T(8,128)(2,1)S(1)} %copy-done.4, f32[64,1152]{1,0:T(8,128)S(1)} %convert_add_fusion, f32[64]{0:T(128)S(1)} %broadcast_select_fusion.2, s32[64]{0:T(128)S(1)} %copy-done.5), kind=kOutput, calls=%fused_computation.1 | convolution fusion | flops 34488320 | bytes 1311744 | tf_op jit(solution)/shard_map/dot_general | solution.py:70
  103.7 0.5 divide_select_fusion
  104.2 3.1 %collective-permute-done.20 = bf16[64,256]{1,0:T(8,128)(2,1)S(1)} collective-permute-done((bf16[64,256]{1,0:T(8,128)(2,1)S(1)}, bf16[64,256]{1,0:T(8,128)(2,1)S(1)}, u32[]{:S(2)}, u32[]{:S(2)}) %collective-permute-start.20) | collective-permute-done | bytes 32800 | tf_op jit(solution)/shard_map/ppermute | solution.py:31
  107.3 0.1 select_convert_fusion
  107.4 0.6 fusion.9
  108.0 0.7 fusion.5
  (31 shorter events, 0.1 us)
Async XLA Ops:
  0.6 12.1 %copy-start = (bf16[256,1024]{1,0:T(8,128)(2,1)S(1)}, bf16[256,1024]{1,0:T(8,128)(2,1)}, u32[]{:S(2)}) copy-start(bf16[256,1024]{1,0:T(8,128)(2,1)} %param.9) | copy-start | bytes 1572868
  0.6 37.9 %copy-start.3 = (bf16[64,512]{1,0:T(8,128)(2,1)S(1)}, bf16[64,512]{1,0:T(8,128)(2,1)}, u32[]{:S(2)}) copy-start(bf16[64,512]{1,0:T(8,128)(2,1)} %q_ref.7) | copy-start | bytes 196612
  3.6 20.3 %all-to-all-start = ((bf16[8,64,256]{2,1,0:T(8,128)(2,1)}), bf16[8,64,256]{2,1,0:T(8,128)(2,1)S(1)}, u32[]{:S(2)}, u32[]{:S(2)}) async-start(bf16[8,64,256]{2,1,0:T(8,128)(2,1)} %broadcast_in_dim.54), calls=%async_computation | async-start | bytes 524288 | tf_op jit(solution)/shard_map/all_to_all | solution.py:42
  13.7 6.7 %collective-permute-start = (bf16[64,1024]{1,0:T(8,128)(2,1)S(1)}, bf16[64,1024]{1,0:T(8,128)(2,1)S(1)}, u32[]{:S(2)}, u32[]{:S(2)}) collective-permute-start(bf16[64,1024]{1,0:T(8,128)(2,1)S(1)} %fusion.1.refs_0_), channel_id=1, source_target_pairs={{0,1},{1,2},{2,3},{3,0},{4,5},{5,6},{6,7},{7,4},{8,9},{9,10},{10,1... | collective-permute-start | bytes 393224 | tf_op jit(solution)/shard_map/ppermute | solution.py:35
  15.2 8.5 %collective-permute-start.1 = (bf16[64,1024]{1,0:T(8,128)(2,1)S(1)}, bf16[64,1024]{1,0:T(8,128)(2,1)S(1)}, u32[]{:S(2)}, u32[]{:S(2)}) collective-permute-start(bf16[64,1024]{1,0:T(8,128)(2,1)S(1)} %fusion.1.refs_0_), channel_id=1, source_target_pairs={{0,2},{1,3},{2,0},{3,1},{4,6},{5,7},{6,4},{7,5},{8,10},{9,11},{10,... | collective-permute-start | bytes 393224 | tf_op jit(solution)/shard_map/ppermute | solution.py:35
  18.0 5.7 %collective-permute-start.2 = (bf16[64,1024]{1,0:T(8,128)(2,1)S(1)}, bf16[64,1024]{1,0:T(8,128)(2,1)S(1)}, u32[]{:S(2)}, u32[]{:S(2)}) collective-permute-start(bf16[64,1024]{1,0:T(8,128)(2,1)S(1)} %fusion.1.refs_0_), channel_id=1, source_target_pairs={{0,3},{1,0},{2,1},{3,2},{4,7},{5,4},{6,5},{7,6},{8,11},{9,8},{10,9... | collective-permute-start | bytes 393224 | tf_op jit(solution)/shard_map/ppermute | solution.py:35
  24.0 9.2 %collective-permute-start.3 = (bf16[512,256]{1,0:T(8,128)(2,1)S(1)}, bf16[512,256]{1,0:T(8,128)(2,1)S(1)}, u32[]{:S(2)}, u32[]{:S(2)}) collective-permute-start(bf16[512,256]{1,0:T(8,128)(2,1)S(1)} %bitcast.11), channel_id=1, source_target_pairs={{0,8},{4,12},{8,16},{12,20},{16,24},{20,28},{24,0},{28,4},{32,40},... | collective-permute-start | bytes 786440 | tf_op jit(solution)/shard_map/ppermute | solution.py:31
  24.2 13.3 %collective-permute-start.4 = (bf16[512,256]{1,0:T(8,128)(2,1)S(1)}, bf16[512,256]{1,0:T(8,128)(2,1)S(1)}, u32[]{:S(2)}, u32[]{:S(2)}) collective-permute-start(bf16[512,256]{1,0:T(8,128)(2,1)S(1)} %bitcast.12), channel_id=1, source_target_pairs={{0,24},{4,28},{8,0},{12,4},{16,8},{20,12},{24,16},{28,20},{32,56},... | collective-permute-start | bytes 786440 | tf_op jit(solution)/shard_map/ppermute | solution.py:31
  26.0 11.5 %collective-permute-start.5 = (bf16[512,256]{1,0:T(8,128)(2,1)S(1)}, bf16[512,256]{1,0:T(8,128)(2,1)S(1)}, u32[]{:S(2)}, u32[]{:S(2)}) collective-permute-start(bf16[512,256]{1,0:T(8,128)(2,1)S(1)} %bitcast.13), channel_id=1, source_target_pairs={{0,16},{4,20},{8,24},{12,28},{16,0},{20,4},{24,8},{28,12},{32,48},... | collective-permute-start | bytes 786440 | tf_op jit(solution)/shard_map/ppermute | solution.py:31
  27.3 2.2 %copy-start.1 = (bf16[512,4096]{1,0:T(8,128)(2,1)S(1)}, bf16[512,4096]{1,0:T(8,128)(2,1)}, u32[]{:S(2)}) copy-start(bf16[512,4096]{1,0:T(8,128)(2,1)} %w_ref.1) | copy-start | bytes 12582916
  37.5 3.4 %collective-permute-start.6 = (bf16[512,256]{1,0:T(8,128)(2,1)S(1)}, bf16[512,256]{1,0:T(8,128)(2,1)S(1)}, u32[]{:S(2)}, u32[]{:S(2)}) collective-permute-start(bf16[512,256]{1,0:T(8,128)(2,1)S(1)} %bitcast.14), channel_id=1, source_target_pairs={{0,4},{4,0},{8,12},{12,8},{16,20},{20,16},{24,28},{28,24},{32,36},... | collective-permute-start | bytes 786440 | tf_op jit(solution)/shard_map/ppermute | solution.py:31
  37.5 3.4 %collective-permute-start.7 = (bf16[512,256]{1,0:T(8,128)(2,1)S(1)}, bf16[512,256]{1,0:T(8,128)(2,1)S(1)}, u32[]{:S(2)}, u32[]{:S(2)}) collective-permute-start(bf16[512,256]{1,0:T(8,128)(2,1)S(1)} %collective-permute-done.3.refs_1_), channel_id=1, source_target_pairs={{0,4},{4,0},{8,12},{12,8},{16,20},{20,16},{24,28},{28,24},{32,36},... | collective-permute-start | bytes 786440 | tf_op jit(solution)/shard_map/ppermute | solution.py:31
  38.0 2.9 %collective-permute-start.8 = (bf16[512,256]{1,0:T(8,128)(2,1)S(1)}, bf16[512,256]{1,0:T(8,128)(2,1)S(1)}, u32[]{:S(2)}, u32[]{:S(2)}) collective-permute-start(bf16[512,256]{1,0:T(8,128)(2,1)S(1)} %collective-permute-done.4.refs_2_), channel_id=1, source_target_pairs={{0,4},{4,0},{8,12},{12,8},{16,20},{20,16},{24,28},{28,24},{32,36},... | collective-permute-start | bytes 786440 | tf_op jit(solution)/shard_map/ppermute | solution.py:31
  38.0 2.9 %collective-permute-start.9 = (bf16[512,256]{1,0:T(8,128)(2,1)S(1)}, bf16[512,256]{1,0:T(8,128)(2,1)S(1)}, u32[]{:S(2)}, u32[]{:S(2)}) collective-permute-start(bf16[512,256]{1,0:T(8,128)(2,1)S(1)} %collective-permute-done.5.refs_3_), channel_id=1, source_target_pairs={{0,4},{4,0},{8,12},{12,8},{16,20},{20,16},{24,28},{28,24},{32,36},... | collective-permute-start | bytes 786440 | tf_op jit(solution)/shard_map/ppermute | solution.py:31
  45.6 6.5 %collective-permute-start.10 = (bf16[2048,256]{1,0:T(8,128)(2,1)S(1)}, bf16[2048,256]{1,0:T(8,128)(2,1)S(1)}, u32[]{:S(2)}, u32[]{:S(2)}) collective-permute-start(bf16[2048,256]{1,0:T(8,128)(2,1)S(1)} %get-tuple-element.80), channel_id=1, source_target_pairs={{0,4},{4,0},{8,12},{12,8},{16,20},{20,16},{24,28},{28,24},{32,36},... | collective-permute-start | bytes 3145736 | tf_op jit(solution)/shard_map/ppermute | solution.py:31
  45.7 10.0 %collective-permute-start.21 = (bf16[64,1536]{1,0:T(8,128)(2,1)S(1)}, bf16[64,1536]{1,0:T(8,128)(2,1)S(1)}, u32[]{:S(2)}, u32[]{:S(2)}) collective-permute-start(bf16[64,1536]{1,0:T(8,128)(2,1)S(1)} %get-tuple-element.101), channel_id=1, source_target_pairs={{0,8},{4,12},{8,16},{12,20},{16,24},{20,28},{24,0},{28,4},{32,40},... | collective-permute-start | bytes 589832 | tf_op jit(solution)/shard_map/ppermute | solution.py:31
  47.2 12.9 %collective-permute-start.22 = (bf16[64,1536]{1,0:T(8,128)(2,1)S(1)}, bf16[64,1536]{1,0:T(8,128)(2,1)S(1)}, u32[]{:S(2)}, u32[]{:S(2)}) collective-permute-start(bf16[64,1536]{1,0:T(8,128)(2,1)S(1)} %get-tuple-element.102), channel_id=1, source_target_pairs={{0,24},{4,28},{8,0},{12,4},{16,8},{20,12},{24,16},{28,20},{32,56},... | collective-permute-start | bytes 589832 | tf_op jit(solution)/shard_map/ppermute | solution.py:31
  47.8 12.3 %collective-permute-start.23 = (bf16[64,1536]{1,0:T(8,128)(2,1)S(1)}, bf16[64,1536]{1,0:T(8,128)(2,1)S(1)}, u32[]{:S(2)}, u32[]{:S(2)}) collective-permute-start(bf16[64,1536]{1,0:T(8,128)(2,1)S(1)} %get-tuple-element.103), channel_id=1, source_target_pairs={{0,16},{4,20},{8,24},{12,28},{16,0},{20,4},{24,8},{28,12},{32,48},... | collective-permute-start | bytes 589832 | tf_op jit(solution)/shard_map/ppermute | solution.py:31
  52.4 18.4 %collective-permute-start.11 = (bf16[512,256]{1,0:T(8,128)(2,1)S(1)}, bf16[512,256]{1,0:T(8,128)(2,1)S(1)}, u32[]{:S(2)}, u32[]{:S(2)}) collective-permute-start(bf16[512,256]{1,0:T(8,128)(2,1)S(1)} %get-tuple-element.85), channel_id=1, source_target_pairs={{0,24},{4,28},{8,0},{12,4},{16,8},{20,12},{24,16},{28,20},{32,56},... | collective-permute-start | bytes 786440 | tf_op jit(solution)/shard_map/ppermute | solution.py:31
  54.0 16.9 %collective-permute-start.12 = (bf16[512,256]{1,0:T(8,128)(2,1)S(1)}, bf16[512,256]{1,0:T(8,128)(2,1)S(1)}, u32[]{:S(2)}, u32[]{:S(2)}) collective-permute-start(bf16[512,256]{1,0:T(8,128)(2,1)S(1)} %get-tuple-element.86), channel_id=1, source_target_pairs={{0,8},{4,12},{8,16},{12,20},{16,24},{20,28},{24,0},{28,4},{32,40},... | collective-permute-start | bytes 786440 | tf_op jit(solution)/shard_map/ppermute | solution.py:31
  55.7 15.1 %collective-permute-start.13 = (bf16[512,256]{1,0:T(8,128)(2,1)S(1)}, bf16[512,256]{1,0:T(8,128)(2,1)S(1)}, u32[]{:S(2)}, u32[]{:S(2)}) collective-permute-start(bf16[512,256]{1,0:T(8,128)(2,1)S(1)} %get-tuple-element.87), channel_id=1, source_target_pairs={{0,16},{4,20},{8,24},{12,28},{16,0},{20,4},{24,8},{28,12},{32,48},... | collective-permute-start | bytes 786440 | tf_op jit(solution)/shard_map/ppermute | solution.py:31
  61.1 15.1 %collective-permute-start.24 = (bf16[512,512]{1,0:T(8,128)(2,1)S(1)}, bf16[512,512]{1,0:T(8,128)(2,1)S(1)}, u32[]{:S(2)}, u32[]{:S(2)}) collective-permute-start(bf16[512,512]{1,0:T(8,128)(2,1)S(1)} %get-tuple-element.105), channel_id=1, source_target_pairs={{0,4},{4,0},{8,12},{12,8},{16,20},{20,16},{24,28},{28,24},{32,36},... | collective-permute-start | bytes 1572872 | tf_op jit(solution)/shard_map/ppermute | solution.py:31
  70.9 21.2 %collective-permute-start.17 = (bf16[192,256]{1,0:T(8,128)(2,1)S(1)}, bf16[192,256]{1,0:T(8,128)(2,1)S(1)}, u32[]{:S(2)}, u32[]{:S(2)}) collective-permute-start(bf16[192,256]{1,0:T(8,128)(2,1)S(1)} %add_convert_fusion.5), channel_id=1, source_target_pairs={{0,96},{4,100},{8,104},{12,108},{16,112},{20,116},{24,120},{28,124... | collective-permute-start | bytes 294920 | tf_op jit(solution)/shard_map/ppermute | solution.py:31
  74.2 28.3 %copy-start.4 = (bf16[256,1024]{1,0:T(8,128)(2,1)S(1)}, bf16[256,1024]{1,0:T(8,128)(2,1)}, u32[]{:S(2)}) copy-start(bf16[256,1024]{1,0:T(8,128)(2,1)} %param.8) | copy-start | bytes 1572868
  74.2 28.3 %copy-start.5 = (s32[64]{0:T(128)S(1)}, s32[64]{0:T(128)}, u32[]{:S(2)}) copy-start(s32[64]{0:T(128)} %param.10) | copy-start | bytes 772
  74.2 18.0 %collective-permute-start.18 = (bf16[128,256]{1,0:T(8,128)(2,1)S(1)}, bf16[128,256]{1,0:T(8,128)(2,1)S(1)}, u32[]{:S(2)}, u32[]{:S(2)}) collective-permute-start(bf16[128,256]{1,0:T(8,128)(2,1)S(1)} %add_convert_fusion.7), channel_id=1, source_target_pairs={{0,160},{4,164},{8,168},{12,172},{16,176},{20,180},{24,184},{28,18... | collective-permute-start | bytes 196616 | tf_op jit(solution)/shard_map/ppermute | solution.py:31
  77.1 26.6 %copy-start.6 = (f32[64]{0:T(128)S(1)}, f32[64]{0:T(128)}, u32[]{:S(2)}) copy-start(f32[64]{0:T(128)} %param.14) | copy-start | bytes 772
  77.1 30.9 %all-to-all-start.1 = ((bf16[8,64,512]{2,1,0:T(8,128)(2,1)}), bf16[8,64,512]{2,1,0:T(8,128)(2,1)S(1)}, u32[]{:S(2)}, u32[]{:S(2)}) async-start(bf16[8,64,512]{2,1,0:T(8,128)(2,1)} %bitcast.5), calls=%async_computation.1 | async-start | bytes 1048576 | tf_op jit(solution)/shard_map/all_to_all | solution.py:42
  83.8 2.2 %copy-start.2 = (bf16[512,4096]{1,0:T(8,128)(2,1)S(1)}, bf16[512,4096]{1,0:T(8,128)(2,1)}, u32[]{:S(2)}) copy-start(bf16[512,4096]{1,0:T(8,128)(2,1)} %w_ref.1) | copy-start | bytes 12582916
  87.3 7.5 %collective-permute-start.14 = (bf16[64,1152]{1,0:T(8,128)(2,1)S(1)}, bf16[64,1152]{1,0:T(8,128)(2,1)S(1)}, u32[]{:S(2)}, u32[]{:S(2)}) collective-permute-start(bf16[64,1152]{1,0:T(8,128)(2,1)S(1)} %get-tuple-element.94), channel_id=1, source_target_pairs={{0,3},{1,0},{2,1},{3,2},{4,7},{5,4},{6,5},{7,6},{8,11},{9,8},{10,9... | collective-permute-start | bytes 442376 | tf_op jit(solution)/shard_map/ppermute | solution.py:35
  90.6 8.6 %collective-permute-start.15 = (bf16[64,1152]{1,0:T(8,128)(2,1)S(1)}, bf16[64,1152]{1,0:T(8,128)(2,1)S(1)}, u32[]{:S(2)}, u32[]{:S(2)}) collective-permute-start(bf16[64,1152]{1,0:T(8,128)(2,1)S(1)} %get-tuple-element.95), channel_id=1, source_target_pairs={{0,1},{1,2},{2,3},{3,0},{4,5},{5,6},{6,7},{7,4},{8,9},{9,10},{10,1... | collective-permute-start | bytes 442376 | tf_op jit(solution)/shard_map/ppermute | solution.py:35
  90.6 8.6 %collective-permute-start.16 = (bf16[64,1152]{1,0:T(8,128)(2,1)S(1)}, bf16[64,1152]{1,0:T(8,128)(2,1)S(1)}, u32[]{:S(2)}, u32[]{:S(2)}) collective-permute-start(bf16[64,1152]{1,0:T(8,128)(2,1)S(1)} %get-tuple-element.96), channel_id=1, source_target_pairs={{0,2},{1,3},{2,0},{3,1},{4,6},{5,7},{6,4},{7,5},{8,10},{9,11},{10,... | collective-permute-start | bytes 442376 | tf_op jit(solution)/shard_map/ppermute | solution.py:35
  99.3 5.0 %collective-permute-start.19 = (bf16[64,256]{1,0:T(8,128)(2,1)S(1)}, bf16[64,256]{1,0:T(8,128)(2,1)S(1)}, u32[]{:S(2)}, u32[]{:S(2)}) collective-permute-start(bf16[64,256]{1,0:T(8,128)(2,1)S(1)} %get-tuple-element.98), channel_id=1, source_target_pairs={{0,224},{4,228},{8,232},{12,236},{16,240},{20,244},{24,248},{28,25... | collective-permute-start | bytes 98312 | tf_op jit(solution)/shard_map/ppermute | solution.py:31
  102.2 5.1 %collective-permute-start.20 = (bf16[64,256]{1,0:T(8,128)(2,1)S(1)}, bf16[64,256]{1,0:T(8,128)(2,1)S(1)}, u32[]{:S(2)}, u32[]{:S(2)}) collective-permute-start(bf16[64,256]{1,0:T(8,128)(2,1)S(1)} %get-tuple-element.99), channel_id=1, source_target_pairs={{0,32},{4,36},{8,40},{12,44},{16,48},{20,52},{24,56},{28,60},{32,6... | collective-permute-start | bytes 98312 | tf_op jit(solution)/shard_map/ppermute | solution.py:31

commit v2 on v1

--- a/solution.py
+++ b/solution.py
@@ -113,14 +113,19 @@
         stats, acc = refs[0], refs[1][...]
         top, total = stats[0:1], stats[8:9]
         refs = refs[2:]
-    for (dy, dc), kv_ref in zip(blocks, kv_refs):
-        t = masked_scores(place, dy, dc, kv_ref, q_rows, diff)
-        new_top = jnp.maximum(top, jnp.max(t, axis=0, keepdims=True))
-        old = jnp.exp2(top - new_top)
-        e = jnp.exp2(t - new_top)
-        total = total * old + jnp.sum(e, axis=0, keepdims=True)
-        acc = acc * old + dot(kv_ref[:, HEAD:], e.astype(BF), 0, 0)
-        top = new_top
+    ts = [
+        masked_scores(place, dy, dc, kv_ref, q_rows, diff)
+        for (dy, dc), kv_ref in zip(blocks, kv_refs)
+    ]
+    old_top = top
+    for t in ts:
+        top = jnp.maximum(top, jnp.max(t, axis=0, keepdims=True))
+    old = jnp.exp2(old_top - top)
+    total, acc = total * old, acc * old
+    for t, kv_ref in zip(ts, kv_refs):
+        e = jnp.exp2(t - top)
+        total = total + jnp.sum(e, axis=0, keepdims=True)
+        acc = acc + dot(kv_ref[:, HEAD:], e.astype(BF), 0, 0)
     if last:
         pieces, refs = refs[:NY], refs[NY:]
     if not last:
@@ -283,7 +288,7 @@
 
     kv_z = exchange_z(jnp.broadcast_to(kv[None], (NZ, *kv.shape)).reshape(ROWS, 2 * HEAD))
     chunks = {m: tp_move(proj_grad, m) for m in (1, 3, 2)}
-    kv_z, chunks[1], chunks[2], chunks[3] = stage((kv_z, chunks[1], chunks[2], chunks[3]))
+    kv_z, chunks[1] = stage((kv_z, chunks[1]))
     attn_grad, *pieces = call(
         attn_grad_kernel,
         place,
@@ -328,7 +333,6 @@
         10 * NY * ROWS * lanes * HEAD,
     )
     sums = [add(a, theirs[i * ROWS : (i + 1) * ROWS]).astype(BF) for i, a in enumerate(own)]
-    sums = stage(sums)
     weight_mine, weight_other = call(
         weight_kernel,
         place,
@@ -342,16 +346,16 @@
     weight_sum = add(weight_mine, weight_theirs).astype(BF)
     weight_sum = exchange_z(weight_sum)
     parts = stage(parts)
+    below, above, here = sum_near(*sum_far(parts))
+    below, above = stage((below, above))
     projected = call(
         project_kernel,
         place,
-        [stage((attended,), *parts)[0], attn_grad, out_weight],
+        [stage((attended,), below, above)[0], attn_grad, out_weight],
         [shape((SLOTS, width // NX + HEAD), BF)] * NX,
-        2 * SLOTS * width * feats,
+        40 * SLOTS * width * feats,
     )
     projected = [projected[0]] + [tp_move(projected[m], -m) for m in (1, 3, 2)]
-    below, above, here = sum_near(*sum_far(parts))
-    below, above = stage((below, above), *projected)
     here = jnp.where(live_col, sum_last(below, above, here), 0.0).astype(BF)
     grad_weight = add(*[weight_sum[k * SLOTS : (k + 1) * SLOTS] for k in range(NZ)]).astype(BF).T
 
@@ -360,7 +364,6 @@
     router_sum = mine[:, width // NX] + mine[:, width // NX + 1] + mine[:, width // NX + 2]
     grad_router = jnp.where(live, router_sum / router, 0.0)
     updated = (residual.astype(F32) + dot(hot, contribution, 0, 0)).astype(BF)
-    grad_query = jnp.where(live_col, grad_query, jnp.zeros((), BF))
     return (updated, grad_query, here[:, :HEAD], here[:, HEAD:], grad_router, grad_weight)
 
 

time: 109 us -> 104 us (0.954)
  starting transfers between devices: 46.4 us -> 43.1 us
  waiting for transfers between devices: 33.5 us -> 31.9 us
    ppermute x19, waiting for transfers between devices: 21.9 us -> 15.8 us  [seq_move(): return lax.ppermute(a, 'seq', pairs)]
    all_to_all x2, waiting for transfers between devices: 0.26 us -> 4.04 us  [exchange_z(): lax.all_to_all(a, 'seq', split_axis=0, concat_axis=0, axis_index_groups=L...]
    all_to_all x2, starting transfers between devices: 15.1 us -> 12 us  [exchange_z(): lax.all_to_all(a, 'seq', split_axis=0, concat_axis=0, axis_index_groups=L...]
  transfers between devices with their start and end apart: 27 -> 27, of which waited for: 10 -> 9; matrix products, arithmetic and copies ran while one was open for 6% -> 6% of each run, Pallas kernels for 8% -> 9%
where the time goes in v2:
time: 104 us; the launch traced here: 103 us
  starting transfers between devices  43.1 us (41%)
  waiting for transfers between devices  31.9 us (31%)
  Pallas kernels  13.5 us (13%)
  other arithmetic  5.9 us (6%)
  local copies, waits for them, and re-layouts  5.74 us (6%)
  matrix products  2.09 us (2%)
    ppermute x19, starting transfers between devices, seq_move(): return lax.ppermute(a, 'seq', pairs)  21.2 us
    ppermute x19, waiting for transfers between devices, seq_move(): return lax.ppermute(a, 'seq', pairs)  15.8 us
    pallas_call x7, Pallas kernels, call(): pl.pallas_call(kernel, out_shape=shapes, in_specs=[SM] + [VM] * len(args)...  13.5 us
    ppermute x6, waiting for transfers between devices, tp_move(): return lax.ppermute(a, 'tp', [(x, (x + dx) % NX) for x in range(NX)])  12 us
    all_to_all x2, starting transfers between devices, exchange_z(): lax.all_to_all(a, 'seq', split_axis=0, concat_axis=0, axis_index_groups=L...  12 us
    ppermute x6, starting transfers between devices, tp_move(): return lax.ppermute(a, 'tp', [(x, (x + dx) % NX) for x in range(NX)])  10 us
    unnamed x14, local copies, waits for them, and re-layouts  4.41 us
    all_to_all x2, waiting for transfers between devices, exchange_z(): lax.all_to_all(a, 'seq', split_axis=0, concat_axis=0, axis_index_groups=L...  4.04 us
  transfers between devices with their start and end apart: 27, of which 9 were waited for; matrix products, arithmetic and copies ran while one was open for 6% of the time, Pallas kernels for 9%

profile of v2, /device:TPU:24, one launch (start us, length us, event | category | flops | bytes accessed | tf_op | source)
XLA Modules:
  0.0 103.1 jit_solution(16897982322791171081)
XLA Ops:
  0.6 0.0 copy-start
  0.7 0.7 broadcast_compare_fusion
  1.4 0.8 broadcast_select_fusion
  2.2 0.7 pad_maximum_fusion
  2.9 0.7 broadcast_in_dim.42
  3.6 8.5 %all-to-all-start = ((bf16[8,64,256]{2,1,0:T(8,128)(2,1)}), bf16[8,64,256]{2,1,0:T(8,128)(2,1)S(1)}, u32[]{:S(2)}, u32[]{:S(2)}) async-start(bf16[8,64,256]{2,1,0:T(8,128)(2,1)} %broadcast_in_dim.42), calls=%async_computation | async-start | bytes 524288 | tf_op jit(solution)/shard_map/all_to_all | solution.py:42
  12.1 0.7 broadcast_select_fusion.1
  12.8 0.9 fusion.1.refs_0_
  13.7 1.6 %collective-permute-start = (bf16[64,1024]{1,0:T(8,128)(2,1)S(1)}, bf16[64,1024]{1,0:T(8,128)(2,1)S(1)}, u32[]{:S(2)}, u32[]{:S(2)}) collective-permute-start(bf16[64,1024]{1,0:T(8,128)(2,1)S(1)} %fusion.1.refs_0_), channel_id=1, source_target_pairs={{0,1},{1,2},{2,3},{3,0},{4,5},{5,6},{6,7},{7,4},{8,9},{9,10},{10,1... | collective-permute-start | bytes 393224 | tf_op jit(solution)/shard_map/ppermute | solution.py:35
  15.2 4.7 %collective-permute-done.refs_1_ = bf16[64,1024]{1,0:T(8,128)(2,1)S(1)} collective-permute-done((bf16[64,1024]{1,0:T(8,128)(2,1)S(1)}, bf16[64,1024]{1,0:T(8,128)(2,1)S(1)}, u32[]{:S(2)}, u32[]{:S(2)}) %collective-permute-start) | collective-permute-done | bytes 131104 | tf_op jit(solution)/shard_map/ppermute | solution.py:35
  19.9 4.0 %all-to-all-done = bf16[8,64,256]{2,1,0:T(8,128)(2,1)S(1)} async-done(((bf16[8,64,256]{2,1,0:T(8,128)(2,1)}), bf16[8,64,256]{2,1,0:T(8,128)(2,1)S(1)}, u32[]{:S(2)}, u32[]{:S(2)}) %all-to-all-start) | async-done | bytes 262176 | tf_op jit(solution)/shard_map/all_to_all | solution.py:42
  24.0 0.2 collective-permute-start.1
  24.2 1.8 %collective-permute-start.2 = (bf16[512,256]{1,0:T(8,128)(2,1)S(1)}, bf16[512,256]{1,0:T(8,128)(2,1)S(1)}, u32[]{:S(2)}, u32[]{:S(2)}) collective-permute-start(bf16[512,256]{1,0:T(8,128)(2,1)S(1)} %bitcast.12), channel_id=1, source_target_pairs={{0,24},{4,28},{8,0},{12,4},{16,8},{20,12},{24,16},{28,20},{32,56},... | collective-permute-start | bytes 786440 | tf_op jit(solution)/shard_map/ppermute | solution.py:31
  26.0 1.2 %collective-permute-start.3 = (bf16[512,256]{1,0:T(8,128)(2,1)S(1)}, bf16[512,256]{1,0:T(8,128)(2,1)S(1)}, u32[]{:S(2)}, u32[]{:S(2)}) collective-permute-start(bf16[512,256]{1,0:T(8,128)(2,1)S(1)} %bitcast.13), channel_id=1, source_target_pairs={{0,16},{4,20},{8,24},{12,28},{16,0},{20,4},{24,8},{28,12},{32,48},... | collective-permute-start | bytes 786440 | tf_op jit(solution)/shard_map/ppermute | solution.py:31
  27.2 3.0 %collective-permute-start.4 = (bf16[64,1024]{1,0:T(8,128)(2,1)S(1)}, bf16[64,1024]{1,0:T(8,128)(2,1)S(1)}, u32[]{:S(2)}, u32[]{:S(2)}) collective-permute-start(bf16[64,1024]{1,0:T(8,128)(2,1)S(1)} %fusion.1.refs_0_), channel_id=1, source_target_pairs={{0,2},{1,3},{2,0},{3,1},{4,6},{5,7},{6,4},{7,5},{8,10},{9,11},{10,... | collective-permute-start | bytes 393224 | tf_op jit(solution)/shard_map/ppermute | solution.py:35
  30.2 1.1 %collective-permute-start.5 = (bf16[64,1024]{1,0:T(8,128)(2,1)S(1)}, bf16[64,1024]{1,0:T(8,128)(2,1)S(1)}, u32[]{:S(2)}, u32[]{:S(2)}) collective-permute-start(bf16[64,1024]{1,0:T(8,128)(2,1)S(1)} %fusion.1.refs_0_), channel_id=1, source_target_pairs={{0,3},{1,0},{2,1},{3,2},{4,7},{5,4},{6,5},{7,6},{8,11},{9,8},{10,9... | collective-permute-start | bytes 393224 | tf_op jit(solution)/shard_map/ppermute | solution.py:35
  31.4 0.1 pad_add_fusion.place
  31.5 2.2 %collective-permute-done.4.refs_2_ = bf16[64,1024]{1,0:T(8,128)(2,1)S(1)} collective-permute-done((bf16[64,1024]{1,0:T(8,128)(2,1)S(1)}, bf16[64,1024]{1,0:T(8,128)(2,1)S(1)}, u32[]{:S(2)}, u32[]{:S(2)}) %collective-permute-start.4) | collective-permute-done | bytes 131104 | tf_op jit(solution)/shard_map/ppermute | solution.py:35
  33.7 1.5 %collective-permute-done.5.refs_3_ = bf16[64,1024]{1,0:T(8,128)(2,1)S(1)} collective-permute-done((bf16[64,1024]{1,0:T(8,128)(2,1)S(1)}, bf16[64,1024]{1,0:T(8,128)(2,1)S(1)}, u32[]{:S(2)}, u32[]{:S(2)}) %collective-permute-start.5) | collective-permute-done | bytes 131104 | tf_op jit(solution)/shard_map/ppermute | solution.py:35
  35.2 2.2 %copy-done.1 = bf16[512,4096]{1,0:T(8,128)(2,1)S(1)} copy-done((bf16[512,4096]{1,0:T(8,128)(2,1)S(1)}, bf16[512,4096]{1,0:T(8,128)(2,1)}, u32[]{:S(2)}) %copy-start.1) | copy-done | bytes 4194328
  37.4 2.0 %shard_map.127 = (bf16[64,512]{1,0:T(8,128)(2,1)S(1)}, bf16[64,1024]{1,0:T(8,128)(2,1)S(1)}, bf16[64,1024]{1,0:T(8,128)(2,1)S(1)}, bf16[64,1024]{1,0:T(8,128)(2,1)S(1)}, bf16[64,1024]{1,0:T(8,128)(2,1)S(1)}) custom-call(s32[4]{0:T(128)S(1)} %pad_add_fusion.place, bf16[64,1024]{1,0:T(8,128)(2,1)S(1)} %fusion.1.refs_0_, ...), custom_call_target="tpu_custom_call" | custom-call | flops 268435456 | bytes 5308416 | tf_op jit(solution)/shard_map/pallas_call | solution.py:247
  39.4 0.0 collective-permute-done.1.refs_1_
  39.4 0.1 collective-permute-start.6
  39.5 0.5 collective-permute-start.7
  40.0 0.1 collective-permute-start.8
  40.1 0.4 collective-permute-start.9
  40.5 1.9 %shard_map.128 = (f32[16,256]{1,0:T(8,128)S(1)}, f32[128,256]{1,0:T(8,128)S(1)}) custom-call(s32[4]{0:T(128)S(1)} %pad_add_fusion.place, bf16[64,512]{1,0:T(8,128)(2,1)S(1)} %copy-done.3, bf16[512,256]{1,0:T(8,128)(2,1)S(1)} %bitcast.15, bf16[512,256]{1,0:T(8,128)(2,1)S(1)} %collective-permute-done.1.refs_1_, ...), custom_call_target="tpu_custom_call" | custom-call | flops 268435456 | bytes 1261568 | tf_op jit(solution)/shard_map/pallas_call | solution.py:247
  42.5 2.0 %shard_map.129 = (bf16[64,512]{1,0:T(8,128)(2,1)S(1)}, f32[8,256]{1,0:T(8,128)S(1)}, bf16[64,1536]{1,0:T(8,128)(2,1)S(1)}, bf16[64,1536]{1,0:T(8,128)(2,1)S(1)},...) custom-call(s32[4]{0:T(128)S(1)} %pad_add_fusion.place, bf16[64,512]{1,0:T(8,128)(2,1)S(1)} %copy-done.3, ...), custom_call_target="tpu_custom_call" | custom-call | flops 268435456 | bytes 2646016 | tf_op jit(solution)/shard_map/pallas_call | solution.py:247
  44.6 2.2 %shard_map.130 = (bf16[2048,256]{1,0:T(8,128)(2,1)S(1)}, f32[128,256]{1,0:T(8,128)S(1)}) custom-call(s32[4]{0:T(128)S(1)} %pad_add_fusion.place, bf16[64,512]{1,0:T(8,128)(2,1)S(1)} %copy-done.3, bf16[64,512]{1,0:T(8,128)(2,1)S(1)} %get-tuple-element.68.g_ref, bf16[64,512]{1,0:T(8,128)(2,1)S(1)} %get-tuple-element.82.att_ref, ...), custom_call_target="tpu_custom_call" | custom-call | flops 671088640 | bytes 2433024 | tf_op jit(solution)/shard_map/pallas_call | solution.py:247
  46.8 0.2 collective-permute-start.10
  47.0 2.2 %collective-permute-start.21 = (bf16[64,1536]{1,0:T(8,128)(2,1)S(1)}, bf16[64,1536]{1,0:T(8,128)(2,1)S(1)}, u32[]{:S(2)}, u32[]{:S(2)}) collective-permute-start(bf16[64,1536]{1,0:T(8,128)(2,1)S(1)} %get-tuple-element.89), channel_id=1, source_target_pairs={{0,8},{4,12},{8,16},{12,20},{16,24},{20,28},{24,0},{28,4},{32,40},... | collective-permute-start | bytes 589832 | tf_op jit(solution)/shard_map/ppermute | solution.py:31
  49.2 2.1 %collective-permute-start.23 = (bf16[64,1536]{1,0:T(8,128)(2,1)S(1)}, bf16[64,1536]{1,0:T(8,128)(2,1)S(1)}, u32[]{:S(2)}, u32[]{:S(2)}) collective-permute-start(bf16[64,1536]{1,0:T(8,128)(2,1)S(1)} %get-tuple-element.91), channel_id=1, source_target_pairs={{0,16},{4,20},{8,24},{12,28},{16,0},{20,4},{24,8},{28,12},{32,48},... | collective-permute-start | bytes 589832 | tf_op jit(solution)/shard_map/ppermute | solution.py:31
  51.3 2.9 %shard_map.131 = (bf16[512,256]{1,0:T(8,128)(2,1)S(1)}, bf16[512,256]{1,0:T(8,128)(2,1)S(1)}, bf16[512,256]{1,0:T(8,128)(2,1)S(1)}, bf16[512,256]{1,0:T(8,128)(2,1)S(1)}, bf16[64,512]{1,0:T(8,128)(2,1)}) custom-call(s32[4]{0:T(128)S(1)} %pad_add_fusion.place, bf16[64,512]{1,0:T(8,128)(2,1)S(1)} %copy-done.3, bf16[64,512]{1,0:T(8,128)(2,1)S(1)} %get-tuple-element.68.g_ref, ...), custom_call_target="tpu_custom_call" | custom-call | flops 671088640 | bytes 2498560 | tf_op jit(solution)/shard_map/pallas_call | solution.py:247
  54.2 0.3 add_convert_fusion.1
  54.5 2.0 %collective-permute-start.11 = (bf16[512,256]{1,0:T(8,128)(2,1)S(1)}, bf16[512,256]{1,0:T(8,128)(2,1)S(1)}, u32[]{:S(2)}, u32[]{:S(2)}) collective-permute-start(bf16[512,256]{1,0:T(8,128)(2,1)S(1)} %get-tuple-element.98), channel_id=1, source_target_pairs={{0,24},{4,28},{8,0},{12,4},{16,8},{20,12},{24,16},{28,20},{32,56},... | collective-permute-start | bytes 786440 | tf_op jit(solution)/shard_map/ppermute | solution.py:31
  56.5 1.3 %collective-permute-start.12 = (bf16[512,256]{1,0:T(8,128)(2,1)S(1)}, bf16[512,256]{1,0:T(8,128)(2,1)S(1)}, u32[]{:S(2)}, u32[]{:S(2)}) collective-permute-start(bf16[512,256]{1,0:T(8,128)(2,1)S(1)} %get-tuple-element.97), channel_id=1, source_target_pairs={{0,8},{4,12},{8,16},{12,20},{16,24},{20,28},{24,0},{28,4},{32,40},... | collective-permute-start | bytes 786440 | tf_op jit(solution)/shard_map/ppermute | solution.py:31
  57.8 0.6 collective-permute-done.21.refs_1_
  58.4 0.2 collective-permute-start.13
  58.7 3.6 %collective-permute-done.22.refs_2_ = bf16[64,1536]{1,0:T(8,128)(2,1)S(1)} collective-permute-done((bf16[64,1536]{1,0:T(8,128)(2,1)S(1)}, bf16[64,1536]{1,0:T(8,128)(2,1)S(1)}, u32[]{:S(2)}, u32[]{:S(2)}) %collective-permute-start.22) | collective-permute-done | bytes 196640 | tf_op jit(solution)/shard_map/ppermute | solution.py:31
  62.3 1.0 shard_map.133
  63.3 0.1 collective-permute-start.24
  63.4 9.3 %collective-permute-done.11 = bf16[512,256]{1,0:T(8,128)(2,1)S(1)} collective-permute-done((bf16[512,256]{1,0:T(8,128)(2,1)S(1)}, bf16[512,256]{1,0:T(8,128)(2,1)S(1)}, u32[]{:S(2)}, u32[]{:S(2)}) %collective-permute-start.11) | collective-permute-done | bytes 262176 | tf_op jit(solution)/shard_map/ppermute | solution.py:31
  72.8 0.1 add_convert_fusion.5
  72.8 0.6 collective-permute-start.14
  73.4 4.8 %collective-permute-start.15 = (bf16[128,256]{1,0:T(8,128)(2,1)S(1)}, bf16[128,256]{1,0:T(8,128)(2,1)S(1)}, u32[]{:S(2)}, u32[]{:S(2)}) collective-permute-start(bf16[128,256]{1,0:T(8,128)(2,1)S(1)} %add_convert_fusion.7), channel_id=1, source_target_pairs={{0,160},{4,164},{8,168},{12,172},{16,176},{20,180},{24,184},{28,18... | collective-permute-start | bytes 196616 | tf_op jit(solution)/shard_map/ppermute | solution.py:31
  78.3 0.9 add_convert_fusion
  79.2 3.5 %all-to-all-start.1 = ((bf16[8,64,512]{2,1,0:T(8,128)(2,1)}), bf16[8,64,512]{2,1,0:T(8,128)(2,1)S(1)}, u32[]{:S(2)}, u32[]{:S(2)}) async-start(bf16[8,64,512]{2,1,0:T(8,128)(2,1)} %bitcast.5), calls=%async_computation.1 | async-start | bytes 1048576 | tf_op jit(solution)/shard_map/all_to_all | solution.py:42
  82.7 0.1 add_convert_fusion.8
  82.8 0.0 copy-start.5
  82.8 0.0 copy-start.6
  82.8 3.2 %collective-permute-start.19 = (bf16[64,256]{1,0:T(8,128)(2,1)S(1)}, bf16[64,256]{1,0:T(8,128)(2,1)S(1)}, u32[]{:S(2)}, u32[]{:S(2)}) collective-permute-start(bf16[64,256]{1,0:T(8,128)(2,1)S(1)} %get-tuple-element.80), channel_id=1, source_target_pairs={{0,224},{4,228},{8,232},{12,236},{16,240},{20,244},{24,248},{28,25... | collective-permute-start | bytes 98312 | tf_op jit(solution)/shard_map/ppermute | solution.py:31
  86.1 2.2 %copy-done.2 = bf16[512,4096]{1,0:T(8,128)(2,1)S(1)} copy-done((bf16[512,4096]{1,0:T(8,128)(2,1)S(1)}, bf16[512,4096]{1,0:T(8,128)(2,1)}, u32[]{:S(2)}) %copy-start.2) | copy-done | bytes 4194328
  88.2 1.4 %shard_map.132 = (bf16[64,1152]{1,0:T(8,128)(2,1)S(1)}, bf16[64,1152]{1,0:T(8,128)(2,1)S(1)}, bf16[64,1152]{1,0:T(8,128)(2,1)S(1)}, bf16[64,1152]{1,0:T(8,128)(2,1)S(1)}) custom-call(s32[4]{0:T(128)S(1)} %pad_add_fusion.place, bf16[64,512]{1,0:T(8,128)(2,1)S(1)} %get-tuple-element.82.att_ref, bf16[64,512]{1,0:T(8,128)(2,1)S(1)} %get-tuple-element.68.g_ref, ...), custom_call_target="tpu_custom_call" | custom-call | flops 5368709120 | bytes 4915200 | tf_op jit(solution)/shard_map/pallas_call | solution.py:247
  89.6 2.7 %collective-permute-start.16 = (bf16[64,1152]{1,0:T(8,128)(2,1)S(1)}, bf16[64,1152]{1,0:T(8,128)(2,1)S(1)}, u32[]{:S(2)}, u32[]{:S(2)}) collective-permute-start(bf16[64,1152]{1,0:T(8,128)(2,1)S(1)} %get-tuple-element.84), channel_id=1, source_target_pairs={{0,3},{1,0},{2,1},{3,2},{4,7},{5,4},{6,5},{7,6},{8,11},{9,8},{10,9... | collective-permute-start | bytes 442376 | tf_op jit(solution)/shard_map/ppermute | solution.py:35
  92.4 1.6 %collective-permute-start.18 = (bf16[64,1152]{1,0:T(8,128)(2,1)S(1)}, bf16[64,1152]{1,0:T(8,128)(2,1)S(1)}, u32[]{:S(2)}, u32[]{:S(2)}) collective-permute-start(bf16[64,1152]{1,0:T(8,128)(2,1)S(1)} %get-tuple-element.86), channel_id=1, source_target_pairs={{0,2},{1,3},{2,0},{3,1},{4,6},{5,7},{6,4},{7,5},{8,10},{9,11},{10,... | collective-permute-start | bytes 442376 | tf_op jit(solution)/shard_map/ppermute | solution.py:35
  93.9 2.2 %collective-permute-done.19 = bf16[64,256]{1,0:T(8,128)(2,1)S(1)} collective-permute-done((bf16[64,256]{1,0:T(8,128)(2,1)S(1)}, bf16[64,256]{1,0:T(8,128)(2,1)S(1)}, u32[]{:S(2)}, u32[]{:S(2)}) %collective-permute-start.19) | collective-permute-done | bytes 32800 | tf_op jit(solution)/shard_map/ppermute | solution.py:31
  96.1 0.1 select_convert_fusion
  96.2 0.6 fusion.9
  96.8 3.6 %collective-permute-done.17 = bf16[64,1152]{1,0:T(8,128)(2,1)S(1)} collective-permute-done((bf16[64,1152]{1,0:T(8,128)(2,1)S(1)}, bf16[64,1152]{1,0:T(8,128)(2,1)S(1)}, u32[]{:S(2)}, u32[]{:S(2)}) %collective-permute-start.17) | collective-permute-done | bytes 147488 | tf_op jit(solution)/shard_map/ppermute | solution.py:35
  100.4 0.1 convert_add_fusion
  100.5 0.2 fusion.6
  100.7 0.5 divide_select_fusion
  101.2 1.2 %fusion = bf16[256,1024]{1,0:T(8,128)(2,1)} fusion(bf16[256,1024]{1,0:T(8,128)(2,1)S(1)} %copy-done.4, f32[64,1152]{1,0:T(8,128)S(1)} %convert_add_fusion, f32[64]{0:T(128)S(1)} %broadcast_select_fusion.1, s32[64]{0:T(128)S(1)} %copy-done.5), kind=kOutput, calls=%fused_computation.1 | convolution fusion | flops 34488320 | bytes 1311744 | tf_op jit(solution)/shard_map/dot_general | solution.py:70
  102.4 0.7 fusion.5
  (30 shorter events, 0.1 us)
Async XLA Ops:
  0.6 12.1 %copy-start = (bf16[256,1024]{1,0:T(8,128)(2,1)S(1)}, bf16[256,1024]{1,0:T(8,128)(2,1)}, u32[]{:S(2)}) copy-start(bf16[256,1024]{1,0:T(8,128)(2,1)} %param.9) | copy-start | bytes 1572868
  0.6 39.9 %copy-start.3 = (bf16[64,512]{1,0:T(8,128)(2,1)S(1)}, bf16[64,512]{1,0:T(8,128)(2,1)}, u32[]{:S(2)}) copy-start(bf16[64,512]{1,0:T(8,128)(2,1)} %q_ref.7) | copy-start | bytes 196612
  3.6 20.3 %all-to-all-start = ((bf16[8,64,256]{2,1,0:T(8,128)(2,1)}), bf16[8,64,256]{2,1,0:T(8,128)(2,1)S(1)}, u32[]{:S(2)}, u32[]{:S(2)}) async-start(bf16[8,64,256]{2,1,0:T(8,128)(2,1)} %broadcast_in_dim.42), calls=%async_computation | async-start | bytes 524288 | tf_op jit(solution)/shard_map/all_to_all | solution.py:42
  13.7 6.3 %collective-permute-start = (bf16[64,1024]{1,0:T(8,128)(2,1)S(1)}, bf16[64,1024]{1,0:T(8,128)(2,1)S(1)}, u32[]{:S(2)}, u32[]{:S(2)}) collective-permute-start(bf16[64,1024]{1,0:T(8,128)(2,1)S(1)} %fusion.1.refs_0_), channel_id=1, source_target_pairs={{0,1},{1,2},{2,3},{3,0},{4,5},{5,6},{6,7},{7,4},{8,9},{9,10},{10,1... | collective-permute-start | bytes 393224 | tf_op jit(solution)/shard_map/ppermute | solution.py:35
  24.0 15.4 %collective-permute-start.1 = (bf16[512,256]{1,0:T(8,128)(2,1)S(1)}, bf16[512,256]{1,0:T(8,128)(2,1)S(1)}, u32[]{:S(2)}, u32[]{:S(2)}) collective-permute-start(bf16[512,256]{1,0:T(8,128)(2,1)S(1)} %bitcast.11), channel_id=1, source_target_pairs={{0,8},{4,12},{8,16},{12,20},{16,24},{20,28},{24,0},{28,4},{32,40},... | collective-permute-start | bytes 786440 | tf_op jit(solution)/shard_map/ppermute | solution.py:31
  24.2 15.2 %collective-permute-start.2 = (bf16[512,256]{1,0:T(8,128)(2,1)S(1)}, bf16[512,256]{1,0:T(8,128)(2,1)S(1)}, u32[]{:S(2)}, u32[]{:S(2)}) collective-permute-start(bf16[512,256]{1,0:T(8,128)(2,1)S(1)} %bitcast.12), channel_id=1, source_target_pairs={{0,24},{4,28},{8,0},{12,4},{16,8},{20,12},{24,16},{28,20},{32,56},... | collective-permute-start | bytes 786440 | tf_op jit(solution)/shard_map/ppermute | solution.py:31
  26.0 13.4 %collective-permute-start.3 = (bf16[512,256]{1,0:T(8,128)(2,1)S(1)}, bf16[512,256]{1,0:T(8,128)(2,1)S(1)}, u32[]{:S(2)}, u32[]{:S(2)}) collective-permute-start(bf16[512,256]{1,0:T(8,128)(2,1)S(1)} %bitcast.13), channel_id=1, source_target_pairs={{0,16},{4,20},{8,24},{12,28},{16,0},{20,4},{24,8},{28,12},{32,48},... | collective-permute-start | bytes 786440 | tf_op jit(solution)/shard_map/ppermute | solution.py:31
  27.2 6.5 %collective-permute-start.4 = (bf16[64,1024]{1,0:T(8,128)(2,1)S(1)}, bf16[64,1024]{1,0:T(8,128)(2,1)S(1)}, u32[]{:S(2)}, u32[]{:S(2)}) collective-permute-start(bf16[64,1024]{1,0:T(8,128)(2,1)S(1)} %fusion.1.refs_0_), channel_id=1, source_target_pairs={{0,2},{1,3},{2,0},{3,1},{4,6},{5,7},{6,4},{7,5},{8,10},{9,11},{10,... | collective-permute-start | bytes 393224 | tf_op jit(solution)/shard_map/ppermute | solution.py:35
  30.2 5.0 %collective-permute-start.5 = (bf16[64,1024]{1,0:T(8,128)(2,1)S(1)}, bf16[64,1024]{1,0:T(8,128)(2,1)S(1)}, u32[]{:S(2)}, u32[]{:S(2)}) collective-permute-start(bf16[64,1024]{1,0:T(8,128)(2,1)S(1)} %fusion.1.refs_0_), channel_id=1, source_target_pairs={{0,3},{1,0},{2,1},{3,2},{4,7},{5,4},{6,5},{7,6},{8,11},{9,8},{10,9... | collective-permute-start | bytes 393224 | tf_op jit(solution)/shard_map/ppermute | solution.py:35
  35.2 2.2 %copy-start.1 = (bf16[512,4096]{1,0:T(8,128)(2,1)S(1)}, bf16[512,4096]{1,0:T(8,128)(2,1)}, u32[]{:S(2)}) copy-start(bf16[512,4096]{1,0:T(8,128)(2,1)} %w_ref.1) | copy-start | bytes 12582916
  39.4 3.1 %collective-permute-start.6 = (bf16[512,256]{1,0:T(8,128)(2,1)S(1)}, bf16[512,256]{1,0:T(8,128)(2,1)S(1)}, u32[]{:S(2)}, u32[]{:S(2)}) collective-permute-start(bf16[512,256]{1,0:T(8,128)(2,1)S(1)} %bitcast.14), channel_id=1, source_target_pairs={{0,4},{4,0},{8,12},{12,8},{16,20},{20,16},{24,28},{28,24},{32,36},... | collective-permute-start | bytes 786440 | tf_op jit(solution)/shard_map/ppermute | solution.py:31
  39.5 3.0 %collective-permute-start.7 = (bf16[512,256]{1,0:T(8,128)(2,1)S(1)}, bf16[512,256]{1,0:T(8,128)(2,1)S(1)}, u32[]{:S(2)}, u32[]{:S(2)}) collective-permute-start(bf16[512,256]{1,0:T(8,128)(2,1)S(1)} %collective-permute-done.1.refs_1_), channel_id=1, source_target_pairs={{0,4},{4,0},{8,12},{12,8},{16,20},{20,16},{24,28},{28,24},{32,36},... | collective-permute-start | bytes 786440 | tf_op jit(solution)/shard_map/ppermute | solution.py:31
  40.0 2.5 %collective-permute-start.8 = (bf16[512,256]{1,0:T(8,128)(2,1)S(1)}, bf16[512,256]{1,0:T(8,128)(2,1)S(1)}, u32[]{:S(2)}, u32[]{:S(2)}) collective-permute-start(bf16[512,256]{1,0:T(8,128)(2,1)S(1)} %collective-permute-done.2.refs_2_), channel_id=1, source_target_pairs={{0,4},{4,0},{8,12},{12,8},{16,20},{20,16},{24,28},{28,24},{32,36},... | collective-permute-start | bytes 786440 | tf_op jit(solution)/shard_map/ppermute | solution.py:31
  40.1 2.4 %collective-permute-start.9 = (bf16[512,256]{1,0:T(8,128)(2,1)S(1)}, bf16[512,256]{1,0:T(8,128)(2,1)S(1)}, u32[]{:S(2)}, u32[]{:S(2)}) collective-permute-start(bf16[512,256]{1,0:T(8,128)(2,1)S(1)} %collective-permute-done.3.refs_3_), channel_id=1, source_target_pairs={{0,4},{4,0},{8,12},{12,8},{16,20},{20,16},{24,28},{28,24},{32,36},... | collective-permute-start | bytes 786440 | tf_op jit(solution)/shard_map/ppermute | solution.py:31
  46.8 7.4 %collective-permute-start.10 = (bf16[2048,256]{1,0:T(8,128)(2,1)S(1)}, bf16[2048,256]{1,0:T(8,128)(2,1)S(1)}, u32[]{:S(2)}, u32[]{:S(2)}) collective-permute-start(bf16[2048,256]{1,0:T(8,128)(2,1)S(1)} %get-tuple-element.72), channel_id=1, source_target_pairs={{0,4},{4,0},{8,12},{12,8},{16,20},{20,16},{24,28},{28,24},{32,36},... | collective-permute-start | bytes 3145736 | tf_op jit(solution)/shard_map/ppermute | solution.py:31
  47.0 11.5 %collective-permute-start.21 = (bf16[64,1536]{1,0:T(8,128)(2,1)S(1)}, bf16[64,1536]{1,0:T(8,128)(2,1)S(1)}, u32[]{:S(2)}, u32[]{:S(2)}) collective-permute-start(bf16[64,1536]{1,0:T(8,128)(2,1)S(1)} %get-tuple-element.89), channel_id=1, source_target_pairs={{0,8},{4,12},{8,16},{12,20},{16,24},{20,28},{24,0},{28,4},{32,40},... | collective-permute-start | bytes 589832 | tf_op jit(solution)/shard_map/ppermute | solution.py:31
  49.2 13.2 %collective-permute-start.22 = (bf16[64,1536]{1,0:T(8,128)(2,1)S(1)}, bf16[64,1536]{1,0:T(8,128)(2,1)S(1)}, u32[]{:S(2)}, u32[]{:S(2)}) collective-permute-start(bf16[64,1536]{1,0:T(8,128)(2,1)S(1)} %get-tuple-element.90), channel_id=1, source_target_pairs={{0,24},{4,28},{8,0},{12,4},{16,8},{20,12},{24,16},{28,20},{32,56},... | collective-permute-start | bytes 589832 | tf_op jit(solution)/shard_map/ppermute | solution.py:31
  49.2 13.2 %collective-permute-start.23 = (bf16[64,1536]{1,0:T(8,128)(2,1)S(1)}, bf16[64,1536]{1,0:T(8,128)(2,1)S(1)}, u32[]{:S(2)}, u32[]{:S(2)}) collective-permute-start(bf16[64,1536]{1,0:T(8,128)(2,1)S(1)} %get-tuple-element.91), channel_id=1, source_target_pairs={{0,16},{4,20},{8,24},{12,28},{16,0},{20,4},{24,8},{28,12},{32,48},... | collective-permute-start | bytes 589832 | tf_op jit(solution)/shard_map/ppermute | solution.py:31
  54.5 18.3 %collective-permute-start.11 = (bf16[512,256]{1,0:T(8,128)(2,1)S(1)}, bf16[512,256]{1,0:T(8,128)(2,1)S(1)}, u32[]{:S(2)}, u32[]{:S(2)}) collective-permute-start(bf16[512,256]{1,0:T(8,128)(2,1)S(1)} %get-tuple-element.98), channel_id=1, source_target_pairs={{0,24},{4,28},{8,0},{12,4},{16,8},{20,12},{24,16},{28,20},{32,56},... | collective-permute-start | bytes 786440 | tf_op jit(solution)/shard_map/ppermute | solution.py:31
  56.5 16.2 %collective-permute-start.12 = (bf16[512,256]{1,0:T(8,128)(2,1)S(1)}, bf16[512,256]{1,0:T(8,128)(2,1)S(1)}, u32[]{:S(2)}, u32[]{:S(2)}) collective-permute-start(bf16[512,256]{1,0:T(8,128)(2,1)S(1)} %get-tuple-element.97), channel_id=1, source_target_pairs={{0,8},{4,12},{8,16},{12,20},{16,24},{20,28},{24,0},{28,4},{32,40},... | collective-permute-start | bytes 786440 | tf_op jit(solution)/shard_map/ppermute | solution.py:31
  58.4 14.3 %collective-permute-start.13 = (bf16[512,256]{1,0:T(8,128)(2,1)S(1)}, bf16[512,256]{1,0:T(8,128)(2,1)S(1)}, u32[]{:S(2)}, u32[]{:S(2)}) collective-permute-start(bf16[512,256]{1,0:T(8,128)(2,1)S(1)} %get-tuple-element.96), channel_id=1, source_target_pairs={{0,16},{4,20},{8,24},{12,28},{16,0},{20,4},{24,8},{28,12},{32,48},... | collective-permute-start | bytes 786440 | tf_op jit(solution)/shard_map/ppermute | solution.py:31
  63.3 14.9 %collective-permute-start.24 = (bf16[512,512]{1,0:T(8,128)(2,1)S(1)}, bf16[512,512]{1,0:T(8,128)(2,1)S(1)}, u32[]{:S(2)}, u32[]{:S(2)}) collective-permute-start(bf16[512,512]{1,0:T(8,128)(2,1)S(1)} %get-tuple-element.93), channel_id=1, source_target_pairs={{0,4},{4,0},{8,12},{12,8},{16,20},{20,16},{24,28},{28,24},{32,36},... | collective-permute-start | bytes 1572872 | tf_op jit(solution)/shard_map/ppermute | solution.py:31
  72.8 9.9 %collective-permute-start.14 = (bf16[192,256]{1,0:T(8,128)(2,1)S(1)}, bf16[192,256]{1,0:T(8,128)(2,1)S(1)}, u32[]{:S(2)}, u32[]{:S(2)}) collective-permute-start(bf16[192,256]{1,0:T(8,128)(2,1)S(1)} %add_convert_fusion.5), channel_id=1, source_target_pairs={{0,96},{4,100},{8,104},{12,108},{16,112},{20,116},{24,120},{28,124... | collective-permute-start | bytes 294920 | tf_op jit(solution)/shard_map/ppermute | solution.py:31
  73.4 9.3 %collective-permute-start.15 = (bf16[128,256]{1,0:T(8,128)(2,1)S(1)}, bf16[128,256]{1,0:T(8,128)(2,1)S(1)}, u32[]{:S(2)}, u32[]{:S(2)}) collective-permute-start(bf16[128,256]{1,0:T(8,128)(2,1)S(1)} %add_convert_fusion.7), channel_id=1, source_target_pairs={{0,160},{4,164},{8,168},{12,172},{16,176},{20,180},{24,184},{28,18... | collective-permute-start | bytes 196616 | tf_op jit(solution)/shard_map/ppermute | solution.py:31
  79.2 23.2 %all-to-all-start.1 = ((bf16[8,64,512]{2,1,0:T(8,128)(2,1)}), bf16[8,64,512]{2,1,0:T(8,128)(2,1)S(1)}, u32[]{:S(2)}, u32[]{:S(2)}) async-start(bf16[8,64,512]{2,1,0:T(8,128)(2,1)} %bitcast.5), calls=%async_computation.1 | async-start | bytes 1048576 | tf_op jit(solution)/shard_map/all_to_all | solution.py:42
  82.8 17.9 %copy-start.5 = (s32[64]{0:T(128)S(1)}, s32[64]{0:T(128)}, u32[]{:S(2)}) copy-start(s32[64]{0:T(128)} %param.10) | copy-start | bytes 772
  82.8 17.9 %copy-start.6 = (f32[64]{0:T(128)S(1)}, f32[64]{0:T(128)}, u32[]{:S(2)}) copy-start(f32[64]{0:T(128)} %param.14) | copy-start | bytes 772
  82.8 13.3 %collective-permute-start.19 = (bf16[64,256]{1,0:T(8,128)(2,1)S(1)}, bf16[64,256]{1,0:T(8,128)(2,1)S(1)}, u32[]{:S(2)}, u32[]{:S(2)}) collective-permute-start(bf16[64,256]{1,0:T(8,128)(2,1)S(1)} %get-tuple-element.80), channel_id=1, source_target_pairs={{0,224},{4,228},{8,232},{12,236},{16,240},{20,244},{24,248},{28,25... | collective-permute-start | bytes 98312 | tf_op jit(solution)/shard_map/ppermute | solution.py:31
  86.0 10.1 %collective-permute-start.20 = (bf16[64,256]{1,0:T(8,128)(2,1)S(1)}, bf16[64,256]{1,0:T(8,128)(2,1)S(1)}, u32[]{:S(2)}, u32[]{:S(2)}) collective-permute-start(bf16[64,256]{1,0:T(8,128)(2,1)S(1)} %get-tuple-element.81), channel_id=1, source_target_pairs={{0,32},{4,36},{8,40},{12,44},{16,48},{20,52},{24,56},{28,60},{32,6... | collective-permute-start | bytes 98312 | tf_op jit(solution)/shard_map/ppermute | solution.py:31
  86.0 2.2 %copy-start.2 = (bf16[512,4096]{1,0:T(8,128)(2,1)S(1)}, bf16[512,4096]{1,0:T(8,128)(2,1)}, u32[]{:S(2)}) copy-start(bf16[512,4096]{1,0:T(8,128)(2,1)} %w_ref.1) | copy-start | bytes 12582916
  88.2 13.0 %copy-start.4 = (bf16[256,1024]{1,0:T(8,128)(2,1)S(1)}, bf16[256,1024]{1,0:T(8,128)(2,1)}, u32[]{:S(2)}) copy-start(bf16[256,1024]{1,0:T(8,128)(2,1)} %param.8) | copy-start | bytes 1572868
  89.6 7.2 %collective-permute-start.16 = (bf16[64,1152]{1,0:T(8,128)(2,1)S(1)}, bf16[64,1152]{1,0:T(8,128)(2,1)S(1)}, u32[]{:S(2)}, u32[]{:S(2)}) collective-permute-start(bf16[64,1152]{1,0:T(8,128)(2,1)S(1)} %get-tuple-element.84), channel_id=1, source_target_pairs={{0,3},{1,0},{2,1},{3,2},{4,7},{5,4},{6,5},{7,6},{8,11},{9,8},{10,9... | collective-permute-start | bytes 442376 | tf_op jit(solution)/shard_map/ppermute | solution.py:35
  92.4 8.0 %collective-permute-start.17 = (bf16[64,1152]{1,0:T(8,128)(2,1)S(1)}, bf16[64,1152]{1,0:T(8,128)(2,1)S(1)}, u32[]{:S(2)}, u32[]{:S(2)}) collective-permute-start(bf16[64,1152]{1,0:T(8,128)(2,1)S(1)} %get-tuple-element.85), channel_id=1, source_target_pairs={{0,1},{1,2},{2,3},{3,0},{4,5},{5,6},{6,7},{7,4},{8,9},{9,10},{10,1... | collective-permute-start | bytes 442376 | tf_op jit(solution)/shard_map/ppermute | solution.py:35
  92.4 8.0 %collective-permute-start.18 = (bf16[64,1152]{1,0:T(8,128)(2,1)S(1)}, bf16[64,1152]{1,0:T(8,128)(2,1)S(1)}, u32[]{:S(2)}, u32[]{:S(2)}) collective-permute-start(bf16[64,1152]{1,0:T(8,128)(2,1)S(1)} %get-tuple-element.86), channel_id=1, source_target_pairs={{0,2},{1,3},{2,0},{3,1},{4,6},{5,7},{6,4},{7,5},{8,10},{9,11},{10,... | collective-permute-start | bytes 442376 | tf_op jit(solution)/shard_map/ppermute | solution.py:35

commit v3 on v2

--- a/solution.py
+++ b/solution.py
@@ -209,9 +209,17 @@
             piece[:, (NZ + k) * half : (NZ + k + 2) * half] = other
 
 
-def project_kernel(place, att_ref, g_ref, w_ref, *outs):
+def project_kernel(place, att_ref, g_ref, w_ref, *refs):
+    outs, (blocks, sems) = refs[:NX], refs[NX:]
     x = place[3]
     width = w_ref.shape[1] // NX
+    copies = []
+    for m in range(NX):
+        start = pl.multiple_of(((x + NX - m) & (NX - 1)) * width, width)
+        copies.append(
+            pltpu.make_async_copy(w_ref.at[:, pl.ds(start, width)], blocks.at[m], sems.at[m])
+        )
+        copies[m].start()
     att = att_ref[...]
     delta = jnp.sum(att.astype(F32) * g_ref[...].astype(F32), axis=1, keepdims=True)
     high = delta.astype(BF).astype(F32)
@@ -221,8 +229,8 @@
     zero = jnp.zeros((), F32)
     extra = jnp.where(lane == 0, high, jnp.where(lane == 1, mid, jnp.where(lane == 2, low, zero)))
     for m in range(NX):
-        start = pl.multiple_of(((x + NX - m) & (NX - 1)) * width, width)
-        outs[m][:, :width] = dot(att, w_ref[:, pl.ds(start, width)], 1, 0).astype(BF)
+        copies[m].wait()
+        outs[m][:, :width] = dot(att, blocks[m], 1, 0).astype(BF)
         outs[m][:, width:] = extra.astype(BF)
 
 
@@ -241,13 +249,13 @@
 SM = pl.BlockSpec(memory_space=pltpu.SMEM)
 
 
-def call(kernel, place, args, shapes, flops, scratch=(), limit=32):
+def call(kernel, place, args, shapes, flops, scratch=(), limit=32, last=VM):
     size = sum(math.prod(a.shape) * a.dtype.itemsize for a in args)
     size += sum(math.prod(s.shape) * s.dtype.itemsize for s in shapes)
     return pl.pallas_call(
         kernel,
         out_shape=shapes,
-        in_specs=[SM] + [VM] * len(args),
+        in_specs=[SM] + [VM] * (len(args) - 1) + [last],
         out_specs=[VM] * len(shapes),
         scratch_shapes=list(scratch),
         compiler_params=pltpu.CompilerParams(vmem_limit_bytes=limit * 1024 * 1024),
@@ -354,6 +362,8 @@
         [stage((attended,), below, above)[0], attn_grad, out_weight],
         [shape((SLOTS, width // NX + HEAD), BF)] * NX,
         40 * SLOTS * width * feats,
+        [pltpu.VMEM((NX, feats, width // NX), BF), pltpu.SemaphoreType.DMA((NX,))],
+        last=pl.BlockSpec(memory_space=pltpu.HBM),
     )
     projected = [projected[0]] + [tp_move(projected[m], -m) for m in (1, 3, 2)]
     here = jnp.where(live_col, sum_last(below, above, here), 0.0).astype(BF)

time: 104 us -> 105 us (level)
    ppermute x6, waiting for transfers between devices: 12 us -> 13.1 us  [tp_move(): return lax.ppermute(a, 'tp', [(x, (x + dx) % NX) for x in range(NX)])]
    ppermute x19, waiting for transfers between devices: 15.8 us -> 14.8 us  [seq_move(): return lax.ppermute(a, 'seq', pairs)]
    pallas_call x7, Pallas kernels: 13.5 us -> 14.5 us  [call(): pl.pallas_call(kernel, out_shape=shapes, in_specs=[SM] + [VM] * (len(args...]
  transfers between devices with their start and end apart: 27 -> 27, of which waited for: 9 -> 10; matrix products, arithmetic and copies ran while one was open for 6% -> 5% of each run, Pallas kernels for 9% -> 10%
where the time goes in v3:
time: 105 us; the launch traced here: 104 us
  starting transfers between devices  43.1 us (41%)
  waiting for transfers between devices  31.9 us (30%)
  Pallas kernels  14.5 us (14%)
  other arithmetic  5.9 us (6%)
  local copies, waits for them, and re-layouts  5.74 us (5%)
  matrix products  2.09 us (2%)
    ppermute x19, starting transfers between devices, seq_move(): return lax.ppermute(a, 'seq', pairs)  21.2 us
    ppermute x19, waiting for transfers between devices, seq_move(): return lax.ppermute(a, 'seq', pairs)  14.8 us
    pallas_call x7, Pallas kernels, call(): pl.pallas_call(kernel, out_shape=shapes, in_specs=[SM] + [VM] * (len(args...  14.5 us
    ppermute x6, waiting for transfers between devices, tp_move(): return lax.ppermute(a, 'tp', [(x, (x + dx) % NX) for x in range(NX)])  13.1 us
    all_to_all x2, starting transfers between devices, exchange_z(): lax.all_to_all(a, 'seq', split_axis=0, concat_axis=0, axis_index_groups=L...  12 us
    ppermute x6, starting transfers between devices, tp_move(): return lax.ppermute(a, 'tp', [(x, (x + dx) % NX) for x in range(NX)])  10 us
    unnamed x14, local copies, waits for them, and re-layouts  4.41 us
    all_to_all x2, waiting for transfers between devices, exchange_z(): lax.all_to_all(a, 'seq', split_axis=0, concat_axis=0, axis_index_groups=L...  4.04 us
  transfers between devices with their start and end apart: 27, of which 10 were waited for; matrix products, arithmetic and copies ran while one was open for 5% of the time, Pallas kernels for 10%

profile of v3, /device:TPU:24, one launch (start us, length us, event | category | flops | bytes accessed | tf_op | source)
XLA Modules:
  0.0 104.2 jit_solution(14185999944942651069)
XLA Ops:
  0.6 0.0 copy-start
  0.7 0.7 broadcast_compare_fusion
  1.4 0.8 broadcast_select_fusion
  2.2 0.7 pad_maximum_fusion
  2.9 0.7 broadcast_in_dim.42
  3.6 8.5 %all-to-all-start = ((bf16[8,64,256]{2,1,0:T(8,128)(2,1)}), bf16[8,64,256]{2,1,0:T(8,128)(2,1)S(1)}, u32[]{:S(2)}, u32[]{:S(2)}) async-start(bf16[8,64,256]{2,1,0:T(8,128)(2,1)} %broadcast_in_dim.42), calls=%async_computation | async-start | bytes 524288 | tf_op jit(solution)/shard_map/all_to_all | solution.py:42
  12.1 0.7 broadcast_select_fusion.1
  12.8 0.9 fusion.1.refs_0_
  13.7 1.6 %collective-permute-start = (bf16[64,1024]{1,0:T(8,128)(2,1)S(1)}, bf16[64,1024]{1,0:T(8,128)(2,1)S(1)}, u32[]{:S(2)}, u32[]{:S(2)}) collective-permute-start(bf16[64,1024]{1,0:T(8,128)(2,1)S(1)} %fusion.1.refs_0_), channel_id=1, source_target_pairs={{0,1},{1,2},{2,3},{3,0},{4,5},{5,6},{6,7},{7,4},{8,9},{9,10},{10,1... | collective-permute-start | bytes 393224 | tf_op jit(solution)/shard_map/ppermute | solution.py:35
  15.2 4.7 %collective-permute-done.refs_1_ = bf16[64,1024]{1,0:T(8,128)(2,1)S(1)} collective-permute-done((bf16[64,1024]{1,0:T(8,128)(2,1)S(1)}, bf16[64,1024]{1,0:T(8,128)(2,1)S(1)}, u32[]{:S(2)}, u32[]{:S(2)}) %collective-permute-start) | collective-permute-done | bytes 131104 | tf_op jit(solution)/shard_map/ppermute | solution.py:35
  19.9 4.0 %all-to-all-done = bf16[8,64,256]{2,1,0:T(8,128)(2,1)S(1)} async-done(((bf16[8,64,256]{2,1,0:T(8,128)(2,1)}), bf16[8,64,256]{2,1,0:T(8,128)(2,1)S(1)}, u32[]{:S(2)}, u32[]{:S(2)}) %all-to-all-start) | async-done | bytes 262176 | tf_op jit(solution)/shard_map/all_to_all | solution.py:42
  24.0 0.2 collective-permute-start.1
  24.2 1.8 %collective-permute-start.2 = (bf16[512,256]{1,0:T(8,128)(2,1)S(1)}, bf16[512,256]{1,0:T(8,128)(2,1)S(1)}, u32[]{:S(2)}, u32[]{:S(2)}) collective-permute-start(bf16[512,256]{1,0:T(8,128)(2,1)S(1)} %bitcast.12), channel_id=1, source_target_pairs={{0,24},{4,28},{8,0},{12,4},{16,8},{20,12},{24,16},{28,20},{32,56},... | collective-permute-start | bytes 786440 | tf_op jit(solution)/shard_map/ppermute | solution.py:31
  26.0 1.2 %collective-permute-start.3 = (bf16[512,256]{1,0:T(8,128)(2,1)S(1)}, bf16[512,256]{1,0:T(8,128)(2,1)S(1)}, u32[]{:S(2)}, u32[]{:S(2)}) collective-permute-start(bf16[512,256]{1,0:T(8,128)(2,1)S(1)} %bitcast.13), channel_id=1, source_target_pairs={{0,16},{4,20},{8,24},{12,28},{16,0},{20,4},{24,8},{28,12},{32,48},... | collective-permute-start | bytes 786440 | tf_op jit(solution)/shard_map/ppermute | solution.py:31
  27.2 3.0 %collective-permute-start.4 = (bf16[64,1024]{1,0:T(8,128)(2,1)S(1)}, bf16[64,1024]{1,0:T(8,128)(2,1)S(1)}, u32[]{:S(2)}, u32[]{:S(2)}) collective-permute-start(bf16[64,1024]{1,0:T(8,128)(2,1)S(1)} %fusion.1.refs_0_), channel_id=1, source_target_pairs={{0,2},{1,3},{2,0},{3,1},{4,6},{5,7},{6,4},{7,5},{8,10},{9,11},{10,... | collective-permute-start | bytes 393224 | tf_op jit(solution)/shard_map/ppermute | solution.py:35
  30.2 1.1 %collective-permute-start.5 = (bf16[64,1024]{1,0:T(8,128)(2,1)S(1)}, bf16[64,1024]{1,0:T(8,128)(2,1)S(1)}, u32[]{:S(2)}, u32[]{:S(2)}) collective-permute-start(bf16[64,1024]{1,0:T(8,128)(2,1)S(1)} %fusion.1.refs_0_), channel_id=1, source_target_pairs={{0,3},{1,0},{2,1},{3,2},{4,7},{5,4},{6,5},{7,6},{8,11},{9,8},{10,9... | collective-permute-start | bytes 393224 | tf_op jit(solution)/shard_map/ppermute | solution.py:35
  31.4 0.1 pad_add_fusion.place
  31.5 2.2 %collective-permute-done.4.refs_2_ = bf16[64,1024]{1,0:T(8,128)(2,1)S(1)} collective-permute-done((bf16[64,1024]{1,0:T(8,128)(2,1)S(1)}, bf16[64,1024]{1,0:T(8,128)(2,1)S(1)}, u32[]{:S(2)}, u32[]{:S(2)}) %collective-permute-start.4) | collective-permute-done | bytes 131104 | tf_op jit(solution)/shard_map/ppermute | solution.py:35
  33.7 1.5 %collective-permute-done.5.refs_3_ = bf16[64,1024]{1,0:T(8,128)(2,1)S(1)} collective-permute-done((bf16[64,1024]{1,0:T(8,128)(2,1)S(1)}, bf16[64,1024]{1,0:T(8,128)(2,1)S(1)}, u32[]{:S(2)}, u32[]{:S(2)}) %collective-permute-start.5) | collective-permute-done | bytes 131104 | tf_op jit(solution)/shard_map/ppermute | solution.py:35
  35.2 2.2 %copy-done.1 = bf16[512,4096]{1,0:T(8,128)(2,1)S(1)} copy-done((bf16[512,4096]{1,0:T(8,128)(2,1)S(1)}, bf16[512,4096]{1,0:T(8,128)(2,1)}, u32[]{:S(2)}) %copy-start.1) | copy-done | bytes 4194328
  37.4 2.0 %shard_map.127 = (bf16[64,512]{1,0:T(8,128)(2,1)S(1)}, bf16[64,1024]{1,0:T(8,128)(2,1)S(1)}, bf16[64,1024]{1,0:T(8,128)(2,1)S(1)}, bf16[64,1024]{1,0:T(8,128)(2,1)S(1)}, bf16[64,1024]{1,0:T(8,128)(2,1)S(1)}) custom-call(s32[4]{0:T(128)S(1)} %pad_add_fusion.place, bf16[64,1024]{1,0:T(8,128)(2,1)S(1)} %fusion.1.refs_0_, ...), custom_call_target="tpu_custom_call" | custom-call | flops 268435456 | bytes 5308416 | tf_op jit(solution)/shard_map/pallas_call | solution.py:255
  39.4 0.1 collective-permute-start.6
  39.5 0.5 collective-permute-start.7
  40.0 0.1 collective-permute-start.8
  40.1 0.4 collective-permute-start.9
  40.5 1.9 %shard_map.128 = (f32[16,256]{1,0:T(8,128)S(1)}, f32[128,256]{1,0:T(8,128)S(1)}) custom-call(s32[4]{0:T(128)S(1)} %pad_add_fusion.place, bf16[64,512]{1,0:T(8,128)(2,1)S(1)} %copy-done.3, bf16[512,256]{1,0:T(8,128)(2,1)S(1)} %bitcast.15, bf16[512,256]{1,0:T(8,128)(2,1)S(1)} %collective-permute-done.1.refs_1_, ...), custom_call_target="tpu_custom_call" | custom-call | flops 268435456 | bytes 1261568 | tf_op jit(solution)/shard_map/pallas_call | solution.py:255
  42.5 2.0 %shard_map.129 = (bf16[64,512]{1,0:T(8,128)(2,1)S(1)}, f32[8,256]{1,0:T(8,128)S(1)}, bf16[64,1536]{1,0:T(8,128)(2,1)S(1)}, bf16[64,1536]{1,0:T(8,128)(2,1)S(1)},...) custom-call(s32[4]{0:T(128)S(1)} %pad_add_fusion.place, bf16[64,512]{1,0:T(8,128)(2,1)S(1)} %copy-done.3, ...), custom_call_target="tpu_custom_call" | custom-call | flops 268435456 | bytes 2646016 | tf_op jit(solution)/shard_map/pallas_call | solution.py:255
  44.6 2.2 %shard_map.130 = (bf16[2048,256]{1,0:T(8,128)(2,1)S(1)}, f32[128,256]{1,0:T(8,128)S(1)}) custom-call(s32[4]{0:T(128)S(1)} %pad_add_fusion.place, bf16[64,512]{1,0:T(8,128)(2,1)S(1)} %copy-done.3, bf16[64,512]{1,0:T(8,128)(2,1)S(1)} %get-tuple-element.68.g_ref, bf16[64,512]{1,0:T(8,128)(2,1)S(1)} %get-tuple-element.82.att_ref, ...), custom_call_target="tpu_custom_call" | custom-call | flops 671088640 | bytes 2433024 | tf_op jit(solution)/shard_map/pallas_call | solution.py:255
  46.8 0.2 collective-permute-start.10
  47.0 2.2 %collective-permute-start.21 = (bf16[64,1536]{1,0:T(8,128)(2,1)S(1)}, bf16[64,1536]{1,0:T(8,128)(2,1)S(1)}, u32[]{:S(2)}, u32[]{:S(2)}) collective-permute-start(bf16[64,1536]{1,0:T(8,128)(2,1)S(1)} %get-tuple-element.89), channel_id=1, source_target_pairs={{0,8},{4,12},{8,16},{12,20},{16,24},{20,28},{24,0},{28,4},{32,40},... | collective-permute-start | bytes 589832 | tf_op jit(solution)/shard_map/ppermute | solution.py:31
  49.2 2.1 %collective-permute-start.23 = (bf16[64,1536]{1,0:T(8,128)(2,1)S(1)}, bf16[64,1536]{1,0:T(8,128)(2,1)S(1)}, u32[]{:S(2)}, u32[]{:S(2)}) collective-permute-start(bf16[64,1536]{1,0:T(8,128)(2,1)S(1)} %get-tuple-element.91), channel_id=1, source_target_pairs={{0,16},{4,20},{8,24},{12,28},{16,0},{20,4},{24,8},{28,12},{32,48},... | collective-permute-start | bytes 589832 | tf_op jit(solution)/shard_map/ppermute | solution.py:31
  51.3 2.9 %shard_map.131 = (bf16[512,256]{1,0:T(8,128)(2,1)S(1)}, bf16[512,256]{1,0:T(8,128)(2,1)S(1)}, bf16[512,256]{1,0:T(8,128)(2,1)S(1)}, bf16[512,256]{1,0:T(8,128)(2,1)S(1)}, bf16[64,512]{1,0:T(8,128)(2,1)}) custom-call(s32[4]{0:T(128)S(1)} %pad_add_fusion.place, bf16[64,512]{1,0:T(8,128)(2,1)S(1)} %copy-done.3, bf16[64,512]{1,0:T(8,128)(2,1)S(1)} %get-tuple-element.68.g_ref, ...), custom_call_target="tpu_custom_call" | custom-call | flops 671088640 | bytes 2498560 | tf_op jit(solution)/shard_map/pallas_call | solution.py:255
  54.2 0.3 add_convert_fusion.1
  54.5 2.0 %collective-permute-start.11 = (bf16[512,256]{1,0:T(8,128)(2,1)S(1)}, bf16[512,256]{1,0:T(8,128)(2,1)S(1)}, u32[]{:S(2)}, u32[]{:S(2)}) collective-permute-start(bf16[512,256]{1,0:T(8,128)(2,1)S(1)} %get-tuple-element.98), channel_id=1, source_target_pairs={{0,24},{4,28},{8,0},{12,4},{16,8},{20,12},{24,16},{28,20},{32,56},... | collective-permute-start | bytes 786440 | tf_op jit(solution)/shard_map/ppermute | solution.py:31
  56.5 1.3 %collective-permute-start.12 = (bf16[512,256]{1,0:T(8,128)(2,1)S(1)}, bf16[512,256]{1,0:T(8,128)(2,1)S(1)}, u32[]{:S(2)}, u32[]{:S(2)}) collective-permute-start(bf16[512,256]{1,0:T(8,128)(2,1)S(1)} %get-tuple-element.97), channel_id=1, source_target_pairs={{0,8},{4,12},{8,16},{12,20},{16,24},{20,28},{24,0},{28,4},{32,40},... | collective-permute-start | bytes 786440 | tf_op jit(solution)/shard_map/ppermute | solution.py:31
  57.8 0.6 collective-permute-done.21.refs_1_
  58.4 0.2 collective-permute-start.13
  58.7 3.6 %collective-permute-done.22.refs_2_ = bf16[64,1536]{1,0:T(8,128)(2,1)S(1)} collective-permute-done((bf16[64,1536]{1,0:T(8,128)(2,1)S(1)}, bf16[64,1536]{1,0:T(8,128)(2,1)S(1)}, u32[]{:S(2)}, u32[]{:S(2)}) %collective-permute-start.22) | collective-permute-done | bytes 196640 | tf_op jit(solution)/shard_map/ppermute | solution.py:31
  62.3 1.0 shard_map.133
  63.3 0.1 collective-permute-start.24
  63.4 9.3 %collective-permute-done.11 = bf16[512,256]{1,0:T(8,128)(2,1)S(1)} collective-permute-done((bf16[512,256]{1,0:T(8,128)(2,1)S(1)}, bf16[512,256]{1,0:T(8,128)(2,1)S(1)}, u32[]{:S(2)}, u32[]{:S(2)}) %collective-permute-start.11) | collective-permute-done | bytes 262176 | tf_op jit(solution)/shard_map/ppermute | solution.py:31
  72.8 0.1 add_convert_fusion.5
  72.8 0.6 collective-permute-start.14
  73.4 4.8 %collective-permute-start.15 = (bf16[128,256]{1,0:T(8,128)(2,1)S(1)}, bf16[128,256]{1,0:T(8,128)(2,1)S(1)}, u32[]{:S(2)}, u32[]{:S(2)}) collective-permute-start(bf16[128,256]{1,0:T(8,128)(2,1)S(1)} %add_convert_fusion.7), channel_id=1, source_target_pairs={{0,160},{4,164},{8,168},{12,172},{16,176},{20,180},{24,184},{28,18... | collective-permute-start | bytes 196616 | tf_op jit(solution)/shard_map/ppermute | solution.py:31
  78.3 0.9 add_convert_fusion
  79.2 3.5 %all-to-all-start.1 = ((bf16[8,64,512]{2,1,0:T(8,128)(2,1)}), bf16[8,64,512]{2,1,0:T(8,128)(2,1)S(1)}, u32[]{:S(2)}, u32[]{:S(2)}) async-start(bf16[8,64,512]{2,1,0:T(8,128)(2,1)} %bitcast.5), calls=%async_computation.1 | async-start | bytes 1048576 | tf_op jit(solution)/shard_map/all_to_all | solution.py:42
  82.7 0.1 add_convert_fusion.8
  82.8 0.0 copy-start.5
  82.8 0.0 copy-start.6
  82.8 3.2 %collective-permute-start.19 = (bf16[64,256]{1,0:T(8,128)(2,1)S(1)}, bf16[64,256]{1,0:T(8,128)(2,1)S(1)}, u32[]{:S(2)}, u32[]{:S(2)}) collective-permute-start(bf16[64,256]{1,0:T(8,128)(2,1)S(1)} %get-tuple-element.80), channel_id=1, source_target_pairs={{0,224},{4,228},{8,232},{12,236},{16,240},{20,244},{24,248},{28,25... | collective-permute-start | bytes 98312 | tf_op jit(solution)/shard_map/ppermute | solution.py:31
  86.1 2.2 %copy-done.2 = bf16[512,4096]{1,0:T(8,128)(2,1)S(1)} copy-done((bf16[512,4096]{1,0:T(8,128)(2,1)S(1)}, bf16[512,4096]{1,0:T(8,128)(2,1)}, u32[]{:S(2)}) %copy-start.2) | copy-done | bytes 4194328
  88.2 2.4 %shard_map.132 = (bf16[64,1152]{1,0:T(8,128)(2,1)S(1)}, bf16[64,1152]{1,0:T(8,128)(2,1)S(1)}, bf16[64,1152]{1,0:T(8,128)(2,1)S(1)}, bf16[64,1152]{1,0:T(8,128)(2,1)S(1)}) custom-call(s32[4]{0:T(128)S(1)} %pad_add_fusion.place, bf16[64,512]{1,0:T(8,128)(2,1)S(1)} %get-tuple-element.82.att_ref, bf16[64,512]{1,0:T(8,128)(2,1)S(1)} %get-tuple-element.68.g_ref, ...), custom_call_target="tpu_custom_call" | custom-call | flops 5368709120 | bytes 4915200 | tf_op jit(solution)/shard_map/pallas_call | solution.py:255
  90.7 2.7 %collective-permute-start.16 = (bf16[64,1152]{1,0:T(8,128)(2,1)S(1)}, bf16[64,1152]{1,0:T(8,128)(2,1)S(1)}, u32[]{:S(2)}, u32[]{:S(2)}) collective-permute-start(bf16[64,1152]{1,0:T(8,128)(2,1)S(1)} %get-tuple-element.84), channel_id=1, source_target_pairs={{0,3},{1,0},{2,1},{3,2},{4,7},{5,4},{6,5},{7,6},{8,11},{9,8},{10,9... | collective-permute-start | bytes 442376 | tf_op jit(solution)/shard_map/ppermute | solution.py:35
  93.4 1.6 %collective-permute-start.18 = (bf16[64,1152]{1,0:T(8,128)(2,1)S(1)}, bf16[64,1152]{1,0:T(8,128)(2,1)S(1)}, u32[]{:S(2)}, u32[]{:S(2)}) collective-permute-start(bf16[64,1152]{1,0:T(8,128)(2,1)S(1)} %get-tuple-element.86), channel_id=1, source_target_pairs={{0,2},{1,3},{2,0},{3,1},{4,6},{5,7},{6,4},{7,5},{8,10},{9,11},{10,... | collective-permute-start | bytes 442376 | tf_op jit(solution)/shard_map/ppermute | solution.py:35
  95.0 1.1 %collective-permute-done.19 = bf16[64,256]{1,0:T(8,128)(2,1)S(1)} collective-permute-done((bf16[64,256]{1,0:T(8,128)(2,1)S(1)}, bf16[64,256]{1,0:T(8,128)(2,1)S(1)}, u32[]{:S(2)}, u32[]{:S(2)}) %collective-permute-start.19) | collective-permute-done | bytes 32800 | tf_op jit(solution)/shard_map/ppermute | solution.py:31
  96.1 0.1 select_convert_fusion
  96.2 0.6 fusion.9
  96.8 0.9 collective-permute-done.16
  97.7 3.8 %collective-permute-done.17 = bf16[64,1152]{1,0:T(8,128)(2,1)S(1)} collective-permute-done((bf16[64,1152]{1,0:T(8,128)(2,1)S(1)}, bf16[64,1152]{1,0:T(8,128)(2,1)S(1)}, u32[]{:S(2)}, u32[]{:S(2)}) %collective-permute-start.17) | collective-permute-done | bytes 147488 | tf_op jit(solution)/shard_map/ppermute | solution.py:35
  101.5 0.1 convert_add_fusion
  101.5 0.2 fusion.6
  101.7 0.5 divide_select_fusion
  102.3 1.2 %fusion = bf16[256,1024]{1,0:T(8,128)(2,1)} fusion(bf16[256,1024]{1,0:T(8,128)(2,1)S(1)} %copy-done.4, f32[64,1152]{1,0:T(8,128)S(1)} %convert_add_fusion, f32[64]{0:T(128)S(1)} %broadcast_select_fusion.1, s32[64]{0:T(128)S(1)} %copy-done.5), kind=kOutput, calls=%fused_computation.1 | convolution fusion | flops 34488320 | bytes 1311744 | tf_op jit(solution)/shard_map/dot_general | solution.py:70
  103.5 0.7 fusion.5
  (30 shorter events, 0.1 us)
Async XLA Ops:
  0.6 12.1 %copy-start = (bf16[256,1024]{1,0:T(8,128)(2,1)S(1)}, bf16[256,1024]{1,0:T(8,128)(2,1)}, u32[]{:S(2)}) copy-start(bf16[256,1024]{1,0:T(8,128)(2,1)} %param.9) | copy-start | bytes 1572868
  0.6 39.9 %copy-start.3 = (bf16[64,512]{1,0:T(8,128)(2,1)S(1)}, bf16[64,512]{1,0:T(8,128)(2,1)}, u32[]{:S(2)}) copy-start(bf16[64,512]{1,0:T(8,128)(2,1)} %q_ref.7) | copy-start | bytes 196612
  3.6 20.3 %all-to-all-start = ((bf16[8,64,256]{2,1,0:T(8,128)(2,1)}), bf16[8,64,256]{2,1,0:T(8,128)(2,1)S(1)}, u32[]{:S(2)}, u32[]{:S(2)}) async-start(bf16[8,64,256]{2,1,0:T(8,128)(2,1)} %broadcast_in_dim.42), calls=%async_computation | async-start | bytes 524288 | tf_op jit(solution)/shard_map/all_to_all | solution.py:42
  13.7 6.3 %collective-permute-start = (bf16[64,1024]{1,0:T(8,128)(2,1)S(1)}, bf16[64,1024]{1,0:T(8,128)(2,1)S(1)}, u32[]{:S(2)}, u32[]{:S(2)}) collective-permute-start(bf16[64,1024]{1,0:T(8,128)(2,1)S(1)} %fusion.1.refs_0_), channel_id=1, source_target_pairs={{0,1},{1,2},{2,3},{3,0},{4,5},{5,6},{6,7},{7,4},{8,9},{9,10},{10,1... | collective-permute-start | bytes 393224 | tf_op jit(solution)/shard_map/ppermute | solution.py:35
  24.0 15.4 %collective-permute-start.1 = (bf16[512,256]{1,0:T(8,128)(2,1)S(1)}, bf16[512,256]{1,0:T(8,128)(2,1)S(1)}, u32[]{:S(2)}, u32[]{:S(2)}) collective-permute-start(bf16[512,256]{1,0:T(8,128)(2,1)S(1)} %bitcast.11), channel_id=1, source_target_pairs={{0,8},{4,12},{8,16},{12,20},{16,24},{20,28},{24,0},{28,4},{32,40},... | collective-permute-start | bytes 786440 | tf_op jit(solution)/shard_map/ppermute | solution.py:31
  24.2 15.2 %collective-permute-start.2 = (bf16[512,256]{1,0:T(8,128)(2,1)S(1)}, bf16[512,256]{1,0:T(8,128)(2,1)S(1)}, u32[]{:S(2)}, u32[]{:S(2)}) collective-permute-start(bf16[512,256]{1,0:T(8,128)(2,1)S(1)} %bitcast.12), channel_id=1, source_target_pairs={{0,24},{4,28},{8,0},{12,4},{16,8},{20,12},{24,16},{28,20},{32,56},... | collective-permute-start | bytes 786440 | tf_op jit(solution)/shard_map/ppermute | solution.py:31
  26.0 13.4 %collective-permute-start.3 = (bf16[512,256]{1,0:T(8,128)(2,1)S(1)}, bf16[512,256]{1,0:T(8,128)(2,1)S(1)}, u32[]{:S(2)}, u32[]{:S(2)}) collective-permute-start(bf16[512,256]{1,0:T(8,128)(2,1)S(1)} %bitcast.13), channel_id=1, source_target_pairs={{0,16},{4,20},{8,24},{12,28},{16,0},{20,4},{24,8},{28,12},{32,48},... | collective-permute-start | bytes 786440 | tf_op jit(solution)/shard_map/ppermute | solution.py:31
  27.2 6.5 %collective-permute-start.4 = (bf16[64,1024]{1,0:T(8,128)(2,1)S(1)}, bf16[64,1024]{1,0:T(8,128)(2,1)S(1)}, u32[]{:S(2)}, u32[]{:S(2)}) collective-permute-start(bf16[64,1024]{1,0:T(8,128)(2,1)S(1)} %fusion.1.refs_0_), channel_id=1, source_target_pairs={{0,2},{1,3},{2,0},{3,1},{4,6},{5,7},{6,4},{7,5},{8,10},{9,11},{10,... | collective-permute-start | bytes 393224 | tf_op jit(solution)/shard_map/ppermute | solution.py:35
  30.2 5.0 %collective-permute-start.5 = (bf16[64,1024]{1,0:T(8,128)(2,1)S(1)}, bf16[64,1024]{1,0:T(8,128)(2,1)S(1)}, u32[]{:S(2)}, u32[]{:S(2)}) collective-permute-start(bf16[64,1024]{1,0:T(8,128)(2,1)S(1)} %fusion.1.refs_0_), channel_id=1, source_target_pairs={{0,3},{1,0},{2,1},{3,2},{4,7},{5,4},{6,5},{7,6},{8,11},{9,8},{10,9... | collective-permute-start | bytes 393224 | tf_op jit(solution)/shard_map/ppermute | solution.py:35
  35.2 2.2 %copy-start.1 = (bf16[512,4096]{1,0:T(8,128)(2,1)S(1)}, bf16[512,4096]{1,0:T(8,128)(2,1)}, u32[]{:S(2)}) copy-start(bf16[512,4096]{1,0:T(8,128)(2,1)} %w_ref.1) | copy-start | bytes 12582916
  39.4 3.1 %collective-permute-start.6 = (bf16[512,256]{1,0:T(8,128)(2,1)S(1)}, bf16[512,256]{1,0:T(8,128)(2,1)S(1)}, u32[]{:S(2)}, u32[]{:S(2)}) collective-permute-start(bf16[512,256]{1,0:T(8,128)(2,1)S(1)} %bitcast.14), channel_id=1, source_target_pairs={{0,4},{4,0},{8,12},{12,8},{16,20},{20,16},{24,28},{28,24},{32,36},... | collective-permute-start | bytes 786440 | tf_op jit(solution)/shard_map/ppermute | solution.py:31
  39.5 3.0 %collective-permute-start.7 = (bf16[512,256]{1,0:T(8,128)(2,1)S(1)}, bf16[512,256]{1,0:T(8,128)(2,1)S(1)}, u32[]{:S(2)}, u32[]{:S(2)}) collective-permute-start(bf16[512,256]{1,0:T(8,128)(2,1)S(1)} %collective-permute-done.1.refs_1_), channel_id=1, source_target_pairs={{0,4},{4,0},{8,12},{12,8},{16,20},{20,16},{24,28},{28,24},{32,36},... | collective-permute-start | bytes 786440 | tf_op jit(solution)/shard_map/ppermute | solution.py:31
  40.0 2.5 %collective-permute-start.8 = (bf16[512,256]{1,0:T(8,128)(2,1)S(1)}, bf16[512,256]{1,0:T(8,128)(2,1)S(1)}, u32[]{:S(2)}, u32[]{:S(2)}) collective-permute-start(bf16[512,256]{1,0:T(8,128)(2,1)S(1)} %collective-permute-done.2.refs_2_), channel_id=1, source_target_pairs={{0,4},{4,0},{8,12},{12,8},{16,20},{20,16},{24,28},{28,24},{32,36},... | collective-permute-start | bytes 786440 | tf_op jit(solution)/shard_map/ppermute | solution.py:31
  40.1 2.4 %collective-permute-start.9 = (bf16[512,256]{1,0:T(8,128)(2,1)S(1)}, bf16[512,256]{1,0:T(8,128)(2,1)S(1)}, u32[]{:S(2)}, u32[]{:S(2)}) collective-permute-start(bf16[512,256]{1,0:T(8,128)(2,1)S(1)} %collective-permute-done.3.refs_3_), channel_id=1, source_target_pairs={{0,4},{4,0},{8,12},{12,8},{16,20},{20,16},{24,28},{28,24},{32,36},... | collective-permute-start | bytes 786440 | tf_op jit(solution)/shard_map/ppermute | solution.py:31
  46.8 7.4 %collective-permute-start.10 = (bf16[2048,256]{1,0:T(8,128)(2,1)S(1)}, bf16[2048,256]{1,0:T(8,128)(2,1)S(1)}, u32[]{:S(2)}, u32[]{:S(2)}) collective-permute-start(bf16[2048,256]{1,0:T(8,128)(2,1)S(1)} %get-tuple-element.72), channel_id=1, source_target_pairs={{0,4},{4,0},{8,12},{12,8},{16,20},{20,16},{24,28},{28,24},{32,36},... | collective-permute-start | bytes 3145736 | tf_op jit(solution)/shard_map/ppermute | solution.py:31
  47.0 11.5 %collective-permute-start.21 = (bf16[64,1536]{1,0:T(8,128)(2,1)S(1)}, bf16[64,1536]{1,0:T(8,128)(2,1)S(1)}, u32[]{:S(2)}, u32[]{:S(2)}) collective-permute-start(bf16[64,1536]{1,0:T(8,128)(2,1)S(1)} %get-tuple-element.89), channel_id=1, source_target_pairs={{0,8},{4,12},{8,16},{12,20},{16,24},{20,28},{24,0},{28,4},{32,40},... | collective-permute-start | bytes 589832 | tf_op jit(solution)/shard_map/ppermute | solution.py:31
  49.2 13.2 %collective-permute-start.22 = (bf16[64,1536]{1,0:T(8,128)(2,1)S(1)}, bf16[64,1536]{1,0:T(8,128)(2,1)S(1)}, u32[]{:S(2)}, u32[]{:S(2)}) collective-permute-start(bf16[64,1536]{1,0:T(8,128)(2,1)S(1)} %get-tuple-element.90), channel_id=1, source_target_pairs={{0,24},{4,28},{8,0},{12,4},{16,8},{20,12},{24,16},{28,20},{32,56},... | collective-permute-start | bytes 589832 | tf_op jit(solution)/shard_map/ppermute | solution.py:31
  49.2 13.2 %collective-permute-start.23 = (bf16[64,1536]{1,0:T(8,128)(2,1)S(1)}, bf16[64,1536]{1,0:T(8,128)(2,1)S(1)}, u32[]{:S(2)}, u32[]{:S(2)}) collective-permute-start(bf16[64,1536]{1,0:T(8,128)(2,1)S(1)} %get-tuple-element.91), channel_id=1, source_target_pairs={{0,16},{4,20},{8,24},{12,28},{16,0},{20,4},{24,8},{28,12},{32,48},... | collective-permute-start | bytes 589832 | tf_op jit(solution)/shard_map/ppermute | solution.py:31
  54.5 18.3 %collective-permute-start.11 = (bf16[512,256]{1,0:T(8,128)(2,1)S(1)}, bf16[512,256]{1,0:T(8,128)(2,1)S(1)}, u32[]{:S(2)}, u32[]{:S(2)}) collective-permute-start(bf16[512,256]{1,0:T(8,128)(2,1)S(1)} %get-tuple-element.98), channel_id=1, source_target_pairs={{0,24},{4,28},{8,0},{12,4},{16,8},{20,12},{24,16},{28,20},{32,56},... | collective-permute-start | bytes 786440 | tf_op jit(solution)/shard_map/ppermute | solution.py:31
  56.5 16.2 %collective-permute-start.12 = (bf16[512,256]{1,0:T(8,128)(2,1)S(1)}, bf16[512,256]{1,0:T(8,128)(2,1)S(1)}, u32[]{:S(2)}, u32[]{:S(2)}) collective-permute-start(bf16[512,256]{1,0:T(8,128)(2,1)S(1)} %get-tuple-element.97), channel_id=1, source_target_pairs={{0,8},{4,12},{8,16},{12,20},{16,24},{20,28},{24,0},{28,4},{32,40},... | collective-permute-start | bytes 786440 | tf_op jit(solution)/shard_map/ppermute | solution.py:31
  58.4 14.3 %collective-permute-start.13 = (bf16[512,256]{1,0:T(8,128)(2,1)S(1)}, bf16[512,256]{1,0:T(8,128)(2,1)S(1)}, u32[]{:S(2)}, u32[]{:S(2)}) collective-permute-start(bf16[512,256]{1,0:T(8,128)(2,1)S(1)} %get-tuple-element.96), channel_id=1, source_target_pairs={{0,16},{4,20},{8,24},{12,28},{16,0},{20,4},{24,8},{28,12},{32,48},... | collective-permute-start | bytes 786440 | tf_op jit(solution)/shard_map/ppermute | solution.py:31
  63.3 14.9 %collective-permute-start.24 = (bf16[512,512]{1,0:T(8,128)(2,1)S(1)}, bf16[512,512]{1,0:T(8,128)(2,1)S(1)}, u32[]{:S(2)}, u32[]{:S(2)}) collective-permute-start(bf16[512,512]{1,0:T(8,128)(2,1)S(1)} %get-tuple-element.93), channel_id=1, source_target_pairs={{0,4},{4,0},{8,12},{12,8},{16,20},{20,16},{24,28},{28,24},{32,36},... | collective-permute-start | bytes 1572872 | tf_op jit(solution)/shard_map/ppermute | solution.py:31
  72.8 9.9 %collective-permute-start.14 = (bf16[192,256]{1,0:T(8,128)(2,1)S(1)}, bf16[192,256]{1,0:T(8,128)(2,1)S(1)}, u32[]{:S(2)}, u32[]{:S(2)}) collective-permute-start(bf16[192,256]{1,0:T(8,128)(2,1)S(1)} %add_convert_fusion.5), channel_id=1, source_target_pairs={{0,96},{4,100},{8,104},{12,108},{16,112},{20,116},{24,120},{28,124... | collective-permute-start | bytes 294920 | tf_op jit(solution)/shard_map/ppermute | solution.py:31
  73.4 9.3 %collective-permute-start.15 = (bf16[128,256]{1,0:T(8,128)(2,1)S(1)}, bf16[128,256]{1,0:T(8,128)(2,1)S(1)}, u32[]{:S(2)}, u32[]{:S(2)}) collective-permute-start(bf16[128,256]{1,0:T(8,128)(2,1)S(1)} %add_convert_fusion.7), channel_id=1, source_target_pairs={{0,160},{4,164},{8,168},{12,172},{16,176},{20,180},{24,184},{28,18... | collective-permute-start | bytes 196616 | tf_op jit(solution)/shard_map/ppermute | solution.py:31
  79.2 24.3 %all-to-all-start.1 = ((bf16[8,64,512]{2,1,0:T(8,128)(2,1)}), bf16[8,64,512]{2,1,0:T(8,128)(2,1)S(1)}, u32[]{:S(2)}, u32[]{:S(2)}) async-start(bf16[8,64,512]{2,1,0:T(8,128)(2,1)} %bitcast.5), calls=%async_computation.1 | async-start | bytes 1048576 | tf_op jit(solution)/shard_map/all_to_all | solution.py:42
  82.8 18.9 %copy-start.5 = (s32[64]{0:T(128)S(1)}, s32[64]{0:T(128)}, u32[]{:S(2)}) copy-start(s32[64]{0:T(128)} %param.10) | copy-start | bytes 772
  82.8 18.9 %copy-start.6 = (f32[64]{0:T(128)S(1)}, f32[64]{0:T(128)}, u32[]{:S(2)}) copy-start(f32[64]{0:T(128)} %param.14) | copy-start | bytes 772
  82.8 13.3 %collective-permute-start.19 = (bf16[64,256]{1,0:T(8,128)(2,1)S(1)}, bf16[64,256]{1,0:T(8,128)(2,1)S(1)}, u32[]{:S(2)}, u32[]{:S(2)}) collective-permute-start(bf16[64,256]{1,0:T(8,128)(2,1)S(1)} %get-tuple-element.80), channel_id=1, source_target_pairs={{0,224},{4,228},{8,232},{12,236},{16,240},{20,244},{24,248},{28,25... | collective-permute-start | bytes 98312 | tf_op jit(solution)/shard_map/ppermute | solution.py:31
  86.0 10.1 %collective-permute-start.20 = (bf16[64,256]{1,0:T(8,128)(2,1)S(1)}, bf16[64,256]{1,0:T(8,128)(2,1)S(1)}, u32[]{:S(2)}, u32[]{:S(2)}) collective-permute-start(bf16[64,256]{1,0:T(8,128)(2,1)S(1)} %get-tuple-element.81), channel_id=1, source_target_pairs={{0,32},{4,36},{8,40},{12,44},{16,48},{20,52},{24,56},{28,60},{32,6... | collective-permute-start | bytes 98312 | tf_op jit(solution)/shard_map/ppermute | solution.py:31
  86.0 2.2 %copy-start.2 = (bf16[512,4096]{1,0:T(8,128)(2,1)S(1)}, bf16[512,4096]{1,0:T(8,128)(2,1)}, u32[]{:S(2)}) copy-start(bf16[512,4096]{1,0:T(8,128)(2,1)} %w_ref.1) | copy-start | bytes 12582916
  88.2 14.0 %copy-start.4 = (bf16[256,1024]{1,0:T(8,128)(2,1)S(1)}, bf16[256,1024]{1,0:T(8,128)(2,1)}, u32[]{:S(2)}) copy-start(bf16[256,1024]{1,0:T(8,128)(2,1)} %param.8) | copy-start | bytes 1572868
  90.7 7.0 %collective-permute-start.16 = (bf16[64,1152]{1,0:T(8,128)(2,1)S(1)}, bf16[64,1152]{1,0:T(8,128)(2,1)S(1)}, u32[]{:S(2)}, u32[]{:S(2)}) collective-permute-start(bf16[64,1152]{1,0:T(8,128)(2,1)S(1)} %get-tuple-element.84), channel_id=1, source_target_pairs={{0,3},{1,0},{2,1},{3,2},{4,7},{5,4},{6,5},{7,6},{8,11},{9,8},{10,9... | collective-permute-start | bytes 442376 | tf_op jit(solution)/shard_map/ppermute | solution.py:35
  93.4 8.0 %collective-permute-start.17 = (bf16[64,1152]{1,0:T(8,128)(2,1)S(1)}, bf16[64,1152]{1,0:T(8,128)(2,1)S(1)}, u32[]{:S(2)}, u32[]{:S(2)}) collective-permute-start(bf16[64,1152]{1,0:T(8,128)(2,1)S(1)} %get-tuple-element.85), channel_id=1, source_target_pairs={{0,1},{1,2},{2,3},{3,0},{4,5},{5,6},{6,7},{7,4},{8,9},{9,10},{10,1... | collective-permute-start | bytes 442376 | tf_op jit(solution)/shard_map/ppermute | solution.py:35
  93.4 8.0 %collective-permute-start.18 = (bf16[64,1152]{1,0:T(8,128)(2,1)S(1)}, bf16[64,1152]{1,0:T(8,128)(2,1)S(1)}, u32[]{:S(2)}, u32[]{:S(2)}) collective-permute-start(bf16[64,1152]{1,0:T(8,128)(2,1)S(1)} %get-tuple-element.86), channel_id=1, source_target_pairs={{0,2},{1,3},{2,0},{3,1},{4,6},{5,7},{6,4},{7,5},{8,10},{9,11},{10,... | collective-permute-start | bytes 442376 | tf_op jit(solution)/shard_map/ppermute | solution.py:35
